TPU v7x, 32 devices: a whole 2x2x4 slice. The times are simulated.
32 devices in a mesh: ctx: 8 (over y, x, core), head: 4 (over z).
Axes of the slice: x: 2, y: 2, z: 4, core: 2. Of those that a mesh axis runs over, the one named last changes fastest.
Arguments:
- queries: bfloat16 [2048, 4096], P('ctx', 'head'), may hold values from -80 to 80
- keys: bfloat16 [2048, 2048], P('ctx', 'head'), may hold values from -6 to 6
- values: bfloat16 [2048, 2048], P('ctx', 'head'), may hold values from -6 to 6
- grad_out: bfloat16 [2048, 4096], P('ctx', 'head'), may hold values from -6 to 6
- chosen: int32 [32, 16, 16], P('ctx', 'head'), may hold values from 0 to 31, as said below
- w_query: bfloat16 [4608, 4096], P(None, 'head'), may hold values from -0.09375 to 0.09375
- w_key: bfloat16 [4608, 2048], P(None, 'head'), may hold values from -0.09375 to 0.09375
- w_value: bfloat16 [4608, 2048], P(None, 'head'), may hold values from -0.09375 to 0.09375
Outputs:
- grad_queries: bfloat16 [2048, 4096], P('ctx', 'head')
- grad_keys: bfloat16 [2048, 2048], P('ctx', 'head')
- grad_values: bfloat16 [2048, 2048], P('ctx', 'head')
- grad_input: bfloat16 [2048, 4608], P('ctx', 'head')
Inputs may be any that keep to these rules, and one draw needn't show every extreme that they name: `chosen`: each list names 16 different blocks; it always names block 0 and the query's own block, and a query block b below 16 names every block 0 .. b; entries above the query's own block contribute no keys.
All inputs are finite; a program needn't handle non-finite values.
Results may differ from a plain program's by a relative error of at most 0.019.
Values may be sent and summed in bfloat16 or wider, within the bound.
No kernel may reach another device: no remote copies, remote signals or barrier semaphores. Data moves between devices by JAX's collectives and lax.ppermute only.
A program may use at most 128 MiB of HBM per device.

v0:
```python
import functools
import math

import jax
import jax.numpy as jnp
from jax import lax
from jax.experimental import pallas as pl
from jax.experimental.pallas import tpu as pltpu
from jax.sharding import PartitionSpec as P

HEAD_DIM = 128
BLOCK = 64
LOG2E = math.log2(math.e)


def attention_kernel(n_ctx, topk, first_group, groups_here, chosen, place, *refs):
    pieces = refs[:n_ctx]
    q_ref, g_ref = refs[n_ctx : n_ctx + 2]
    dq_ref, keep_ref, send_ref = refs[n_ctx + 2 : n_ctx + 5]
    kv, acc, near, scores, packed = refs[n_ctx + 5 :]
    rows = q_ref.shape[0]
    wide = 2 * HEAD_DIM
    heads_per = q_ref.shape[1] // HEAD_DIM
    lanes = heads_per * BLOCK
    me = place[0]
    group = first_group + pl.program_id(0)
    scaling = 1.0 / math.sqrt(HEAD_DIM)
    step = scaling * LOG2E

    for k in range(n_ctx):
        kv[pl.ds(pl.multiple_of((me ^ k) * rows, rows), rows), :] = pieces[k][...]
    acc[...] = jnp.zeros_like(acc)
    offset = lax.broadcasted_iota(jnp.int32, (BLOCK, lanes), 0) - (
        lax.broadcasted_iota(jnp.int32, (BLOCK, lanes), 1) % BLOCK
    )
    blank = jnp.zeros((lanes, HEAD_DIM), jnp.bfloat16)

    def one_block(b, carry):
        own = me * (rows // BLOCK) + b
        base = (b * groups_here + group) * topk
        start = pl.multiple_of(b * BLOCK, BLOCK)
        picks = [chosen[base + i] for i in range(topk)]
        for i in range(topk):
            near[i * BLOCK : (i + 1) * BLOCK, :] = kv[
                pl.ds(pl.multiple_of(picks[i] * BLOCK, BLOCK), BLOCK), :
            ]
        q_rows = jnp.concatenate(
            [q_ref[pl.ds(start, BLOCK), h * HEAD_DIM : (h + 1) * HEAD_DIM] for h in range(heads_per)], axis=0
        )
        g_rows = jnp.concatenate(
            [g_ref[pl.ds(start, BLOCK), h * HEAD_DIM : (h + 1) * HEAD_DIM] for h in range(heads_per)], axis=0
        )
        both = jnp.concatenate(
            [jnp.concatenate([q_rows, blank], axis=1), jnp.concatenate([blank, g_rows], axis=1)], axis=0
        )
        scores[...] = lax.dot_general(
            near[...], both, (((1,), (1,)), ((), ())), preferred_element_type=jnp.float32
        )
        limits = [(own - picks[i]) * BLOCK for i in range(topk)]

        def masked(i):
            s = scores[i * BLOCK : (i + 1) * BLOCK, :lanes]
            return jnp.where(offset <= limits[i], s, -1e30)

        top = masked(0)
        for i in range(1, topk):
            top = jnp.maximum(top, masked(i))
        top = jnp.max(top, axis=0, keepdims=True)
        total = jnp.zeros((BLOCK, lanes), jnp.float32)
        delta = jnp.zeros((BLOCK, lanes), jnp.float32)
        for i in range(topk):
            part = slice(i * BLOCK, (i + 1) * BLOCK)
            e = jnp.exp2((masked(i) - top) * step)
            scores[part, :lanes] = e
            total = total + e
            delta = delta + e * scores[part, lanes:]
        total = 1.0 / jnp.sum(total, axis=0, keepdims=True)
        delta = jnp.sum(delta, axis=0, keepdims=True) * total
        for i in range(topk):
            part = slice(i * BLOCK, (i + 1) * BLOCK)
            w = scores[part, :lanes] * total
            packed[part, lanes:] = w.astype(jnp.bfloat16)
            packed[part, :lanes] = (w * (scores[part, lanes:] - delta)).astype(jnp.bfloat16)
        terms = jnp.dot(packed[...], both, preferred_element_type=jnp.float32)
        for i in range(topk):
            at = pl.ds(pl.multiple_of(picks[i] * BLOCK, BLOCK), BLOCK)
            acc[at, :] += terms[i * BLOCK : (i + 1) * BLOCK, :]
        dq = scaling * lax.dot_general(
            packed[:, :lanes],
            near[:, :HEAD_DIM],
            (((0,), (0,)), ((), ())),
            preferred_element_type=jnp.float32,
        )
        dq = dq.astype(jnp.bfloat16)
        for h in range(heads_per):
            dq_ref[pl.ds(start, BLOCK), h * HEAD_DIM : (h + 1) * HEAD_DIM] = dq[h * BLOCK : (h + 1) * BLOCK, :]
        return carry

    lax.fori_loop(0, rows // BLOCK, one_block, 0)

    for k in range(n_ctx // 2):
        for core, out in ((0, keep_ref), (1, send_ref)):
            at = pl.ds(pl.multiple_of((me ^ (2 * k + core)) * rows, rows), rows)
            out[k * rows : (k + 1) * rows, :HEAD_DIM] = (acc[at, :HEAD_DIM] * scaling).astype(jnp.bfloat16)
            out[k * rows : (k + 1) * rows, HEAD_DIM:] = acc[at, HEAD_DIM:].astype(jnp.bfloat16)


def attention(pieces, queries, grad_out, chosen, me, first_group, groups_here):
    n_ctx = len(pieces)
    rows = queries.shape[0]
    topk = chosen.shape[-1]
    wide = 2 * HEAD_DIM
    calls = pieces[0].shape[1] // wide
    width = queries.shape[1] // groups_here
    lanes = width // HEAD_DIM * BLOCK
    half = n_ctx // 2 * rows
    flops = calls * (rows // BLOCK) * 10 * topk * BLOCK * lanes * HEAD_DIM
    return pl.pallas_call(
        functools.partial(attention_kernel, n_ctx, topk, first_group, groups_here),
        out_shape=(
            jax.ShapeDtypeStruct((rows, calls * width), jnp.bfloat16),
            jax.ShapeDtypeStruct((half, calls * wide), jnp.bfloat16),
            jax.ShapeDtypeStruct((half, calls * wide), jnp.bfloat16),
        ),
        grid_spec=pltpu.PrefetchScalarGridSpec(
            num_scalar_prefetch=2,
            grid=(calls,),
            in_specs=[pl.BlockSpec((rows, wide), lambda j, *_: (0, j))] * n_ctx
            + [pl.BlockSpec((rows, width), lambda j, *_: (0, first_group + j))] * 2,
            out_specs=[
                pl.BlockSpec((rows, width), lambda j, *_: (0, j)),
                pl.BlockSpec((half, wide), lambda j, *_: (0, j)),
                pl.BlockSpec((half, wide), lambda j, *_: (0, j)),
            ],
            scratch_shapes=[
                pltpu.VMEM((n_ctx * rows, wide), jnp.bfloat16),
                pltpu.VMEM((n_ctx * rows, wide), jnp.float32),
                pltpu.VMEM((topk * BLOCK, wide), jnp.bfloat16),
                pltpu.VMEM((topk * BLOCK, 2 * lanes), jnp.float32),
                pltpu.VMEM((topk * BLOCK, 2 * lanes), jnp.bfloat16),
            ],
        ),
        compiler_params=pltpu.CompilerParams(vmem_limit_bytes=40 * 2**20),
        cost_estimate=pl.CostEstimate(
            flops=flops, bytes_accessed=8 * n_ctx * rows * wide * calls, transcendentals=0
        ),
        name="attention",
    )(chosen.reshape(-1), me.reshape(1), *pieces, queries, grad_out)


def projection_kernel(gq_ref, gk_ref, gv_ref, wq_ref, wk_ref, wv_ref, out_ref):
    contract = (((1,), (1,)), ((), ()))
    total = lax.dot_general(gq_ref[...], wq_ref[...], contract, preferred_element_type=jnp.float32)
    total += lax.dot_general(gk_ref[...], wk_ref[...], contract, preferred_element_type=jnp.float32)
    total += lax.dot_general(gv_ref[...], wv_ref[...], contract, preferred_element_type=jnp.float32)
    out_ref[...] = total.astype(jnp.bfloat16)


def projection(gq, gk, gv, wq, wk, wv):
    rows = gq.shape[0]
    out = wq.shape[0]
    tile = math.gcd(out, 512)
    held = lambda a: pl.BlockSpec(a.shape, lambda j: (0, 0))
    cut = lambda a: pl.BlockSpec((tile, a.shape[1]), lambda j: (j, 0))
    return pl.pallas_call(
        projection_kernel,
        out_shape=jax.ShapeDtypeStruct((rows, out), jnp.bfloat16),
        grid=(out // tile,),
        in_specs=[held(gq), held(gk), held(gv), cut(wq), cut(wk), cut(wv)],
        out_specs=pl.BlockSpec((rows, tile), lambda j: (0, j)),
        compiler_params=pltpu.CompilerParams(vmem_limit_bytes=40 * 2**20),
        name="projection",
    )(gq, gk, gv, wq, wk, wv)


def bits_of(mask):
    return [1 << i for i in range(mask.bit_length()) if mask >> i & 1]


def cuts_of(rows, count):
    edges = [rows * i // count // 16 * 16 for i in range(count)] + [rows]
    return [slice(edges[i], edges[i + 1]) for i in range(count)]


def exchange(x, axis, mask):
    n = lax.axis_size(axis)
    return lax.ppermute(x, axis, [(i, i ^ mask) for i in range(n)])


def gather_pieces(own, axis):
    n = lax.axis_size(axis)
    pieces = {0: own}
    far = sorted(range(2, n, 2), key=lambda m: (m.bit_count(), m))
    for mask in far:
        bits = bits_of(mask)
        cuts = cuts_of(own.shape[0], len(bits))
        parts = [exchange(pieces[mask ^ bit][cut], axis, bit) for bit, cut in zip(bits, cuts)]
        pieces[mask] = parts[0] if len(parts) == 1 else jnp.concatenate(parts, axis=0)
    for mask in range(0, n, 2):
        pieces[mask | 1] = exchange(pieces[mask], axis, 1)
    return [pieces[k] for k in range(n)]


def scatter_sum(keep, send, axis):
    n = lax.axis_size(axis)
    rows = keep.shape[0] // (n // 2)
    got = exchange(send, axis, 1)
    sums = {}
    for mask in range(0, n, 2):
        cut = slice(mask // 2 * rows, (mask // 2 + 1) * rows)
        sums[mask] = keep[cut].astype(jnp.float32) + got[cut].astype(jnp.float32)
    for mask in sorted(range(2, n, 2), key=lambda m: (-m.bit_count(), m)):
        bits = bits_of(mask)
        cuts = cuts_of(rows, len(bits))
        for bit, cut in zip(bits, cuts):
            part = exchange(sums[mask][cut].astype(jnp.bfloat16), axis, bit).astype(jnp.float32)
            whole = sums[mask ^ bit]
            pads = [(cut.start, rows - cut.stop), (0, 0)]
            sums[mask ^ bit] = whole + (part if part.shape == whole.shape else jnp.pad(part, pads))
    return sums[0].astype(jnp.bfloat16)


def line_scatter_sum(partial, axis):
    n = lax.axis_size(axis)
    me = lax.axis_index(axis)
    width = partial.shape[1] // n

    def chunk(d):
        return lax.dynamic_slice_in_dim(partial, jnp.clip(d, 0, n - 1) * width, width, 1).astype(jnp.float32)

    from_left = from_right = 0.0
    for t in range(1, n):
        right = (chunk(n - t + me) + from_left).astype(jnp.bfloat16)
        left = (chunk(t - n + me) + from_right).astype(jnp.bfloat16)
        from_left = lax.ppermute(right, axis, [(i, i + 1) for i in range(t)]).astype(jnp.float32)
        from_right = lax.ppermute(left, axis, [(n - 1 - i, n - 2 - i) for i in range(t)]).astype(jnp.float32)
    return (chunk(me) + from_left + from_right).astype(jnp.bfloat16)


def body(queries, keys, values, grad_out, chosen, w_query, w_key, w_value):
    groups = keys.shape[1] // HEAD_DIM
    rows = keys.shape[0]
    wide = 2 * HEAD_DIM
    me = lax.axis_index("ctx")
    pairs = jnp.concatenate(
        [keys.reshape(rows, groups, HEAD_DIM), values.reshape(rows, groups, HEAD_DIM)], axis=2
    ).reshape(rows, groups * wide)
    pieces = gather_pieces(pairs, "ctx")
    grad_queries, keep, send = attention(pieces, queries, grad_out, chosen, me, 0, groups)
    total = scatter_sum(keep, send, "ctx").reshape(rows, groups, wide)
    grad_keys = total[:, :, :HEAD_DIM].reshape(rows, groups * HEAD_DIM)
    grad_values = total[:, :, HEAD_DIM:].reshape(rows, groups * HEAD_DIM)
    partial = projection(grad_queries, grad_keys, grad_values, w_query, w_key, w_value)
    grad_input = line_scatter_sum(partial, "head")
    return (grad_queries, grad_keys, grad_values, grad_input)


def solution(mesh):
    return jax.shard_map(
        body,
        mesh=mesh,
        in_specs=(
            P("ctx", "head"),
            P("ctx", "head"),
            P("ctx", "head"),
            P("ctx", "head"),
            P("ctx", "head", None),
            P(None, "head"),
            P(None, "head"),
            P(None, "head"),
        ),
        out_specs=(P("ctx", "head"), P("ctx", "head"), P("ctx", "head"), P("ctx", "head")),
        check_vma=False,
    )
```

profile of v0, /device:TPU:16, one launch (start us, length us, event | category | flops | bytes accessed | tf_op | source)
XLA Modules:
  0.0 166.8 jit_solution(4056264368085468184)
XLA Ops:
  0.6 1.0 reshape.34
  1.6 1.0 reshape.35
  2.7 0.0 copy-start.16
  2.7 0.3 pad_maximum_fusion
  3.0 0.1 copy.12
  3.1 1.6 collective-permute-start.3
  4.7 1.5 collective-permute-start.1
  6.1 10.7 %collective-permute-done.3.refs_4_ = bf16[256,1024]{1,0:T(8,128)(2,1)S(1)} collective-permute-done((bf16[256,1024]{1,0:T(8,128)(2,1)S(1)}, bf16[256,1024]{1,0:T(8,128)(2,1)S(1)}, u32[]{:S(2)}, u32[]{:S(2)}) %collective-permute-start.3) | collective-permute-done | bytes 524320 | tf_op jit(solution)/shard_map/ppermute | solution.py:187
  16.8 1.6 collective-permute-start.5
  18.4 1.6 collective-permute-start.6
  20.0 0.5 collective-permute-start.2
  20.5 3.6 %collective-permute-done.5 = bf16[128,1024]{1,0:T(8,128)(2,1)S(1)} collective-permute-done((bf16[128,1024]{1,0:T(8,128)(2,1)S(1)}, bf16[128,1024]{1,0:T(8,128)(2,1)S(1)}, u32[]{:S(2)}, u32[]{:S(2)}) %collective-permute-start.5) | collective-permute-done | bytes 262176 | tf_op jit(solution)/shard_map/ppermute | solution.py:187
  24.1 1.3 collective-permute-done.6
  25.4 0.1 collective-permute-start.7
  25.5 0.8 copy-done.7
  26.3 0.1 reshape.32.chosen
  26.4 0.0 copy-start.11
  26.4 0.8 copy-done.11
  27.2 0.8 copy-done.13
  28.0 0.0 copy-start.6
  28.0 1.0 copy-done.6
  29.0 1.0 copy-done.8
  30.1 1.0 copy-done.9
  31.1 1.0 copy-done.10
  32.1 1.0 copy-done.12
  33.2 1.0 copy-done.14
  34.2 23.4 %attention.1 = (bf16[256,1024]{1,0:T(8,128)(2,1)}, bf16[1024,1024]{1,0:T(8,128)(2,1)S(1)}, bf16[1024,1024]{1,0:T(8,128)(2,1)S(1)}) custom-call(s32[256]{0:T(256)S(1)} %reshape.32.chosen, s32[1]{0:T(128)} %bitcast.place, bf16[256,1024]{1,0:T(8,128)(2,1)S(1)} %bitcast.12, bf16[256,1024]{1,0:T(8,128)(2,1)S(1)} %copy-done.12, bf16[256,1024]{1,0:T(8,128)(2,1)S(1)} %copy-done.6, ...), custom_call_target="tpu_custom_call" | custom-call | flops 2684354560 | bytes 16777216 | tf_op jit(solution)/shard_map/attention/pallas_call | solution.py:118
  57.6 0.5 collective-permute-start.8
  58.1 3.8 %collective-permute-done.8 = bf16[1024,1024]{1,0:T(8,128)(2,1)S(1)} collective-permute-done((bf16[1024,1024]{1,0:T(8,128)(2,1)S(1)}, bf16[1024,1024]{1,0:T(8,128)(2,1)S(1)}, u32[]{:S(2)}, u32[]{:S(2)}) %collective-permute-start.8) | collective-permute-done | bytes 2097184 | tf_op jit(solution)/shard_map/ppermute | solution.py:187
  61.9 0.2 add_convert_fusion.8
  62.1 1.2 collective-permute-start.11
  63.3 0.9 collective-permute-start.9
  64.3 6.5 %collective-permute-done.11 = bf16[128,1024]{1,0:T(8,128)(2,1)S(1)} collective-permute-done((bf16[128,1024]{1,0:T(8,128)(2,1)S(1)}, bf16[128,1024]{1,0:T(8,128)(2,1)S(1)}, u32[]{:S(2)}, u32[]{:S(2)}) %collective-permute-start.11) | collective-permute-done | bytes 262176 | tf_op jit(solution)/shard_map/ppermute | solution.py:187
  70.8 0.8 collective-permute-done.9
  71.6 1.3 add_convert_fusion.7
  72.9 0.9 collective-permute-start.10
  73.8 1.5 collective-permute-start.12
  75.3 10.8 %collective-permute-done.10 = bf16[256,1024]{1,0:T(8,128)(2,1)S(1)} collective-permute-done((bf16[256,1024]{1,0:T(8,128)(2,1)}, bf16[256,1024]{1,0:T(8,128)(2,1)S(1)}, u32[]{:S(2)}, u32[]{:S(2)}) %collective-permute-start.10) | collective-permute-done | bytes 524320 | tf_op jit(solution)/shard_map/ppermute | solution.py:187
  86.2 0.5 collective-permute-done.12
  86.7 1.6 add_convert_fusion.5
  88.3 0.4 reshape.37
  88.7 0.2 fusion
  88.9 0.1 copy_bitcast_fusion
  88.9 0.0 copy-start.2
  88.9 0.0 copy-start.3
  89.0 0.4 copy-done.4
  89.3 2.3 %copy-done = bf16[4608,512]{1,0:T(8,128)(2,1)S(1)} copy-done((bf16[4608,512]{1,0:T(8,128)(2,1)S(1)}, bf16[4608,512]{1,0:T(8,128)(2,1)}, u32[]{:S(2)}) %copy-start) | copy-done | bytes 4718616
  91.7 2.3 %copy-done.1 = bf16[4608,512]{1,0:T(8,128)(2,1)S(1)} copy-done((bf16[4608,512]{1,0:T(8,128)(2,1)S(1)}, bf16[4608,512]{1,0:T(8,128)(2,1)}, u32[]{:S(2)}) %copy-start.1) | copy-done | bytes 4718616
  94.0 10.0 %projection.1 = bf16[256,4608]{1,0:T(8,128)(2,1)S(1)} custom-call(bf16[256,1024]{1,0:T(8,128)(2,1)S(1)} %copy-done.4, bf16[256,512]{1,0:T(8,128)(2,1)S(1)} %get-tuple-element.21.gk_ref, bf16[256,512]{1,0:T(8,128)(2,1)S(1)} %get-tuple-element.20.gv_ref, bf16[4608,1024]{1,0:T(8,128)(2,1)} %wq_ref.1, bf16[4608,512]{1,0:T(8,128)(2,1)S(1)} %copy-done, ...), custom_call_target="tpu_custom_call" | custom-call | tf_op jit(solution)/shard_map/projection/pallas_call | solution.py:165
  104.0 0.9 constant_dynamic-slice_fusion.1
  104.9 1.5 collective-permute-start.13
  106.4 1.3 collective-permute-start.16
  107.7 2.1 %add_convert_fusion.4 = bf16[256,1152]{1,0:T(8,128)(2,1)} fusion(bf16[256,1152]{1,0:T(8,128)(2,1)} %collective-permute-done.13, bf16[256,4608]{1,0:T(8,128)(2,1)S(1)} %projection.1, s32[]{:T(128)S(6)} %select_n.23), kind=kLoop, calls=%fused_computation.4 | loop fusion | flops 1179648 | bytes 1769476 | tf_op jit(solution)/shard_map/convert_element_type | solution.py:233
  109.8 1.3 collective-permute-start.14
  111.1 10.5 %collective-permute-done.16 = bf16[256,1152]{1,0:T(8,128)(2,1)S(1)} collective-permute-done((bf16[256,1152]{1,0:T(8,128)(2,1)S(1)}, bf16[256,1152]{1,0:T(8,128)(2,1)S(1)}, u32[]{:S(2)}, u32[]{:S(2)}) %collective-permute-start.16) | collective-permute-done | bytes 589856 | tf_op jit(solution)/shard_map/ppermute | solution.py:236
  121.6 14.2 %collective-permute-done.14 = bf16[256,1152]{1,0:T(8,128)(2,1)} collective-permute-done((bf16[256,1152]{1,0:T(8,128)(2,1)}, bf16[256,1152]{1,0:T(8,128)(2,1)}, u32[]{:S(2)}, u32[]{:S(2)}) %collective-permute-start.14) | collective-permute-done | bytes 589856 | tf_op jit(solution)/shard_map/ppermute | solution.py:235
  135.7 2.4 %add_convert_fusion.3 = (bf16[256,1152]{1,0:T(8,128)(2,1)}, bf16[256,1152]{1,0:T(8,128)(2,1)}) fusion(bf16[256,1152]{1,0:T(8,128)(2,1)} %collective-permute-done.14, bf16[256,4608]{1,0:T(8,128)(2,1)S(1)} %projection.1, s32[]{:T(128)S(6)} %select_n.22, bf16[256,1152]{1,0:T(8,128)(2,1)S(1)} %collective-permute-done.16, s32[]{:T(128)S(6)} %select_n.26), kind=kLoop, calls=%fused_computation.3 | loop fusion | flops 2359296 | bytes 3538952 | tf_op jit(solution)/shard_map/convert_element_type | solution.py:233
  138.1 3.6 %collective-permute-start.17 = (bf16[256,1152]{1,0:T(8,128)(2,1)}, bf16[256,1152]{1,0:T(8,128)(2,1)S(1)}, u32[]{:S(2)}, u32[]{:S(2)}) collective-permute-start(bf16[256,1152]{1,0:T(8,128)(2,1)} %get-tuple-element.13), channel_id=1, source_target_pairs={{3,2},{2,1},{7,6},{6,5},{11,10},{10,9},{15,14},{14,13},{19,18},{18... | collective-permute-start | bytes 1769480 | tf_op jit(solution)/shard_map/ppermute | solution.py:236
  141.8 2.2 %collective-permute-start.15 = (bf16[256,1152]{1,0:T(8,128)(2,1)}, bf16[256,1152]{1,0:T(8,128)(2,1)S(1)}, u32[]{:S(2)}, u32[]{:S(2)}) collective-permute-start(bf16[256,1152]{1,0:T(8,128)(2,1)} %get-tuple-element.12), channel_id=1, source_target_pairs={{0,1},{1,2},{2,3},{4,5},{5,6},{6,7},{8,9},{9,10},{10,11},{12,13},{... | collective-permute-start | bytes 1769480 | tf_op jit(solution)/shard_map/ppermute | solution.py:235
  144.0 7.9 %collective-permute-done.17 = bf16[256,1152]{1,0:T(8,128)(2,1)S(1)} collective-permute-done((bf16[256,1152]{1,0:T(8,128)(2,1)}, bf16[256,1152]{1,0:T(8,128)(2,1)S(1)}, u32[]{:S(2)}, u32[]{:S(2)}) %collective-permute-start.17) | collective-permute-done | bytes 589856 | tf_op jit(solution)/shard_map/ppermute | solution.py:236
  151.9 1.0 add_convert_fusion.1
  152.9 3.3 %collective-permute-start.18 = (bf16[256,1152]{1,0:T(8,128)(2,1)}, bf16[256,1152]{1,0:T(8,128)(2,1)S(1)}, u32[]{:S(2)}, u32[]{:S(2)}) collective-permute-start(bf16[256,1152]{1,0:T(8,128)(2,1)} %add_convert_fusion.1), channel_id=1, source_target_pairs={{3,2},{2,1},{1,0},{7,6},{6,5},{5,4},{11,10},{10,9},{9,8},{15,14},{... | collective-permute-start | bytes 1769480 | tf_op jit(solution)/shard_map/ppermute | solution.py:236
  156.3 9.5 %collective-permute-done.18 = bf16[256,1152]{1,0:T(8,128)(2,1)S(1)} collective-permute-done((bf16[256,1152]{1,0:T(8,128)(2,1)}, bf16[256,1152]{1,0:T(8,128)(2,1)S(1)}, u32[]{:S(2)}, u32[]{:S(2)}) %collective-permute-start.18) | collective-permute-done | bytes 589856 | tf_op jit(solution)/shard_map/ppermute | solution.py:236
  165.8 1.1 add_convert_fusion
  (31 shorter events, 0.2 us)
Async XLA Ops:
  2.7 23.6 %copy-start.16 = (s32[4,4,16]{2,1,0:T(4,128)S(1)}, s32[4,4,16]{2,1,0:T(4,128)}, u32[]{:S(2)}) copy-start(s32[4,4,16]{2,1,0:T(4,128)} %param.12) | copy-start | bytes 3076
  3.1 13.7 %collective-permute-start.3 = (bf16[256,1024]{1,0:T(8,128)(2,1)S(1)}, bf16[256,1024]{1,0:T(8,128)(2,1)S(1)}, u32[]{:S(2)}, u32[]{:S(2)}) collective-permute-start(bf16[256,1024]{1,0:T(8,128)(2,1)S(1)} %bitcast.9), channel_id=1, source_target_pairs={{0,16},{4,20},{8,24},{12,28},{16,0},{20,4},{24,8},{28,12},{1,17},{... | collective-permute-start | bytes 1572872 | tf_op jit(solution)/shard_map/ppermute | solution.py:187
  4.7 13.7 %collective-permute-start.1 = (bf16[256,1024]{1,0:T(8,128)(2,1)S(1)}, bf16[256,1024]{1,0:T(8,128)(2,1)S(1)}, u32[]{:S(2)}, u32[]{:S(2)}) collective-permute-start(bf16[256,1024]{1,0:T(8,128)(2,1)S(1)} %bitcast.10), channel_id=1, source_target_pairs={{0,8},{4,12},{8,0},{12,4},{16,24},{20,28},{24,16},{28,20},{1,9},{5... | collective-permute-start | bytes 1572872 | tf_op jit(solution)/shard_map/ppermute | solution.py:187
  16.8 7.2 %collective-permute-start.5 = (bf16[128,1024]{1,0:T(8,128)(2,1)S(1)}, bf16[128,1024]{1,0:T(8,128)(2,1)S(1)}, u32[]{:S(2)}, u32[]{:S(2)}) collective-permute-start(bf16[128,1024]{1,0:T(8,128)(2,1)S(1)} %slice.58), channel_id=1, source_target_pairs={{0,8},{4,12},{8,0},{12,4},{16,24},{20,28},{24,16},{28,20},{1,9},{5... | collective-permute-start | bytes 786440 | tf_op jit(solution)/shard_map/ppermute | solution.py:187
  18.4 9.6 %copy-start.5 = (bf16[256,1024]{1,0:T(8,128)(2,1)}, bf16[256,1024]{1,0:T(8,128)(2,1)S(1)}, u32[]{:S(2)}) copy-start(bf16[256,1024]{1,0:T(8,128)(2,1)S(1)} %collective-permute-done.1.refs_2_) | copy-start | bytes 1572868
  18.4 7.0 %collective-permute-start.6 = (bf16[128,1024]{1,0:T(8,128)(2,1)S(1)}, bf16[128,1024]{1,0:T(8,128)(2,1)S(1)}, u32[]{:S(2)}, u32[]{:S(2)}) collective-permute-start(bf16[128,1024]{1,0:T(8,128)(2,1)S(1)} %slice.59), channel_id=1, source_target_pairs={{0,16},{4,20},{8,24},{12,28},{16,0},{20,4},{24,8},{28,12},{1,17},{... | collective-permute-start | bytes 786440 | tf_op jit(solution)/shard_map/ppermute | solution.py:187
  20.0 6.4 %collective-permute-start = (bf16[256,1024]{1,0:T(8,128)(2,1)S(1)}, bf16[256,1024]{1,0:T(8,128)(2,1)S(1)}, u32[]{:S(2)}, u32[]{:S(2)}) collective-permute-start(bf16[256,1024]{1,0:T(8,128)(2,1)S(1)} %bitcast.11), channel_id=1, source_target_pairs={{0,4},{4,0},{8,12},{12,8},{16,20},{20,16},{24,28},{28,24},{1,5},{5... | collective-permute-start | bytes 1572872 | tf_op jit(solution)/shard_map/ppermute | solution.py:187
  20.0 7.2 %collective-permute-start.2 = (bf16[256,1024]{1,0:T(8,128)(2,1)S(1)}, bf16[256,1024]{1,0:T(8,128)(2,1)S(1)}, u32[]{:S(2)}, u32[]{:S(2)}) collective-permute-start(bf16[256,1024]{1,0:T(8,128)(2,1)S(1)} %collective-permute-done.1.refs_2_), channel_id=1, source_target_pairs={{0,4},{4,0},{8,12},{12,8},{16,20},{20,16},{24,28},{28,24},{1,5},{5... | collective-permute-start | bytes 1572872 | tf_op jit(solution)/shard_map/ppermute | solution.py:187
  20.5 7.5 %collective-permute-start.4 = (bf16[256,1024]{1,0:T(8,128)(2,1)S(1)}, bf16[256,1024]{1,0:T(8,128)(2,1)}, u32[]{:S(2)}, u32[]{:S(2)}) collective-permute-start(bf16[256,1024]{1,0:T(8,128)(2,1)S(1)} %collective-permute-done.3.refs_4_), channel_id=1, source_target_pairs={{0,4},{4,0},{8,12},{12,8},{16,20},{20,16},{24,28},{28,24},{1,5},{5... | collective-permute-start | bytes 1572872 | tf_op jit(solution)/shard_map/ppermute | solution.py:187
  25.4 2.6 %collective-permute-start.7 = (bf16[256,1024]{1,0:T(8,128)(2,1)S(1)}, bf16[256,1024]{1,0:T(8,128)(2,1)}, u32[]{:S(2)}, u32[]{:S(2)}) collective-permute-start(bf16[256,1024]{1,0:T(8,128)(2,1)S(1)} %constant_dynamic-update-slice_fusion.refs_6_), channel_id=1, source_target_pairs={{0,4},{4,0},{8,12},{12,8},{16,20},{20,16},{24,28},{28,24},{1,5},{5... | collective-permute-start | bytes 1572872 | tf_op jit(solution)/shard_map/ppermute | solution.py:187
  25.5 0.8 copy-start.7
  26.4 0.8 copy-start.11
  27.2 0.8 copy-start.13
  28.0 1.0 copy-start.6
  29.0 1.0 copy-start.8
  30.1 1.0 copy-start.9
  31.1 1.0 copy-start.10
  32.1 1.0 copy-start.12
  33.2 1.0 copy-start.14
  57.6 4.3 %collective-permute-start.8 = (bf16[1024,1024]{1,0:T(8,128)(2,1)S(1)}, bf16[1024,1024]{1,0:T(8,128)(2,1)S(1)}, u32[]{:S(2)}, u32[]{:S(2)}) collective-permute-start(bf16[1024,1024]{1,0:T(8,128)(2,1)S(1)} %get-tuple-element.9), channel_id=1, source_target_pairs={{0,4},{4,0},{8,12},{12,8},{16,20},{20,16},{24,28},{28,24},{1,5},{5... | collective-permute-start | bytes 6291464 | tf_op jit(solution)/shard_map/ppermute | solution.py:187
  61.9 11.0 %copy-start.15 = (bf16[1024,1024]{1,0:T(8,128)(2,1)}, bf16[1024,1024]{1,0:T(8,128)(2,1)S(1)}, u32[]{:S(2)}) copy-start(bf16[1024,1024]{1,0:T(8,128)(2,1)S(1)} %collective-permute-done.8) | copy-start | bytes 6291460
  62.1 8.7 %collective-permute-start.11 = (bf16[128,1024]{1,0:T(8,128)(2,1)S(1)}, bf16[128,1024]{1,0:T(8,128)(2,1)S(1)}, u32[]{:S(2)}, u32[]{:S(2)}) collective-permute-start(bf16[128,1024]{1,0:T(8,128)(2,1)S(1)} %get-tuple-element.19), channel_id=1, source_target_pairs={{0,8},{4,12},{8,0},{12,4},{16,24},{20,28},{24,16},{28,20},{1,9},{5... | collective-permute-start | bytes 786440 | tf_op jit(solution)/shard_map/ppermute | solution.py:187
  63.3 8.3 %collective-permute-start.9 = (bf16[128,1024]{1,0:T(8,128)(2,1)S(1)}, bf16[128,1024]{1,0:T(8,128)(2,1)S(1)}, u32[]{:S(2)}, u32[]{:S(2)}) collective-permute-start(bf16[128,1024]{1,0:T(8,128)(2,1)S(1)} %get-tuple-element.18), channel_id=1, source_target_pairs={{0,16},{4,20},{8,24},{12,28},{16,0},{20,4},{24,8},{28,12},{1,17},{... | collective-permute-start | bytes 786440 | tf_op jit(solution)/shard_map/ppermute | solution.py:187
  72.9 13.3 %collective-permute-start.10 = (bf16[256,1024]{1,0:T(8,128)(2,1)}, bf16[256,1024]{1,0:T(8,128)(2,1)S(1)}, u32[]{:S(2)}, u32[]{:S(2)}) collective-permute-start(bf16[256,1024]{1,0:T(8,128)(2,1)} %get-tuple-element.10), channel_id=1, source_target_pairs={{0,8},{4,12},{8,0},{12,4},{16,24},{20,28},{24,16},{28,20},{1,9},{5... | collective-permute-start | bytes 1572872 | tf_op jit(solution)/shard_map/ppermute | solution.py:187
  73.8 12.9 %collective-permute-start.12 = (bf16[256,1024]{1,0:T(8,128)(2,1)S(1)}, bf16[256,1024]{1,0:T(8,128)(2,1)}, u32[]{:S(2)}, u32[]{:S(2)}) collective-permute-start(bf16[256,1024]{1,0:T(8,128)(2,1)S(1)} %get-tuple-element.11), channel_id=1, source_target_pairs={{0,16},{4,20},{8,24},{12,28},{16,0},{20,4},{24,8},{28,12},{1,17},{... | collective-permute-start | bytes 1572872 | tf_op jit(solution)/shard_map/ppermute | solution.py:187
  88.3 1.0 copy-start.4
  88.9 15.1 %copy-start.2 = (bf16[256,512]{1,0:T(8,128)(2,1)}, bf16[256,512]{1,0:T(8,128)(2,1)S(1)}, u32[]{:S(2)}) copy-start(bf16[256,512]{1,0:T(8,128)(2,1)S(1)} %get-tuple-element.20.gv_ref) | copy-start | bytes 786436
  88.9 15.1 %copy-start.3 = (bf16[256,512]{1,0:T(8,128)(2,1)}, bf16[256,512]{1,0:T(8,128)(2,1)S(1)}, u32[]{:S(2)}) copy-start(bf16[256,512]{1,0:T(8,128)(2,1)S(1)} %get-tuple-element.21.gk_ref) | copy-start | bytes 786436
  89.3 2.3 %copy-start = (bf16[4608,512]{1,0:T(8,128)(2,1)S(1)}, bf16[4608,512]{1,0:T(8,128)(2,1)}, u32[]{:S(2)}) copy-start(bf16[4608,512]{1,0:T(8,128)(2,1)} %wk_ref.1) | copy-start | bytes 14155780
  91.7 2.3 %copy-start.1 = (bf16[4608,512]{1,0:T(8,128)(2,1)S(1)}, bf16[4608,512]{1,0:T(8,128)(2,1)}, u32[]{:S(2)}) copy-start(bf16[4608,512]{1,0:T(8,128)(2,1)} %wv_ref.1) | copy-start | bytes 14155780
  104.9 2.8 %collective-permute-start.13 = (bf16[256,1152]{1,0:T(8,128)(2,1)}, bf16[256,1152]{1,0:T(8,128)(2,1)}, u32[]{:S(2)}, u32[]{:S(2)}) collective-permute-start(bf16[256,1152]{1,0:T(8,128)(2,1)} %get-tuple-element.14), channel_id=1, source_target_pairs={{0,1},{4,5},{8,9},{12,13},{16,17},{20,21},{24,25},{28,29}} | collective-permute-start | bytes 1769480 | tf_op jit(solution)/shard_map/ppermute | solution.py:235
  106.4 15.1 %collective-permute-start.16 = (bf16[256,1152]{1,0:T(8,128)(2,1)S(1)}, bf16[256,1152]{1,0:T(8,128)(2,1)S(1)}, u32[]{:S(2)}, u32[]{:S(2)}) collective-permute-start(bf16[256,1152]{1,0:T(8,128)(2,1)S(1)} %get-tuple-element.15), channel_id=1, source_target_pairs={{3,2},{7,6},{11,10},{15,14},{19,18},{23,22},{27,26},{31,30}} | collective-permute-start | bytes 1769480 | tf_op jit(solution)/shard_map/ppermute | solution.py:236
  109.8 25.9 %collective-permute-start.14 = (bf16[256,1152]{1,0:T(8,128)(2,1)}, bf16[256,1152]{1,0:T(8,128)(2,1)}, u32[]{:S(2)}, u32[]{:S(2)}) collective-permute-start(bf16[256,1152]{1,0:T(8,128)(2,1)} %add_convert_fusion.4), channel_id=1, source_target_pairs={{0,1},{1,2},{4,5},{5,6},{8,9},{9,10},{12,13},{13,14},{16,17},{17,1... | collective-permute-start | bytes 1769480 | tf_op jit(solution)/shard_map/ppermute | solution.py:235
  138.1 13.8 %collective-permute-start.17 = (bf16[256,1152]{1,0:T(8,128)(2,1)}, bf16[256,1152]{1,0:T(8,128)(2,1)S(1)}, u32[]{:S(2)}, u32[]{:S(2)}) collective-permute-start(bf16[256,1152]{1,0:T(8,128)(2,1)} %get-tuple-element.13), channel_id=1, source_target_pairs={{3,2},{2,1},{7,6},{6,5},{11,10},{10,9},{15,14},{14,13},{19,18},{18... | collective-permute-start | bytes 1769480 | tf_op jit(solution)/shard_map/ppermute | solution.py:236
  141.8 14.5 %collective-permute-start.15 = (bf16[256,1152]{1,0:T(8,128)(2,1)}, bf16[256,1152]{1,0:T(8,128)(2,1)S(1)}, u32[]{:S(2)}, u32[]{:S(2)}) collective-permute-start(bf16[256,1152]{1,0:T(8,128)(2,1)} %get-tuple-element.12), channel_id=1, source_target_pairs={{0,1},{1,2},{2,3},{4,5},{5,6},{6,7},{8,9},{9,10},{10,11},{12,13},{... | collective-permute-start | bytes 1769480 | tf_op jit(solution)/shard_map/ppermute | solution.py:235
  152.9 12.9 %collective-permute-start.18 = (bf16[256,1152]{1,0:T(8,128)(2,1)}, bf16[256,1152]{1,0:T(8,128)(2,1)S(1)}, u32[]{:S(2)}, u32[]{:S(2)}) collective-permute-start(bf16[256,1152]{1,0:T(8,128)(2,1)} %add_convert_fusion.1), channel_id=1, source_target_pairs={{3,2},{2,1},{1,0},{7,6},{6,5},{5,4},{11,10},{10,9},{9,8},{15,14},{... | collective-permute-start | bytes 1769480 | tf_op jit(solution)/shard_map/ppermute | solution.py:236
where the time goes:
time: 170 us; the launch traced here: 167 us
  waiting for transfers between devices  80.1 us (47%)
  Pallas kernels  33.3 us (20%)
  starting transfers between devices  25.1 us (15%)
  local copies, waits for them, and re-layouts  17.6 us (10%)
  other arithmetic  9.83 us (6%)
    ppermute x13, waiting for transfers between devices, exchange(): return lax.ppermute(x, axis, [(i, i ^ mask) for i in range(n)])  38 us
    ppermute x3, waiting for transfers between devices, line_scatter_sum(): lax.ppermute(left, axis, [(n - 1 - i, n - 2 - i) for i in range(t)])  27.9 us
    pallas_call x1, Pallas kernels, attention(): pl.pallas_call(functools.partial(attention_kernel, n_ctx, topk, first_gro...  23.4 us
    ppermute x3, waiting for transfers between devices, line_scatter_sum(): lax.ppermute(right, axis, [(i, i + 1) for i in range(t)])  14.2 us
    unnamed x36, local copies, waits for them, and re-layouts  13.8 us
    ppermute x13, starting transfers between devices, exchange(): return lax.ppermute(x, axis, [(i, i ^ mask) for i in range(n)])  11.9 us
    pallas_call x1, Pallas kernels, projection(): pl.pallas_call(projection_kernel, out_shape=jax.ShapeDtypeStruct((rows, o...  9.98 us
    ppermute x3, starting transfers between devices, line_scatter_sum(): lax.ppermute(left, axis, [(n - 1 - i, n - 2 - i) for i in range(t)])  8.25 us
  transfers between devices with their start and end apart: 19, of which 12 were waited for; matrix products, arithmetic and copies ran while one was open for 2% of the time, Pallas kernels for 0%

commit v1 on v0

v1 whole, which is shorter than its diff:
```python
import functools
import math

import jax
import jax.numpy as jnp
from jax import lax
from jax.experimental import pallas as pl
from jax.experimental.pallas import tpu as pltpu
from jax.sharding import PartitionSpec as P

HEAD_DIM = 128
BLOCK = 64
LOG2E = math.log2(math.e)


def attention_kernel(n_ctx, topk, first_group, groups_here, calls, chosen, place, *refs):
    pieces = refs[:n_ctx]
    q_ref, g_ref = refs[n_ctx : n_ctx + 2]
    dq_ref, keep_ref, send_ref = refs[n_ctx + 2 : n_ctx + 5]
    kv, acc, near, scores, packed, operand, arrived = refs[n_ctx + 5 :]
    rows = q_ref.shape[0]
    wide = 2 * HEAD_DIM
    width = q_ref.shape[1] // calls
    heads_per = width // HEAD_DIM
    lanes = heads_per * BLOCK
    blocks = rows // BLOCK
    me = place[0]
    scaling = 1.0 / math.sqrt(HEAD_DIM)
    step = scaling * LOG2E

    def piece_rows(k):
        return pl.ds(pl.multiple_of((me ^ k) * rows, rows), rows)

    def arrival(j, k):
        return pltpu.make_async_copy(
            pieces[k].at[:, pl.ds(j * wide, wide)], kv.at[j, piece_rows(k), :], arrived.at[j, k]
        )

    for j in range(calls):
        for k in range(n_ctx):
            arrival(j, k).start()
    acc[...] = jnp.zeros_like(acc)
    operand[...] = jnp.zeros_like(operand)
    offset = lax.broadcasted_iota(jnp.int32, (BLOCK, lanes), 0) - (
        lax.broadcasted_iota(jnp.int32, (BLOCK, lanes), 1) % BLOCK
    )

    def picks_of(j, b):
        own = me * blocks + b
        base = (b * groups_here + first_group + j) * topk
        listed = [chosen[base + i] for i in range(topk)]
        return own, [own] + [jnp.where(listed[i] == own, listed[0], listed[i]) for i in range(1, topk)]

    def tile(i):
        return slice(i * BLOCK, (i + 1) * BLOCK)

    def score_stage(j, b, slot):
        _, picks = picks_of(j, b)
        for i in range(topk):
            near[slot, tile(i), :] = kv[j, pl.ds(pl.multiple_of(picks[i] * BLOCK, BLOCK), BLOCK), :]
        for h in range(heads_per):
            at = slice(j * width + h * HEAD_DIM, j * width + (h + 1) * HEAD_DIM)
            operand[slot, tile(h), :HEAD_DIM] = q_ref[tile(b), at]
            operand[slot, lanes + h * BLOCK : lanes + (h + 1) * BLOCK, HEAD_DIM:] = g_ref[tile(b), at]
        scores[slot] = lax.dot_general(
            near[slot], operand[slot], (((1,), (1,)), ((), ())), preferred_element_type=jnp.float32
        )

    def weight_stage(j, b, slot):
        own, picks = picks_of(j, b)
        bias = [jnp.where(picks[i] > own, -1e30, 0.0) for i in range(topk)]
        first = jnp.where(offset <= 0, scores[slot, tile(0), :lanes], -1e30)
        top = first
        for i in range(1, topk):
            top = jnp.maximum(top, scores[slot, tile(i), :lanes] + bias[i])
        top = jnp.max(top, axis=0, keepdims=True)
        total = jnp.zeros((BLOCK, lanes), jnp.float32)
        delta = jnp.zeros((BLOCK, lanes), jnp.float32)
        for i in range(topk):
            s = first - top if i == 0 else scores[slot, tile(i), :lanes] - (top - bias[i])
            e = jnp.exp2(s * step)
            scores[slot, tile(i), :lanes] = e
            total = total + e
            delta = delta + e * scores[slot, tile(i), lanes:]
        total = 1.0 / jnp.sum(total, axis=0, keepdims=True)
        delta = jnp.sum(delta, axis=0, keepdims=True) * total
        for i in range(topk):
            w = scores[slot, tile(i), :lanes] * total
            packed[slot, tile(i), lanes:] = w.astype(jnp.bfloat16)
            packed[slot, tile(i), :lanes] = (w * (scores[slot, tile(i), lanes:] - delta)).astype(jnp.bfloat16)

    def term_stage(j, b, slot):
        _, picks = picks_of(j, b)
        terms = jnp.dot(packed[slot], operand[slot], preferred_element_type=jnp.float32)
        for i in range(topk):
            at = pl.ds(pl.multiple_of(picks[i] * BLOCK, BLOCK), BLOCK)
            acc[j, at, :] += terms[tile(i), :]
        dq = scaling * lax.dot_general(
            packed[slot, :, :lanes],
            near[slot, :, :HEAD_DIM],
            (((0,), (0,)), ((), ())),
            preferred_element_type=jnp.float32,
        )
        dq = dq.astype(jnp.bfloat16)
        for h in range(heads_per):
            dq_ref[tile(b), j * width + h * HEAD_DIM : j * width + (h + 1) * HEAD_DIM] = dq[tile(h), :]

    def out_stage(j):
        for k in range(n_ctx // 2):
            to = slice(k * rows, (k + 1) * rows)
            for core, out in ((0, keep_ref), (1, send_ref)):
                at = piece_rows(2 * k + core)
                cols = slice(j * wide, j * wide + HEAD_DIM)
                out[to, cols] = (acc[j, at, :HEAD_DIM] * scaling).astype(jnp.bfloat16)
                cols = slice(j * wide + HEAD_DIM, (j + 1) * wide)
                out[to, cols] = acc[j, at, HEAD_DIM:].astype(jnp.bfloat16)

    slots = near.shape[0]
    work = [(j, b) for j in range(calls) for b in range(blocks)]
    for t in range(len(work) + 2):
        if t < len(work):
            j, b = work[t]
            if b == 0:
                for k in range(n_ctx):
                    arrival(j, k).wait()
            score_stage(j, b, t % slots)
        if 1 <= t <= len(work):
            weight_stage(*work[t - 1], (t - 1) % slots)
        if t >= 2:
            term_stage(*work[t - 2], (t - 2) % slots)
            if work[t - 2][1] == blocks - 1:
                out_stage(work[t - 2][0])


def attention(pieces, queries, grad_out, chosen, me, first_group, groups_here):
    n_ctx = len(pieces)
    rows = queries.shape[0]
    topk = chosen.shape[-1]
    wide = 2 * HEAD_DIM
    calls = pieces[0].shape[1] // wide
    width = queries.shape[1] // groups_here
    lanes = width // HEAD_DIM * BLOCK
    half = n_ctx // 2 * rows
    flops = calls * (rows // BLOCK) * 10 * topk * BLOCK * lanes * HEAD_DIM
    slots = 3
    whole = lambda shape: pl.BlockSpec(shape, lambda j, *_: (0, 0))
    return pl.pallas_call(
        functools.partial(attention_kernel, n_ctx, topk, first_group, groups_here, calls),
        out_shape=(
            jax.ShapeDtypeStruct((rows, calls * width), jnp.bfloat16),
            jax.ShapeDtypeStruct((half, calls * wide), jnp.bfloat16),
            jax.ShapeDtypeStruct((half, calls * wide), jnp.bfloat16),
        ),
        grid_spec=pltpu.PrefetchScalarGridSpec(
            num_scalar_prefetch=2,
            grid=(1,),
            in_specs=[pl.BlockSpec(memory_space=pltpu.HBM)] * n_ctx
            + [pl.BlockSpec((rows, calls * width), lambda j, *_: (0, first_group // calls))] * 2,
            out_specs=[
                whole((rows, calls * width)),
                whole((half, calls * wide)),
                whole((half, calls * wide)),
            ],
            scratch_shapes=[
                pltpu.VMEM((calls, n_ctx * rows, wide), jnp.bfloat16),
                pltpu.VMEM((calls, n_ctx * rows, wide), jnp.float32),
                pltpu.VMEM((slots, topk * BLOCK, wide), jnp.bfloat16),
                pltpu.VMEM((slots, topk * BLOCK, 2 * lanes), jnp.float32),
                pltpu.VMEM((slots, topk * BLOCK, 2 * lanes), jnp.bfloat16),
                pltpu.VMEM((slots, 2 * lanes, wide), jnp.bfloat16),
                pltpu.SemaphoreType.DMA((calls, n_ctx)),
            ],
        ),
        compiler_params=pltpu.CompilerParams(vmem_limit_bytes=56 * 2**20),
        cost_estimate=pl.CostEstimate(
            flops=flops, bytes_accessed=8 * n_ctx * rows * wide * calls, transcendentals=0
        ),
        name="attention",
    )(chosen.reshape(-1), me.reshape(1), *pieces, queries, grad_out)


def projection_kernel(chunks, width, summed, order, *refs):
    gq_ref, *parts = refs[: summed + 1]
    wq_ref, wk_ref, wv_ref = refs[summed + 1 : summed + 4]
    outs = refs[summed + 4 :]
    if summed > 2:
        gk_ref, gv_ref, *outs = outs
    else:
        gk_ref, gv_ref = parts
    out_refs, (wq, wk, wv, arrived) = outs[:chunks], outs[chunks:]

    def arrivals(i):
        at = pl.ds(pl.multiple_of(order[i] * width, width), width)
        return [
            pltpu.make_async_copy(src.at[at, :], dst.at[i], arrived.at[i, k])
            for k, (src, dst) in enumerate(((wq_ref, wq), (wk_ref, wk), (wv_ref, wv)))
        ]

    for i in range(chunks):
        for copy in arrivals(i):
            copy.start()
    if summed > 2:
        groups = gk_ref.shape[1] // HEAD_DIM
        for g in range(groups):
            for side, out in ((0, gk_ref), (1, gv_ref)):
                at = slice((2 * g + side) * HEAD_DIM, (2 * g + side + 1) * HEAD_DIM)
                total = parts[0][:, at].astype(jnp.float32)
                for part in parts[1:]:
                    total += part[:, at].astype(jnp.float32)
                out[:, g * HEAD_DIM : (g + 1) * HEAD_DIM] = total.astype(jnp.bfloat16)
    contract = (((1,), (1,)), ((), ()))
    for i in range(chunks):
        copies = arrivals(i)
        copies[0].wait()
        total = lax.dot_general(gq_ref[...], wq[i], contract, preferred_element_type=jnp.float32)
        copies[1].wait()
        total += lax.dot_general(gk_ref[...], wk[i], contract, preferred_element_type=jnp.float32)
        copies[2].wait()
        total += lax.dot_general(gv_ref[...], wv[i], contract, preferred_element_type=jnp.float32)
        out_refs[i][...] = total.astype(jnp.bfloat16)


def projection(order, shares, gq, parts, weights):
    rows = gq.shape[0]
    chunks = order.shape[0]
    width = weights[0].shape[0] // shares
    columns = weights[1].shape[1]
    out_shape = [jax.ShapeDtypeStruct((rows, width), jnp.bfloat16)] * chunks
    if len(parts) > 2:
        out_shape = [jax.ShapeDtypeStruct((rows, columns), jnp.bfloat16)] * 2 + out_shape
    front = lambda shape: pl.BlockSpec(shape, lambda j, *_: (0, 0))
    return pl.pallas_call(
        functools.partial(projection_kernel, chunks, width, len(parts)),
        out_shape=out_shape,
        grid_spec=pltpu.PrefetchScalarGridSpec(
            num_scalar_prefetch=1,
            grid=(1,),
            in_specs=[front(gq.shape)]
            + [front((rows, part.shape[1])) for part in parts]
            + [pl.BlockSpec(memory_space=pltpu.HBM)] * 3,
            out_specs=[front(shape.shape) for shape in out_shape],
            scratch_shapes=[pltpu.VMEM((chunks, width, w.shape[1]), jnp.bfloat16) for w in weights]
            + [pltpu.SemaphoreType.DMA((chunks, 3))],
        ),
        compiler_params=pltpu.CompilerParams(vmem_limit_bytes=56 * 2**20),
        cost_estimate=pl.CostEstimate(
            flops=2 * chunks * width * rows * (gq.shape[1] + 2 * columns),
            bytes_accessed=2 * chunks * width * (gq.shape[1] + 2 * columns),
            transcendentals=0,
        ),
        name="projection",
    )(order, gq, *parts, *weights)


def bits_of(mask):
    return [1 << i for i in range(mask.bit_length()) if mask >> i & 1]


def cuts_of(rows, count):
    edges = [rows * i // count // 16 * 16 for i in range(count)] + [rows]
    return [slice(edges[i], edges[i + 1]) for i in range(count)]


def exchange(x, axis, mask):
    n = lax.axis_size(axis)
    return lax.ppermute(x, axis, [(i, i ^ mask) for i in range(n)])


def gather_pieces(own, axis):
    n = lax.axis_size(axis)
    pieces = {0: own}
    far = sorted(range(2, n, 2), key=lambda m: (m.bit_count(), m))
    for mask in far:
        bits = bits_of(mask)
        cuts = cuts_of(own.shape[0], len(bits))
        parts = [exchange(pieces[mask ^ bit][cut], axis, bit) for bit, cut in zip(bits, cuts)]
        pieces[mask] = parts[0] if len(parts) == 1 else jnp.concatenate(parts, axis=0)
    for mask in range(0, n, 2):
        pieces[mask | 1] = exchange(pieces[mask], axis, 1)
    return [pieces[k] for k in range(n)]


def scatter_parts(keep, send, axis):
    n = lax.axis_size(axis)
    rows = keep.shape[0] // (n // 2)
    got = exchange(send, axis, 1)
    parts = [keep, got]
    for mask in range(n - 2, 0, -2):
        cut = slice(mask // 2 * rows, (mask // 2 + 1) * rows)
        both = keep[cut].astype(jnp.float32) + got[cut].astype(jnp.float32)
        parts.append(exchange(both.astype(jnp.bfloat16), axis, mask))
    return parts


def line_order(n, me):
    if n == 4:
        return me ^ jnp.array([2, 3, 1, 0], jnp.int32)
    return (me + 1 + jnp.arange(n, dtype=jnp.int32)) % n


def line_sum(chunks, axis):
    n = lax.axis_size(axis)
    me = lax.axis_index(axis)
    wide = lambda x: x.astype(jnp.float32)
    if n == 4:
        first, second, third, own = chunks
        got_first = lax.ppermute(first, axis, [(0, 1), (3, 2), (1, 3), (2, 0)])
        got_second = lax.ppermute(second, axis, [(0, 3), (3, 0)])
        got_third = lax.ppermute(third, axis, [(0, 1), (2, 3), (1, 0), (3, 2)])
        passed = (wide(second) + wide(got_first)).astype(jnp.bfloat16)
        got_passed = lax.ppermute(passed, axis, [(1, 2), (2, 1)])
        outer = jnp.logical_or(me == 0, me == 3)
        total = wide(own) + jnp.where(outer, wide(got_first), 0.0)
        return (total + wide(got_second) + wide(got_third) + wide(got_passed)).astype(jnp.bfloat16)
    stacked = jnp.stack(chunks)

    def chunk(d):
        return wide(lax.dynamic_index_in_dim(stacked, (d - me - 1) % n, 0, keepdims=False))

    from_left = from_right = 0.0
    for t in range(1, n):
        right = (chunk(n - t + me) + from_left).astype(jnp.bfloat16)
        left = (chunk(t - n + me) + from_right).astype(jnp.bfloat16)
        from_left = wide(lax.ppermute(right, axis, [(i, i + 1) for i in range(t)]))
        from_right = wide(lax.ppermute(left, axis, [(n - 1 - i, n - 2 - i) for i in range(t)]))
    return (chunk(me) + from_left + from_right).astype(jnp.bfloat16)


def body(queries, keys, values, grad_out, chosen, w_query, w_key, w_value):
    groups = keys.shape[1] // HEAD_DIM
    me = lax.axis_index("ctx")
    shares = lax.axis_size("head")
    weights = (w_query, w_key, w_value)
    halves = []
    for g in range(groups):
        at = slice(g * HEAD_DIM, (g + 1) * HEAD_DIM)
        halves += [keys[:, at], values[:, at]]
    pieces = gather_pieces(jnp.concatenate(halves, axis=1), "ctx")
    grad_queries, keep, send = attention(pieces, queries, grad_out, chosen, me, 0, groups)
    parts = scatter_parts(keep, send, "ctx")
    order = line_order(shares, lax.axis_index("head"))
    grad_keys, grad_values, *chunks = projection(order[:1], shares, grad_queries, parts, weights)
    final = [grad_keys, grad_values]
    chunks += projection(order[1:2], shares, grad_queries, final, weights)
    chunks += projection(order[2:], shares, grad_queries, final, weights)
    return (grad_queries, grad_keys, grad_values, line_sum(chunks, "head"))


def solution(mesh):
    return jax.shard_map(
        body,
        mesh=mesh,
        in_specs=(
            P("ctx", "head"),
            P("ctx", "head"),
            P("ctx", "head"),
            P("ctx", "head"),
            P("ctx", "head", None),
            P(None, "head"),
            P(None, "head"),
            P(None, "head"),
        ),
        out_specs=(P("ctx", "head"), P("ctx", "head"), P("ctx", "head"), P("ctx", "head")),
        check_vma=False,
    )
```

time: 170 us -> 142 us (0.84); the launches traced: 167 us -> 141 us
  waiting for transfers between devices: 80.1 us -> 68.5 us
  starting transfers between devices: 25.1 us -> 16.5 us
  local copies, waits for them, and re-layouts: 17.6 us -> 9.75 us
  Pallas kernels: 33.3 us -> 40 us
  other arithmetic: 9.83 us -> 5.23 us
    ppermute x6 -> x4, waiting for transfers between devices: 42.1 us -> 25.2 us  [the longest x1 15.8 us: line_sum(): got_third = lax.ppermute(third, axis, [(0, 1), (2, 3), (1, 0), (3, 2)])]
    pallas_call x1 -> x3, Pallas kernels: 9.98 us -> 23.3 us  [projection(): pl.pallas_call(functools.partial(projection_kernel, chunks, width, len(pa...]
    ppermute x6 -> x4, starting transfers between devices: 13.3 us -> 5.91 us  [the longest x1 2.94 us: line_sum(): got_passed = lax.ppermute(passed, axis, [(1, 2), (2, 1)])]
    unnamed x36 -> x34, local copies, waits for them, and re-layouts: 13.8 us -> 6.89 us
    pallas_call x1, Pallas kernels: 23.4 us -> 16.7 us  [attention(): pl.pallas_call(functools.partial(attention_kernel, n_ctx, topk, first_gro...]
    ppermute x13 -> x12, waiting for transfers between devices: 38 us -> 43.3 us  [exchange(): return lax.ppermute(x, axis, [(i, i ^ mask) for i in range(n)])]
    convert_element_type x6 -> x3, other arithmetic: 9.36 us -> 5.23 us  [the longest x1 2.81 us: scatter_parts(): parts.append(exchange(both.astype(jnp.bfloat16), axis, mask))]
    reshape x4 -> x0, local copies, waits for them, and re-layouts: 2.47 us -> none  [the longest x1 1.02 us: body(): values.reshape(rows, groups, HEAD_DIM)]
  transfers between devices with their start and end apart: 19 -> 16, of which waited for: 12 -> 10; matrix products, arithmetic and copies ran while one was open for 2% -> 2% of each run, Pallas kernels for 0% -> 12%
where the time goes in v1:
time: 142 us; the launch traced here: 141 us
  waiting for transfers between devices  68.5 us (48%)
  Pallas kernels  40 us (28%)
  starting transfers between devices  16.5 us (12%)
  local copies, waits for them, and re-layouts  9.75 us (7%)
  other arithmetic  5.23 us (4%)
    ppermute x12, waiting for transfers between devices, exchange(): return lax.ppermute(x, axis, [(i, i ^ mask) for i in range(n)])  43.3 us
    pallas_call x3, Pallas kernels, projection(): pl.pallas_call(functools.partial(projection_kernel, chunks, width, len(pa...  23.3 us
    pallas_call x1, Pallas kernels, attention(): pl.pallas_call(functools.partial(attention_kernel, n_ctx, topk, first_gro...  16.7 us
    ppermute x1, waiting for transfers between devices, line_sum(): got_third = lax.ppermute(third, axis, [(0, 1), (2, 3), (1, 0), (3, 2)])  15.8 us
    ppermute x12, starting transfers between devices, exchange(): return lax.ppermute(x, axis, [(i, i ^ mask) for i in range(n)])  10.6 us
    ppermute x1, waiting for transfers between devices, line_sum(): got_passed = lax.ppermute(passed, axis, [(1, 2), (2, 1)])  9.41 us
    unnamed x34, local copies, waits for them, and re-layouts  6.89 us
    ppermute x1, starting transfers between devices, line_sum(): got_passed = lax.ppermute(passed, axis, [(1, 2), (2, 1)])  2.94 us
  transfers between devices with their start and end apart: 16, of which 10 were waited for; matrix products, arithmetic and copies ran while one was open for 2% of the time, Pallas kernels for 12%

profile of v1, /device:TPU:16, one launch (start us, length us, event | category | flops | bytes accessed | tf_op | source)
XLA Modules:
  0.0 140.8 jit_solution(17782803919991850642)
XLA Ops:
  0.6 0.9 slice_dynamic-update-slice_fusion.7
  1.5 0.9 slice_dynamic-update-slice_fusion.6
  2.4 0.9 slice_dynamic-update-slice_fusion.5
  3.2 0.9 slice_dynamic-update-slice_fusion.4
  4.1 0.9 slice_dynamic-update-slice_fusion.3
  4.9 0.9 slice_dynamic-update-slice_fusion.2
  5.8 0.0 copy-start.8
  5.8 0.9 slice_dynamic-update-slice_fusion.1
  6.7 0.9 slice_dynamic-update-slice_fusion.refs_0_
  7.5 0.0 copy-start.9
  7.6 1.6 %collective-permute-start.3 = (bf16[256,1024]{1,0:T(8,128)(2,1)S(1)}, bf16[256,1024]{1,0:T(8,128)(2,1)S(1)}, u32[]{:S(2)}, u32[]{:S(2)}) collective-permute-start(bf16[256,1024]{1,0:T(8,128)(2,1)S(1)} %slice_dynamic-update-slice_fusion.refs_0_), channel_id=1, source_target_pairs={{0,16},{4,20},{8,24},{12,28},{16,0},{20,4},{24,8},{28,12},{1,17},{... | collective-permute-start | bytes 1572872 | tf_op jit(solution)/shard_map/ppermute | solution.py:266
  9.1 1.5 %collective-permute-start.1 = (bf16[256,1024]{1,0:T(8,128)(2,1)S(1)}, bf16[256,1024]{1,0:T(8,128)(2,1)S(1)}, u32[]{:S(2)}, u32[]{:S(2)}) collective-permute-start(bf16[256,1024]{1,0:T(8,128)(2,1)S(1)} %slice_dynamic-update-slice_fusion.refs_0_), channel_id=1, source_target_pairs={{0,8},{4,12},{8,0},{12,4},{16,24},{20,28},{24,16},{28,20},{1,9},{5... | collective-permute-start | bytes 1572872 | tf_op jit(solution)/shard_map/ppermute | solution.py:266
  10.6 10.7 %collective-permute-done.3.refs_4_ = bf16[256,1024]{1,0:T(8,128)(2,1)S(1)} collective-permute-done((bf16[256,1024]{1,0:T(8,128)(2,1)S(1)}, bf16[256,1024]{1,0:T(8,128)(2,1)S(1)}, u32[]{:S(2)}, u32[]{:S(2)}) %collective-permute-start.3) | collective-permute-done | bytes 524320 | tf_op jit(solution)/shard_map/ppermute | solution.py:266
  21.3 1.6 %collective-permute-start.5 = (bf16[128,1024]{1,0:T(8,128)(2,1)S(1)}, bf16[128,1024]{1,0:T(8,128)(2,1)S(1)}, u32[]{:S(2)}, u32[]{:S(2)}) collective-permute-start(bf16[128,1024]{1,0:T(8,128)(2,1)S(1)} %slice.76), channel_id=1, source_target_pairs={{0,8},{4,12},{8,0},{12,4},{16,24},{20,28},{24,16},{28,20},{1,9},{5... | collective-permute-start | bytes 786440 | tf_op jit(solution)/shard_map/ppermute | solution.py:266
  22.9 0.0 collective-permute-done.1.refs_2_
  22.9 1.6 %collective-permute-start.6 = (bf16[128,1024]{1,0:T(8,128)(2,1)S(1)}, bf16[128,1024]{1,0:T(8,128)(2,1)S(1)}, u32[]{:S(2)}, u32[]{:S(2)}) collective-permute-start(bf16[128,1024]{1,0:T(8,128)(2,1)S(1)} %slice.77), channel_id=1, source_target_pairs={{0,16},{4,20},{8,24},{12,28},{16,0},{20,4},{24,8},{28,12},{1,17},{... | collective-permute-start | bytes 786440 | tf_op jit(solution)/shard_map/ppermute | solution.py:266
  24.5 0.0 collective-permute-start
  24.5 0.5 collective-permute-start.2
  25.0 0.0 collective-permute-start.4
  25.0 3.6 %collective-permute-done.5 = bf16[128,1024]{1,0:T(8,128)(2,1)S(1)} collective-permute-done((bf16[128,1024]{1,0:T(8,128)(2,1)S(1)}, bf16[128,1024]{1,0:T(8,128)(2,1)S(1)}, u32[]{:S(2)}, u32[]{:S(2)}) %collective-permute-start.5) | collective-permute-done | bytes 262176 | tf_op jit(solution)/shard_map/ppermute | solution.py:266
  28.6 1.3 collective-permute-done.6
  29.9 0.0 copy-start.7
  29.9 0.1 collective-permute-start.7
  30.0 0.0 copy-done.8
  30.0 0.6 reshape.14.chosen
  30.6 0.0 collective-permute-done.refs_1_
  30.6 0.0 collective-permute-done.2.refs_3_
  30.6 0.0 copy-start.11
  30.7 0.0 collective-permute-done.4.refs_5_
  30.7 1.3 collective-permute-done.7.refs_7_
  32.0 0.0 copy-done.9
  32.0 0.0 copy-done.5
  32.0 0.0 copy-done.6
  32.0 0.0 copy-done.7
  32.0 0.0 copy-done.10
  32.0 0.0 copy-done.11
  32.0 16.7 %attention.1 = (bf16[256,1024]{1,0:T(8,128)(2,1)}, bf16[1024,1024]{1,0:T(8,128)(2,1)}, bf16[1024,1024]{1,0:T(8,128)(2,1)}) custom-call(s32[256]{0:T(256)} %reshape.14.chosen, s32[1]{0:T(128)} %bitcast.place, bf16[256,1024]{1,0:T(8,128)(2,1)} %copy-done.9, bf16[256,1024]{1,0:T(8,128)(2,1)} %copy-done.10, bf16[256,1024]{1,0:T(8,128)(2,1)} %copy-done.6, ...), custom_call_target="tpu_custom_call" | custom-call | flops 2684354560 | bytes 16777216 | tf_op jit(solution)/shard_map/attention/pallas_call | solution.py:147
  48.7 0.2 collective-permute-start.8
  48.9 4.2 %collective-permute-done.8.refs_2_ = bf16[1024,1024]{1,0:T(8,128)(2,1)S(1)} collective-permute-done((bf16[1024,1024]{1,0:T(8,128)(2,1)}, bf16[1024,1024]{1,0:T(8,128)(2,1)S(1)}, u32[]{:S(2)}, u32[]{:S(2)}) %collective-permute-start.8) | collective-permute-done | bytes 2097184 | tf_op jit(solution)/shard_map/ppermute | solution.py:266
  53.2 2.8 %add_convert_fusion = (bf16[256,1024]{1,0:T(8,128)(2,1)S(1)}, bf16[256,1024]{1,0:T(8,128)(2,1)S(1)}, bf16[256,1024]{1,0:T(8,128)(2,1)S(1)}) fusion(bf16[1024,1024]{1,0:T(8,128)(2,1)S(1)} %collective-permute-done.8.refs_2_, bf16[1024,1024]{1,0:T(8,128)(2,1)} %get-tuple-element.13.refs_1_), kind=kLoop, calls=%fused_computation.8 | loop fusion | flops 3145728 | bytes 4718592 | tf_op jit(solution)/shard_map/convert_element_type | solution.py:291
  56.0 0.0 copy-done
  56.0 1.6 %collective-permute-start.10 = (bf16[256,1024]{1,0:T(8,128)(2,1)S(1)}, bf16[256,1024]{1,0:T(8,128)(2,1)S(1)}, u32[]{:S(2)}, u32[]{:S(2)}) collective-permute-start(bf16[256,1024]{1,0:T(8,128)(2,1)S(1)} %get-tuple-element.21), channel_id=1, source_target_pairs={{0,16},{4,20},{8,24},{12,28},{16,0},{20,4},{24,8},{28,12},{1,17},{... | collective-permute-start | bytes 1572872 | tf_op jit(solution)/shard_map/ppermute | solution.py:266
  57.6 0.5 collective-permute-start.11
  58.1 1.4 %collective-permute-start.9 = (bf16[256,1024]{1,0:T(8,128)(2,1)S(1)}, bf16[256,1024]{1,0:T(8,128)(2,1)S(1)}, u32[]{:S(2)}, u32[]{:S(2)}) collective-permute-start(bf16[256,1024]{1,0:T(8,128)(2,1)S(1)} %get-tuple-element.22), channel_id=1, source_target_pairs={{0,24},{4,28},{8,16},{12,20},{16,8},{20,12},{24,0},{28,4},{1,25},{... | collective-permute-start | bytes 1572872 | tf_op jit(solution)/shard_map/ppermute | solution.py:266
  59.6 0.0 copy-done.12
  59.6 0.6 fusion.6
  60.2 9.8 %collective-permute-done.10.refs_4_ = bf16[256,1024]{1,0:T(8,128)(2,1)S(1)} collective-permute-done((bf16[256,1024]{1,0:T(8,128)(2,1)S(1)}, bf16[256,1024]{1,0:T(8,128)(2,1)S(1)}, u32[]{:S(2)}, u32[]{:S(2)}) %collective-permute-start.10) | collective-permute-done | bytes 524320 | tf_op jit(solution)/shard_map/ppermute | solution.py:266
  70.0 2.4 %collective-permute-done.11.refs_5_ = bf16[256,1024]{1,0:T(8,128)(2,1)S(1)} collective-permute-done((bf16[256,1024]{1,0:T(8,128)(2,1)S(1)}, bf16[256,1024]{1,0:T(8,128)(2,1)S(1)}, u32[]{:S(2)}, u32[]{:S(2)}) %collective-permute-start.11) | collective-permute-done | bytes 524320 | tf_op jit(solution)/shard_map/ppermute | solution.py:266
  72.4 10.1 %collective-permute-done.9.refs_3_ = bf16[256,1024]{1,0:T(8,128)(2,1)S(1)} collective-permute-done((bf16[256,1024]{1,0:T(8,128)(2,1)S(1)}, bf16[256,1024]{1,0:T(8,128)(2,1)S(1)}, u32[]{:S(2)}, u32[]{:S(2)}) %collective-permute-start.9) | collective-permute-done | bytes 524320 | tf_op jit(solution)/shard_map/ppermute | solution.py:266
  82.5 0.8 copy-done.4
  83.3 7.0 %projection.3 = (bf16[256,512]{1,0:T(8,128)(2,1)}, bf16[256,512]{1,0:T(8,128)(2,1)}, bf16[256,1152]{1,0:T(8,128)(2,1)}) custom-call(s32[1]{0:T(128)} %get-tuple-element.24.order, bf16[256,1024]{1,0:T(8,128)(2,1)} %get-tuple-element.8.refs_0_, bf16[1024,1024]{1,0:T(8,128)(2,1)} %get-tuple-element.13.refs_1_, bf16[1024,1024]{1,0:T(8,128)(2,1)} %copy-done, ...), custom_call_target="tpu_custom_call" | custom-call | flops 1207959552 | bytes 4718592 | tf_op jit(solution)/shard_map/projection/pallas_call | solution.py:232
  90.3 0.4 collective-permute-start.12
  90.7 0.6 slice.74.order
  91.4 9.8 %projection.4 = (bf16[256,1152]{1,0:T(8,128)(2,1)}, bf16[256,1152]{1,0:T(8,128)(2,1)}) custom-call(s32[2]{0:T(128)} %slice.74.order, bf16[256,1024]{1,0:T(8,128)(2,1)} %get-tuple-element.8.refs_0_, bf16[256,512]{1,0:T(8,128)(2,1)} %get-tuple-element.9.refs_1_, bf16[256,512]{1,0:T(8,128)(2,1)} %get-tuple-element.10.refs_2_, bf16[4608,1024]{1,0:T(8,128)(2,1)} %refs_3_.3, ...), custom_call_target="tpu_custom_call" | custom-call | flops 2415919104 | bytes 9437184 | tf_op jit(solution)/shard_map/projection/pallas_call | solution.py:232
  101.2 1.8 %collective-permute-start.14 = (bf16[256,1152]{1,0:T(8,128)(2,1)}, bf16[256,1152]{1,0:T(8,128)(2,1)S(1)}, u32[]{:S(2)}, u32[]{:S(2)}) collective-permute-start(bf16[256,1152]{1,0:T(8,128)(2,1)} %get-tuple-element.19), channel_id=1, source_target_pairs={{0,1},{2,3},{1,0},{3,2},{4,5},{6,7},{5,4},{7,6},{8,9},{10,11},{9,8... | collective-permute-start | bytes 1769480 | tf_op jit(solution)/shard_map/ppermute | solution.py:309
  102.9 6.4 %projection.5 = bf16[256,1152]{1,0:T(8,128)(2,1)} custom-call(s32[1]{0:T(128)} %get-tuple-element.23.order, bf16[256,1024]{1,0:T(8,128)(2,1)} %get-tuple-element.8.refs_0_, bf16[256,512]{1,0:T(8,128)(2,1)} %get-tuple-element.9.refs_1_, bf16[256,512]{1,0:T(8,128)(2,1)} %get-tuple-element.10.refs_2_, bf16[4608,1024]{1,0:T(8,128)(2,1)} %refs_3_.3, ...), custom_call_target="tpu_custom_call" | custom-call | flops 1207959552 | bytes 4718592 | tf_op jit(solution)/shard_map/projection/pallas_call | solution.py:232
  109.4 0.8 collective-permute-start.13
  110.2 0.0 collective-permute-done.12
  110.2 1.2 fusion.5
  111.4 2.9 %collective-permute-start.15 = (bf16[256,1152]{1,0:T(8,128)(2,1)S(1)}, bf16[256,1152]{1,0:T(8,128)(2,1)S(1)}, u32[]{:S(2)}, u32[]{:S(2)}) collective-permute-start(bf16[256,1152]{1,0:T(8,128)(2,1)S(1)} %fusion.5), channel_id=1, source_target_pairs={{1,2},{2,1},{5,6},{6,5},{9,10},{10,9},{13,14},{14,13},{17,18},{18,... | collective-permute-start | bytes 1769480 | tf_op jit(solution)/shard_map/ppermute | solution.py:311
  114.4 15.8 %collective-permute-done.14 = bf16[256,1152]{1,0:T(8,128)(2,1)S(1)} collective-permute-done((bf16[256,1152]{1,0:T(8,128)(2,1)}, bf16[256,1152]{1,0:T(8,128)(2,1)S(1)}, u32[]{:S(2)}, u32[]{:S(2)}) %collective-permute-start.14) | collective-permute-done | bytes 589856 | tf_op jit(solution)/shard_map/ppermute | solution.py:309
  130.2 0.0 collective-permute-done.13
  130.2 9.4 %collective-permute-done.15 = bf16[256,1152]{1,0:T(8,128)(2,1)S(1)} collective-permute-done((bf16[256,1152]{1,0:T(8,128)(2,1)S(1)}, bf16[256,1152]{1,0:T(8,128)(2,1)S(1)}, u32[]{:S(2)}, u32[]{:S(2)}) %collective-permute-start.15) | collective-permute-done | bytes 589856 | tf_op jit(solution)/shard_map/ppermute | solution.py:311
  139.6 1.2 fusion.4
  (17 shorter events, 0.1 us)
Async XLA Ops:
  5.8 24.2 %copy-start.8 = (s32[4,4,16]{2,1,0:T(4,128)S(1)}, s32[4,4,16]{2,1,0:T(4,128)}, u32[]{:S(2)}) copy-start(s32[4,4,16]{2,1,0:T(4,128)} %param.13) | copy-start | bytes 3076
  7.5 24.5 %copy-start.9 = (bf16[256,1024]{1,0:T(8,128)(2,1)}, bf16[256,1024]{1,0:T(8,128)(2,1)S(1)}, u32[]{:S(2)}) copy-start(bf16[256,1024]{1,0:T(8,128)(2,1)S(1)} %slice_dynamic-update-slice_fusion.refs_0_) | copy-start | bytes 1572868
  7.6 13.7 %collective-permute-start.3 = (bf16[256,1024]{1,0:T(8,128)(2,1)S(1)}, bf16[256,1024]{1,0:T(8,128)(2,1)S(1)}, u32[]{:S(2)}, u32[]{:S(2)}) collective-permute-start(bf16[256,1024]{1,0:T(8,128)(2,1)S(1)} %slice_dynamic-update-slice_fusion.refs_0_), channel_id=1, source_target_pairs={{0,16},{4,20},{8,24},{12,28},{16,0},{20,4},{24,8},{28,12},{1,17},{... | collective-permute-start | bytes 1572872 | tf_op jit(solution)/shard_map/ppermute | solution.py:266
  9.1 13.7 %collective-permute-start.1 = (bf16[256,1024]{1,0:T(8,128)(2,1)S(1)}, bf16[256,1024]{1,0:T(8,128)(2,1)S(1)}, u32[]{:S(2)}, u32[]{:S(2)}) collective-permute-start(bf16[256,1024]{1,0:T(8,128)(2,1)S(1)} %slice_dynamic-update-slice_fusion.refs_0_), channel_id=1, source_target_pairs={{0,8},{4,12},{8,0},{12,4},{16,24},{20,28},{24,16},{28,20},{1,9},{5... | collective-permute-start | bytes 1572872 | tf_op jit(solution)/shard_map/ppermute | solution.py:266
  21.3 10.7 %copy-start.5 = (bf16[256,1024]{1,0:T(8,128)(2,1)}, bf16[256,1024]{1,0:T(8,128)(2,1)S(1)}, u32[]{:S(2)}) copy-start(bf16[256,1024]{1,0:T(8,128)(2,1)S(1)} %collective-permute-done.3.refs_4_) | copy-start | bytes 1572868
  21.3 7.2 %collective-permute-start.5 = (bf16[128,1024]{1,0:T(8,128)(2,1)S(1)}, bf16[128,1024]{1,0:T(8,128)(2,1)S(1)}, u32[]{:S(2)}, u32[]{:S(2)}) collective-permute-start(bf16[128,1024]{1,0:T(8,128)(2,1)S(1)} %slice.76), channel_id=1, source_target_pairs={{0,8},{4,12},{8,0},{12,4},{16,24},{20,28},{24,16},{28,20},{1,9},{5... | collective-permute-start | bytes 786440 | tf_op jit(solution)/shard_map/ppermute | solution.py:266
  22.9 9.1 %copy-start.6 = (bf16[256,1024]{1,0:T(8,128)(2,1)}, bf16[256,1024]{1,0:T(8,128)(2,1)S(1)}, u32[]{:S(2)}) copy-start(bf16[256,1024]{1,0:T(8,128)(2,1)S(1)} %collective-permute-done.1.refs_2_) | copy-start | bytes 1572868
  22.9 7.0 %collective-permute-start.6 = (bf16[128,1024]{1,0:T(8,128)(2,1)S(1)}, bf16[128,1024]{1,0:T(8,128)(2,1)S(1)}, u32[]{:S(2)}, u32[]{:S(2)}) collective-permute-start(bf16[128,1024]{1,0:T(8,128)(2,1)S(1)} %slice.77), channel_id=1, source_target_pairs={{0,16},{4,20},{8,24},{12,28},{16,0},{20,4},{24,8},{28,12},{1,17},{... | collective-permute-start | bytes 786440 | tf_op jit(solution)/shard_map/ppermute | solution.py:266
  24.5 6.2 %collective-permute-start = (bf16[256,1024]{1,0:T(8,128)(2,1)S(1)}, bf16[256,1024]{1,0:T(8,128)(2,1)S(1)}, u32[]{:S(2)}, u32[]{:S(2)}) collective-permute-start(bf16[256,1024]{1,0:T(8,128)(2,1)S(1)} %slice_dynamic-update-slice_fusion.refs_0_), channel_id=1, source_target_pairs={{0,4},{4,0},{8,12},{12,8},{16,20},{20,16},{24,28},{28,24},{1,5},{5... | collective-permute-start | bytes 1572872 | tf_op jit(solution)/shard_map/ppermute | solution.py:266
  24.5 6.2 %collective-permute-start.2 = (bf16[256,1024]{1,0:T(8,128)(2,1)S(1)}, bf16[256,1024]{1,0:T(8,128)(2,1)S(1)}, u32[]{:S(2)}, u32[]{:S(2)}) collective-permute-start(bf16[256,1024]{1,0:T(8,128)(2,1)S(1)} %collective-permute-done.1.refs_2_), channel_id=1, source_target_pairs={{0,4},{4,0},{8,12},{12,8},{16,20},{20,16},{24,28},{28,24},{1,5},{5... | collective-permute-start | bytes 1572872 | tf_op jit(solution)/shard_map/ppermute | solution.py:266
  25.0 5.7 %collective-permute-start.4 = (bf16[256,1024]{1,0:T(8,128)(2,1)S(1)}, bf16[256,1024]{1,0:T(8,128)(2,1)}, u32[]{:S(2)}, u32[]{:S(2)}) collective-permute-start(bf16[256,1024]{1,0:T(8,128)(2,1)S(1)} %collective-permute-done.3.refs_4_), channel_id=1, source_target_pairs={{0,4},{4,0},{8,12},{12,8},{16,20},{20,16},{24,28},{28,24},{1,5},{5... | collective-permute-start | bytes 1572872 | tf_op jit(solution)/shard_map/ppermute | solution.py:266
  29.9 2.1 %copy-start.7 = (bf16[256,1024]{1,0:T(8,128)(2,1)}, bf16[256,1024]{1,0:T(8,128)(2,1)S(1)}, u32[]{:S(2)}) copy-start(bf16[256,1024]{1,0:T(8,128)(2,1)S(1)} %constant_dynamic-update-slice_fusion.refs_6_) | copy-start | bytes 1572868
  29.9 2.1 %collective-permute-start.7 = (bf16[256,1024]{1,0:T(8,128)(2,1)S(1)}, bf16[256,1024]{1,0:T(8,128)(2,1)}, u32[]{:S(2)}, u32[]{:S(2)}) collective-permute-start(bf16[256,1024]{1,0:T(8,128)(2,1)S(1)} %constant_dynamic-update-slice_fusion.refs_6_), channel_id=1, source_target_pairs={{0,4},{4,0},{8,12},{12,8},{16,20},{20,16},{24,28},{28,24},{1,5},{5... | collective-permute-start | bytes 1572872 | tf_op jit(solution)/shard_map/ppermute | solution.py:266
  30.6 1.4 copy-start.10
  30.6 1.4 copy-start.11
  48.7 4.4 %collective-permute-start.8 = (bf16[1024,1024]{1,0:T(8,128)(2,1)}, bf16[1024,1024]{1,0:T(8,128)(2,1)S(1)}, u32[]{:S(2)}, u32[]{:S(2)}) collective-permute-start(bf16[1024,1024]{1,0:T(8,128)(2,1)} %get-tuple-element.14), channel_id=1, source_target_pairs={{0,4},{4,0},{8,12},{12,8},{16,20},{20,16},{24,28},{28,24},{1,5},{5... | collective-permute-start | bytes 6291464 | tf_op jit(solution)/shard_map/ppermute | solution.py:266
  53.2 2.8 %copy-start = (bf16[1024,1024]{1,0:T(8,128)(2,1)}, bf16[1024,1024]{1,0:T(8,128)(2,1)S(1)}, u32[]{:S(2)}) copy-start(bf16[1024,1024]{1,0:T(8,128)(2,1)S(1)} %collective-permute-done.8.refs_2_) | copy-start | bytes 6291460
  53.2 6.4 %copy-start.12 = (s32[4]{0:T(128)S(1)}, s32[4]{0:T(128)}, u32[]{:S(2)}) copy-start(s32[4]{0:T(128)} %constant.17.clone) | copy-start | bytes 52
  56.0 14.0 %collective-permute-start.10 = (bf16[256,1024]{1,0:T(8,128)(2,1)S(1)}, bf16[256,1024]{1,0:T(8,128)(2,1)S(1)}, u32[]{:S(2)}, u32[]{:S(2)}) collective-permute-start(bf16[256,1024]{1,0:T(8,128)(2,1)S(1)} %get-tuple-element.21), channel_id=1, source_target_pairs={{0,16},{4,20},{8,24},{12,28},{16,0},{20,4},{24,8},{28,12},{1,17},{... | collective-permute-start | bytes 1572872 | tf_op jit(solution)/shard_map/ppermute | solution.py:266
  57.6 14.8 %collective-permute-start.11 = (bf16[256,1024]{1,0:T(8,128)(2,1)S(1)}, bf16[256,1024]{1,0:T(8,128)(2,1)S(1)}, u32[]{:S(2)}, u32[]{:S(2)}) collective-permute-start(bf16[256,1024]{1,0:T(8,128)(2,1)S(1)} %get-tuple-element.20), channel_id=1, source_target_pairs={{0,8},{4,12},{8,0},{12,4},{16,24},{20,28},{24,16},{28,20},{1,9},{5... | collective-permute-start | bytes 1572872 | tf_op jit(solution)/shard_map/ppermute | solution.py:266
  58.1 24.3 %collective-permute-start.9 = (bf16[256,1024]{1,0:T(8,128)(2,1)S(1)}, bf16[256,1024]{1,0:T(8,128)(2,1)S(1)}, u32[]{:S(2)}, u32[]{:S(2)}) collective-permute-start(bf16[256,1024]{1,0:T(8,128)(2,1)S(1)} %get-tuple-element.22), channel_id=1, source_target_pairs={{0,24},{4,28},{8,16},{12,20},{16,8},{20,12},{24,0},{28,4},{1,25},{... | collective-permute-start | bytes 1572872 | tf_op jit(solution)/shard_map/ppermute | solution.py:266
  70.0 12.4 %copy-start.2 = (bf16[256,1024]{1,0:T(8,128)(2,1)}, bf16[256,1024]{1,0:T(8,128)(2,1)S(1)}, u32[]{:S(2)}) copy-start(bf16[256,1024]{1,0:T(8,128)(2,1)S(1)} %collective-permute-done.10.refs_4_) | copy-start | bytes 1572868
  72.4 10.1 %copy-start.3 = (bf16[256,1024]{1,0:T(8,128)(2,1)}, bf16[256,1024]{1,0:T(8,128)(2,1)S(1)}, u32[]{:S(2)}) copy-start(bf16[256,1024]{1,0:T(8,128)(2,1)S(1)} %collective-permute-done.11.refs_5_) | copy-start | bytes 1572868
  82.5 0.8 copy-start.4
  90.3 19.9 %collective-permute-start.12 = (bf16[256,1152]{1,0:T(8,128)(2,1)}, bf16[256,1152]{1,0:T(8,128)(2,1)S(1)}, u32[]{:S(2)}, u32[]{:S(2)}) collective-permute-start(bf16[256,1152]{1,0:T(8,128)(2,1)} %get-tuple-element.18), channel_id=1, source_target_pairs={{0,1},{3,2},{1,3},{2,0},{4,5},{7,6},{5,7},{6,4},{8,9},{11,10},{9,1... | collective-permute-start | bytes 1769480 | tf_op jit(solution)/shard_map/ppermute | solution.py:307
  101.2 29.0 %collective-permute-start.14 = (bf16[256,1152]{1,0:T(8,128)(2,1)}, bf16[256,1152]{1,0:T(8,128)(2,1)S(1)}, u32[]{:S(2)}, u32[]{:S(2)}) collective-permute-start(bf16[256,1152]{1,0:T(8,128)(2,1)} %get-tuple-element.19), channel_id=1, source_target_pairs={{0,1},{2,3},{1,0},{3,2},{4,5},{6,7},{5,4},{7,6},{8,9},{10,11},{9,8... | collective-permute-start | bytes 1769480 | tf_op jit(solution)/shard_map/ppermute | solution.py:309
  109.3 30.3 %copy-start.1 = (bf16[256,1152]{1,0:T(8,128)(2,1)S(1)}, bf16[256,1152]{1,0:T(8,128)(2,1)}, u32[]{:S(2)}) copy-start(bf16[256,1152]{1,0:T(8,128)(2,1)} %get-tuple-element.17) | copy-start | bytes 1769476
  109.4 20.8 %collective-permute-start.13 = (bf16[256,1152]{1,0:T(8,128)(2,1)}, bf16[256,1152]{1,0:T(8,128)(2,1)S(1)}, u32[]{:S(2)}, u32[]{:S(2)}) collective-permute-start(bf16[256,1152]{1,0:T(8,128)(2,1)} %projection.5), channel_id=1, source_target_pairs={{0,3},{3,0},{4,7},{7,4},{8,11},{11,8},{12,15},{15,12},{16,19},{19,... | collective-permute-start | bytes 1769480 | tf_op jit(solution)/shard_map/ppermute | solution.py:308
  111.4 28.2 %collective-permute-start.15 = (bf16[256,1152]{1,0:T(8,128)(2,1)S(1)}, bf16[256,1152]{1,0:T(8,128)(2,1)S(1)}, u32[]{:S(2)}, u32[]{:S(2)}) collective-permute-start(bf16[256,1152]{1,0:T(8,128)(2,1)S(1)} %fusion.5), channel_id=1, source_target_pairs={{1,2},{2,1},{5,6},{6,5},{9,10},{10,9},{13,14},{14,13},{17,18},{18,... | collective-permute-start | bytes 1769480 | tf_op jit(solution)/shard_map/ppermute | solution.py:311

commit v2 on v1

v2 whole, which is shorter than its diff:
```python
import functools
import math

import jax
import jax.numpy as jnp
from jax import lax
from jax.experimental import pallas as pl
from jax.experimental.pallas import tpu as pltpu
from jax.sharding import PartitionSpec as P

HEAD_DIM = 128
BLOCK = 64
LOG2E = math.log2(math.e)


def in_hbm(x):
    return pltpu.with_memory_space_constraint(x, pltpu.HBM)


def attention_kernel(axis, n_ctx, topk, cuts, chosen, *refs):
    pieces, (q_hbm, g_hbm, dq_hbm, *out_hbm), scratch = refs[: 2 * n_ctx], refs[2 * n_ctx : -13], refs[-13:]
    k_all, v_all, q_all, g_all, acc, near, scores, packed, operand, dq_all, staged, arrived, left = scratch
    calls = acc.shape[0]
    rows = q_hbm.shape[0]
    wide = 2 * HEAD_DIM
    width = q_hbm.shape[1] // calls
    heads_per = width // HEAD_DIM
    lanes = heads_per * BLOCK
    blocks = rows // BLOCK
    me = lax.axis_index(axis)
    scaling = 1.0 / math.sqrt(HEAD_DIM)
    step = scaling * LOG2E

    def device_rows(k, first=0, count=rows):
        return pl.ds(pl.multiple_of((me ^ k) * rows + first, 16), count)

    def arrivals(late):
        at = slice(HEAD_DIM, None) if late else slice(0, HEAD_DIM)
        copies = [] if late else [(q_hbm, q_all), (g_hbm, g_all)]
        for side, held in ((0, k_all), (1, v_all)):
            for k in range(n_ctx):
                copies.append((pieces[side * n_ctx + k].at[:, at], held.at[device_rows(k), at]))
        return [pltpu.make_async_copy(src, dst, arrived.at[late, i]) for i, (src, dst) in enumerate(copies)]

    def departures(j):
        columns = pl.ds(pl.multiple_of(j * width, HEAD_DIM), width)
        copies = [(dq_all.at[:, columns], dq_hbm.at[:, columns])]
        columns = pl.ds(pl.multiple_of(j * wide, HEAD_DIM), wide)
        first = 0
        for out in out_hbm:
            copies.append((staged.at[j, pl.ds(first, out.shape[0]), :], out.at[:, columns]))
            first += out.shape[0]
        return [pltpu.make_async_copy(src, dst, left.at[j, i]) for i, (src, dst) in enumerate(copies)]

    waves = [0] if calls == 1 else [0, 1]
    for late in waves:
        for copy in arrivals(late):
            copy.start()
    acc[...] = jnp.zeros_like(acc)
    for ref in operand:
        ref[...] = jnp.zeros_like(ref)
    offset = lax.broadcasted_iota(jnp.int32, (BLOCK, lanes), 0) - (
        lax.broadcasted_iota(jnp.int32, (BLOCK, lanes), 1) % BLOCK
    )

    def picks_of(j, b):
        own = me * blocks + b
        listed = [chosen[b, j, i] for i in range(topk)]
        return own, [own] + [jnp.where(listed[i] == own, listed[0], listed[i]) for i in range(1, topk)]

    def tile(i):
        return slice(i * BLOCK, (i + 1) * BLOCK)

    def block_rows(i):
        return pl.ds(pl.multiple_of(i * BLOCK, BLOCK), BLOCK)

    def columns_of(i):
        return pl.ds(pl.multiple_of(i * HEAD_DIM, HEAD_DIM), HEAD_DIM)

    def score_stage(j, b):
        _, picks = picks_of(j, b)
        for i in range(topk):
            near[b][tile(i), :HEAD_DIM] = k_all[block_rows(picks[i]), columns_of(j)]
            near[b][tile(i), HEAD_DIM:] = v_all[block_rows(picks[i]), columns_of(j)]
        for h in range(heads_per):
            at = columns_of(j * heads_per + h)
            operand[b][tile(h), :HEAD_DIM] = q_all[tile(b), at]
            operand[b][lanes + h * BLOCK : lanes + (h + 1) * BLOCK, HEAD_DIM:] = g_all[tile(b), at]
        scores[b][...] = lax.dot_general(
            near[b][...], operand[b][...], (((1,), (1,)), ((), ())), preferred_element_type=jnp.float32
        )

    def weight_stage(j, b):
        own, picks = picks_of(j, b)
        bias = [jnp.where(picks[i] > own, -1e30, 0.0) for i in range(topk)]
        score, weigh, pack = scores[b], scores[b], packed[b]
        first = jnp.where(offset <= 0, score[tile(0), :lanes], -1e30)
        top = first
        for i in range(1, topk):
            top = jnp.maximum(top, score[tile(i), :lanes] + bias[i])
        top = jnp.max(top, axis=0, keepdims=True)
        total = jnp.zeros((BLOCK, lanes), jnp.float32)
        delta = jnp.zeros((BLOCK, lanes), jnp.float32)
        for i in range(topk):
            s = first - top if i == 0 else score[tile(i), :lanes] - (top - bias[i])
            e = jnp.exp2(s * step)
            weigh[tile(i), :lanes] = e
            total = total + e
            delta = delta + e * score[tile(i), lanes:]
        total = 1.0 / jnp.sum(total, axis=0, keepdims=True)
        delta = jnp.sum(delta, axis=0, keepdims=True) * total
        for i in range(topk):
            w = weigh[tile(i), :lanes] * total
            pack[tile(i), lanes:] = w.astype(jnp.bfloat16)
            pack[tile(i), :lanes] = (w * (score[tile(i), lanes:] - delta)).astype(jnp.bfloat16)

    def term_stage(j, b):
        _, picks = picks_of(j, b)
        terms = jnp.dot(packed[b][...], operand[b][...], preferred_element_type=jnp.float32)
        for i in range(topk):
            acc[j, block_rows(picks[i]), :] += terms[tile(i), :]
        dq = scaling * lax.dot_general(
            packed[b][:, :lanes],
            near[b][:, :HEAD_DIM],
            (((0,), (0,)), ((), ())),
            preferred_element_type=jnp.float32,
        )
        dq = dq.astype(jnp.bfloat16)
        for h in range(heads_per):
            dq_all[tile(b), columns_of(j * heads_per + h)] = dq[tile(h), :]

    def leave(j):
        first = 0
        for cut in cuts:
            count = cut.stop - cut.start
            for core in range(2):
                for k in range(n_ctx // 2):
                    at = device_rows(2 * k + core, cut.start, count)
                    to = slice(first, first + count)
                    staged[j, to, :HEAD_DIM] = (acc[j, at, :HEAD_DIM] * scaling).astype(jnp.bfloat16)
                    staged[j, to, HEAD_DIM:] = acc[j, at, HEAD_DIM:].astype(jnp.bfloat16)
                    first += count
        for copy in departures(j):
            copy.start()

    def run(group, b, scoring=True, weighing=True, summing=True):
        if scoring:
            score_stage(group + b // blocks, b % blocks)
        if weighing:
            weight_stage(group + (b - 1) // blocks, (b - 1) % blocks)
        if summing:
            term_stage(group + (b - 2) // blocks, (b - 2) % blocks)

    def one_group(group, carry):
        for b in range(2, blocks + 2):
            run(group, b)
        leave(group)
        return carry

    for copy in arrivals(0):
        copy.wait()
    run(0, 0, weighing=False, summing=False)
    run(0, 1, summing=False)
    for late in waves[1:]:
        for copy in arrivals(late):
            copy.wait()
    lax.fori_loop(0, calls - 1, one_group, 0)
    for b in range(2, blocks):
        run(calls - 1, b)
    run(calls - 1, blocks, scoring=False)
    run(calls - 1, blocks + 1, scoring=False, weighing=False)
    leave(calls - 1)
    for j in range(calls):
        for copy in departures(j):
            copy.wait()


def attention(axis, pieces, queries, grad_out, chosen, cuts):
    n_ctx = len(pieces) // 2
    rows = queries.shape[0]
    topk = chosen.shape[-1]
    wide = 2 * HEAD_DIM
    groups = pieces[0].shape[1] // HEAD_DIM
    width = queries.shape[1] // groups
    lanes = width // HEAD_DIM * BLOCK
    blocks = rows // BLOCK
    near = topk * BLOCK
    flops = groups * blocks * 10 * near * lanes * HEAD_DIM
    sizes = [n_ctx // 2 * (cut.stop - cut.start) for cut in cuts for core in range(2)]
    bf16 = lambda *shape: pltpu.VMEM(shape, jnp.bfloat16)
    f32 = lambda *shape: pltpu.VMEM(shape, jnp.float32)
    anywhere = pl.BlockSpec(memory_space=pl.ANY)
    return pl.pallas_call(
        functools.partial(attention_kernel, axis, n_ctx, topk, cuts),
        out_shape=[jax.ShapeDtypeStruct(queries.shape, jnp.bfloat16)]
        + [jax.ShapeDtypeStruct((size, groups * wide), jnp.bfloat16) for size in sizes],
        grid_spec=pltpu.PrefetchScalarGridSpec(
            num_scalar_prefetch=1,
            grid=(1,),
            in_specs=[anywhere] * (2 * n_ctx + 2),
            out_specs=[anywhere] * (1 + len(sizes)),
            scratch_shapes=[
                bf16(n_ctx * rows, groups * HEAD_DIM),
                bf16(n_ctx * rows, groups * HEAD_DIM),
                bf16(*queries.shape),
                bf16(*queries.shape),
                f32(groups, n_ctx * rows, wide),
                [bf16(near, wide)] * blocks,
                [f32(near, 2 * lanes)] * blocks,
                [bf16(near, 2 * lanes)] * blocks,
                [bf16(2 * lanes, wide)] * blocks,
                bf16(*queries.shape),
                bf16(groups, n_ctx * rows, wide),
                pltpu.SemaphoreType.DMA((2, 2 * n_ctx + 2)),
                pltpu.SemaphoreType.DMA((groups, 1 + len(sizes))),
            ],
        ),
        compiler_params=pltpu.CompilerParams(vmem_limit_bytes=36 * 2**20),
        cost_estimate=pl.CostEstimate(flops=flops, bytes_accessed=16 * n_ctx * rows * wide * groups, transcendentals=0),
        name="attention",
    )(chosen, *pieces, in_hbm(queries), in_hbm(grad_out))


def query_term_kernel(gq_ref, w_ref, out_ref):
    out_ref[...] = lax.dot_general(
        gq_ref[...], w_ref[...], (((1,), (1,)), ((), ())), preferred_element_type=jnp.float32
    ).astype(jnp.bfloat16)


def query_term(shares, gq, w):
    rows, depth = gq.shape
    width = w.shape[0] // shares
    return pl.pallas_call(
        query_term_kernel,
        out_shape=jax.ShapeDtypeStruct((shares, rows, width), jnp.bfloat16),
        grid=(shares,),
        in_specs=[pl.BlockSpec((rows, depth), lambda j: (0, 0)), pl.BlockSpec((width, depth), lambda j: (j, 0))],
        out_specs=pl.BlockSpec((None, rows, width), lambda j: (j, 0, 0)),
        compiler_params=pltpu.CompilerParams(vmem_limit_bytes=16 * 2**20),
        cost_estimate=pl.CostEstimate(
            flops=2 * shares * width * rows * depth, bytes_accessed=2 * shares * width * depth, transcendentals=0
        ),
        name="query_term",
    )(gq, w)


def projection_kernel(axis, places, cut, summed, *refs):
    count = len(places)
    parts, (term, wk_hbm, wv_hbm), refs = refs[:summed], refs[summed : summed + 3], refs[summed + 3 :]
    if summed > 2:
        gk_hbm, gv_hbm, *refs = refs
    out_hbm, (wk, wv, terms, held, gk, gv, out, w_sem, part_sem, out_sem) = refs[:count], refs[count:]
    width = wk.shape[1]
    rows = cut.stop - cut.start
    n = lax.axis_size(axis)
    order = [line_order(n, lax.axis_index(axis))[i] for i in places]

    def arrivals(i):
        at = pl.ds(pl.multiple_of(order[i] * width, width), width)
        copies = ((wk_hbm.at[at, :], wk), (wv_hbm.at[at, :], wv), (term.at[order[i], pl.ds(cut.start, rows), :], terms))
        return [pltpu.make_async_copy(src, dst.at[i], w_sem.at[i, k]) for k, (src, dst) in enumerate(copies)]

    targets = [held.at[i] for i in range(summed)] if summed > 2 else [gk, gv]
    part_copies = [
        pltpu.make_async_copy(src.at[pl.ds(0, rows), :], dst, part_sem.at[i])
        for i, (src, dst) in enumerate(zip(parts, targets))
    ]
    for copy in part_copies:
        copy.start()
    for i in range(count):
        for copy in arrivals(i):
            copy.start()
    for copy in part_copies:
        copy.wait()
    leaving = []

    def leave(src, dst):
        leaving.append(pltpu.make_async_copy(src, dst, out_sem.at[len(leaving)]))
        leaving[-1].start()

    if summed > 2:
        for g in range(gk.shape[1] // HEAD_DIM):
            for side, total_ref in ((0, gk), (1, gv)):
                at = slice((2 * g + side) * HEAD_DIM, (2 * g + side + 1) * HEAD_DIM)
                total = held[0, :, at].astype(jnp.float32)
                for i in range(1, summed):
                    total += held[i, :, at].astype(jnp.float32)
                total_ref[:, g * HEAD_DIM : (g + 1) * HEAD_DIM] = total.astype(jnp.bfloat16)
        leave(gk, gk_hbm)
        leave(gv, gv_hbm)
    contract = (((1,), (1,)), ((), ()))
    for i in range(count):
        for copy in arrivals(i):
            copy.wait()
        total = terms[i].astype(jnp.float32)
        total += lax.dot_general(gk[...], wk[i], contract, preferred_element_type=jnp.float32)
        total += lax.dot_general(gv[...], wv[i], contract, preferred_element_type=jnp.float32)
        out[i] = total.astype(jnp.bfloat16)
        leave(out.at[i], out_hbm[i])
    for copy in leaving:
        copy.wait()


def projection(axis, places, cut, parts, term, weights):
    count = len(places)
    summed = len(parts)
    rows = cut.stop - cut.start
    columns = weights[0].shape[1]
    width = term.shape[2]
    out_shape = [jax.ShapeDtypeStruct((rows, width), jnp.bfloat16)] * count
    if summed > 2:
        out_shape = [jax.ShapeDtypeStruct((rows, columns), jnp.bfloat16)] * 2 + out_shape
    bf16 = lambda *shape: pltpu.VMEM(shape, jnp.bfloat16)
    anywhere = pl.BlockSpec(memory_space=pl.ANY)
    return pl.pallas_call(
        functools.partial(projection_kernel, axis, places, cut, summed),
        out_shape=out_shape,
        in_specs=[anywhere] * (summed + 3),
        out_specs=[anywhere] * len(out_shape),
        scratch_shapes=[
            bf16(count, width, columns),
            bf16(count, width, columns),
            bf16(count, rows, width),
            bf16(summed, rows, parts[0].shape[1]),
            bf16(rows, columns),
            bf16(rows, columns),
            bf16(count, rows, width),
            pltpu.SemaphoreType.DMA((count, 3)),
            pltpu.SemaphoreType.DMA((summed,)),
            pltpu.SemaphoreType.DMA((len(out_shape),)),
        ],
        compiler_params=pltpu.CompilerParams(vmem_limit_bytes=16 * 2**20),
        cost_estimate=pl.CostEstimate(
            flops=4 * count * width * rows * columns, bytes_accessed=4 * count * width * columns, transcendentals=0
        ),
        name="projection",
    )(*parts, term, *map(in_hbm, weights))


def exchange(x, axis, mask):
    n = lax.axis_size(axis)
    return lax.ppermute(x, axis, [(i, i ^ mask) for i in range(n)])


def gather_pieces(sides, axis):
    n = lax.axis_size(axis)
    pieces = [{0: side} for side in sides]
    for mask in sorted(range(2, n, 2), key=lambda m: (m.bit_count(), m)):
        bits = [1 << i for i in range(n.bit_length()) if mask >> i & 1]
        for i, held in enumerate(pieces):
            bit = bits[(i - 1) % len(bits)]
            held[mask] = exchange(held[mask ^ bit], axis, bit)
    for held in pieces:
        for mask in range(0, n, 2):
            held[mask | 1] = exchange(held[mask], axis, 1)
    return [held[k] for held in pieces for k in range(n)]


def scatter_parts(keep, got, axis):
    n = lax.axis_size(axis)
    rows = keep.shape[0] // (n // 2)
    sums = {}
    for mask in range(n - 2, 0, -2):
        cut = slice(mask // 2 * rows, (mask // 2 + 1) * rows)
        sums[mask] = (keep[cut].astype(jnp.float32) + got[cut].astype(jnp.float32)).astype(jnp.bfloat16)
    return [keep, got] + [exchange(x, axis, mask) for mask, x in sums.items()], list(sums.values())


def line_order(n, me):
    if n == 4:
        return [me ^ 2, me ^ 3, me ^ 1, me]
    return [(me + 1 + i) % n for i in range(n)]


def line_sum(chunks, axis, after):
    n = lax.axis_size(axis)
    me = lax.axis_index(axis)
    wide = lambda x: x.astype(jnp.float32)
    if after:
        chunks[1:], _ = lax.optimization_barrier((chunks[1:], after))
    if n == 4:
        first, second, third, own = chunks
        got_first = lax.ppermute(first, axis, [(0, 1), (3, 2), (1, 3), (2, 0)])
        got_second = lax.ppermute(second, axis, [(0, 3), (3, 0)])
        got_third = lax.ppermute(third, axis, [(0, 1), (2, 3), (1, 0), (3, 2)])
        passed = (wide(second) + wide(got_first)).astype(jnp.bfloat16)
        got_passed = lax.ppermute(passed, axis, [(1, 2), (2, 1)])
        outer = jnp.logical_or(me == 0, me == 3)
        total = wide(own) + jnp.where(outer, wide(got_first), 0.0)
        return (total + wide(got_second) + wide(got_third) + wide(got_passed)).astype(jnp.bfloat16), [
            got_first,
            got_second,
            got_third,
        ]
    stacked = jnp.stack(chunks)

    def chunk(d):
        return wide(lax.dynamic_index_in_dim(stacked, (d - me - 1) % n, 0, keepdims=False))

    from_left = from_right = 0.0
    for t in range(1, n):
        right = (chunk(n - t + me) + from_left).astype(jnp.bfloat16)
        left = (chunk(t - n + me) + from_right).astype(jnp.bfloat16)
        from_left = wide(lax.ppermute(right, axis, [(i, i + 1) for i in range(t)]))
        from_right = wide(lax.ppermute(left, axis, [(n - 1 - i, n - 2 - i) for i in range(t)]))
    return (chunk(me) + from_left + from_right).astype(jnp.bfloat16), [from_left, from_right]


def body(queries, keys, values, grad_out, chosen, w_query, w_key, w_value):
    rows = queries.shape[0]
    front = rows * 3 // 8 // 16 * 16
    cuts = [slice(0, front), slice(front, rows)]
    shares = lax.axis_size("head")
    pieces = gather_pieces((keys, values), "ctx")
    pieces[0], pieces[len(pieces) // 2] = in_hbm(keys), in_hbm(values)
    grad_queries, *terms = attention("ctx", pieces, queries, grad_out, chosen, cuts)
    held = [(keep, exchange(send, "ctx", 1)) for keep, send in zip(terms[::2], terms[1::2])]
    term = query_term(shares, grad_queries, w_query)
    weights = (w_key, w_value)
    received = []
    sent = []
    for keep, got in held:
        if sent:
            keep, got, _ = lax.optimization_barrier((keep, got, sent))
        arrived, sent = scatter_parts(keep, got, "ctx")
        received.append(arrived)
    grads = []
    after = []
    for cut, arrived in zip(cuts, received):
        grad_k, grad_v, *chunks = projection("head", range(shares // 2), cut, arrived, term, weights)
        chunks += projection("head", range(shares // 2, shares), cut, [grad_k, grad_v], term, weights)
        total, after = line_sum(chunks, "head", after)
        grads.append((grad_k, grad_v, total))
    grad_keys, grad_values, grad_input = (jnp.concatenate(halves, axis=0) for halves in zip(*grads))
    return (grad_queries, grad_keys, grad_values, grad_input)


def solution(mesh):
    return jax.shard_map(
        body,
        mesh=mesh,
        in_specs=(
            P("ctx", "head"),
            P("ctx", "head"),
            P("ctx", "head"),
            P("ctx", "head"),
            P("ctx", "head", None),
            P(None, "head"),
            P(None, "head"),
            P(None, "head"),
        ),
        out_specs=(P("ctx", "head"), P("ctx", "head"), P("ctx", "head"), P("ctx", "head")),
        check_vma=False,
    )
```

time: 142 us -> 113 us (0.80)
  waiting for transfers between devices: 68.5 us -> 32.9 us
  starting transfers between devices: 16.5 us -> 33.5 us
  local copies, waits for them, and re-layouts: 9.75 us -> 1.61 us
  Pallas kernels: 40 us -> 38 us
    ppermute x12 -> x22, waiting for transfers between devices: 43.3 us -> 19.4 us  [exchange(): return lax.ppermute(x, axis, [(i, i ^ mask) for i in range(n)])]
    ppermute x1 -> x2, waiting for transfers between devices: 15.8 us -> 0.01 us  [line_sum(): got_third = lax.ppermute(third, axis, [(0, 1), (2, 3), (1, 0), (3, 2)])]
    ppermute x12 -> x22, starting transfers between devices: 10.6 us -> 16.8 us  [exchange(): return lax.ppermute(x, axis, [(i, i ^ mask) for i in range(n)])]
    ppermute x1 -> x2, starting transfers between devices: 2.94 us -> 9.17 us  [line_sum(): got_passed = lax.ppermute(passed, axis, [(1, 2), (2, 1)])]
    unnamed x34 -> x18, local copies, waits for them, and re-layouts: 6.89 us -> 1.61 us
    ppermute x1 -> x2, waiting for transfers between devices: 0.01 us -> 4.5 us  [line_sum(): got_first = lax.ppermute(first, axis, [(0, 1), (3, 2), (1, 3), (2, 0)])]
    ppermute x1 -> x2, starting transfers between devices: 0.39 us -> 4.33 us  [line_sum(): got_first = lax.ppermute(first, axis, [(0, 1), (3, 2), (1, 3), (2, 0)])]
    pallas_call x4 -> x6, Pallas kernels: 40 us -> 38 us  [the longest x4 19 us: projection(): pl.pallas_call(functools.partial(projection_kernel, axis, places, cut, su...]
  transfers between devices with their start and end apart: 16 -> 30, of which waited for: 10 -> 14; matrix products, arithmetic and copies ran while one was open for 2% -> 4% of each run, Pallas kernels for 12% -> 20%
where the time goes in v2:
time: 113 us; the launch traced here: 112 us
  Pallas kernels  38 us (34%)
  starting transfers between devices  33.5 us (30%)
  waiting for transfers between devices  32.9 us (29%)
  other arithmetic  5.51 us (5%)
  local copies, waits for them, and re-layouts  1.61 us (1%)
    ppermute x22, waiting for transfers between devices, exchange(): return lax.ppermute(x, axis, [(i, i ^ mask) for i in range(n)])  19.4 us
    pallas_call x4, Pallas kernels, projection(): pl.pallas_call(functools.partial(projection_kernel, axis, places, cut, su...  19 us
    ppermute x22, starting transfers between devices, exchange(): return lax.ppermute(x, axis, [(i, i ^ mask) for i in range(n)])  16.8 us
    pallas_call x1, Pallas kernels, attention(): pl.pallas_call(functools.partial(attention_kernel, axis, n_ctx, topk, cut...  15.4 us
    ppermute x2, starting transfers between devices, line_sum(): got_passed = lax.ppermute(passed, axis, [(1, 2), (2, 1)])  9.17 us
    ppermute x2, waiting for transfers between devices, line_sum(): got_passed = lax.ppermute(passed, axis, [(1, 2), (2, 1)])  9.07 us
    ppermute x2, waiting for transfers between devices, line_sum(): got_first = lax.ppermute(first, axis, [(0, 1), (3, 2), (1, 3), (2, 0)])  4.5 us
    ppermute x2, starting transfers between devices, line_sum(): got_first = lax.ppermute(first, axis, [(0, 1), (3, 2), (1, 3), (2, 0)])  4.33 us
  transfers between devices with their start and end apart: 30, of which 14 were waited for; matrix products, arithmetic and copies ran while one was open for 4% of the time, Pallas kernels for 20%

profile of v2, /device:TPU:16, one launch (start us, length us, event | category | flops | bytes accessed | tf_op | source)
XLA Modules:
  0.0 112.3 jit_solution(15029199310509188409)
XLA Ops:
  0.6 1.6 %collective-permute-start.10 = (bf16[256,512]{1,0:T(8,128)(2,1)}, bf16[256,512]{1,0:T(8,128)(2,1)S(1)}, u32[]{:S(2)}, u32[]{:S(2)}) collective-permute-start(bf16[256,512]{1,0:T(8,128)(2,1)} %refs_8_.1), channel_id=1, source_target_pairs={{0,16},{4,20},{8,24},{12,28},{16,0},{20,4},{24,8},{28,12},{1,17},{... | collective-permute-start | bytes 786440 | tf_op jit(solution)/shard_map/ppermute | solution.py:342
  2.2 1.5 %collective-permute-start.1 = (bf16[256,512]{1,0:T(8,128)(2,1)}, bf16[256,512]{1,0:T(8,128)(2,1)S(1)}, u32[]{:S(2)}, u32[]{:S(2)}) collective-permute-start(bf16[256,512]{1,0:T(8,128)(2,1)} %refs_0_.1), channel_id=1, source_target_pairs={{0,8},{4,12},{8,0},{12,4},{16,24},{20,28},{24,16},{28,20},{1,9},{5... | collective-permute-start | bytes 786440 | tf_op jit(solution)/shard_map/ppermute | solution.py:342
  3.7 0.5 collective-permute-start.3
  4.2 0.5 collective-permute-start.8
  4.8 0.0 collective-permute-start
  4.8 5.3 %collective-permute-done.10.refs_12_ = bf16[256,512]{1,0:T(8,128)(2,1)S(1)} collective-permute-done((bf16[256,512]{1,0:T(8,128)(2,1)}, bf16[256,512]{1,0:T(8,128)(2,1)S(1)}, u32[]{:S(2)}, u32[]{:S(2)}) %collective-permute-start.10) | collective-permute-done | bytes 262176 | tf_op jit(solution)/shard_map/ppermute | solution.py:342
  10.1 0.0 collective-permute-start.7
  10.1 1.6 %collective-permute-done.1.refs_2_ = bf16[256,512]{1,0:T(8,128)(2,1)S(1)} collective-permute-done((bf16[256,512]{1,0:T(8,128)(2,1)}, bf16[256,512]{1,0:T(8,128)(2,1)S(1)}, u32[]{:S(2)}, u32[]{:S(2)}) %collective-permute-start.1) | collective-permute-done | bytes 262176 | tf_op jit(solution)/shard_map/ppermute | solution.py:342
  11.7 1.5 %collective-permute-start.12 = (bf16[256,512]{1,0:T(8,128)(2,1)S(1)}, bf16[256,512]{1,0:T(8,128)(2,1)S(1)}, u32[]{:S(2)}, u32[]{:S(2)}) collective-permute-start(bf16[256,512]{1,0:T(8,128)(2,1)S(1)} %collective-permute-done.10.refs_12_), channel_id=1, source_target_pairs={{0,8},{4,12},{8,0},{12,4},{16,24},{20,28},{24,16},{28,20},{1,9},{5... | collective-permute-start | bytes 786440 | tf_op jit(solution)/shard_map/ppermute | solution.py:342
  13.2 1.4 %collective-permute-done.3.refs_4_ = bf16[256,512]{1,0:T(8,128)(2,1)S(1)} collective-permute-done((bf16[256,512]{1,0:T(8,128)(2,1)}, bf16[256,512]{1,0:T(8,128)(2,1)S(1)}, u32[]{:S(2)}, u32[]{:S(2)}) %collective-permute-start.3) | collective-permute-done | bytes 262176 | tf_op jit(solution)/shard_map/ppermute | solution.py:342
  14.6 1.5 %collective-permute-start.5 = (bf16[256,512]{1,0:T(8,128)(2,1)S(1)}, bf16[256,512]{1,0:T(8,128)(2,1)S(1)}, u32[]{:S(2)}, u32[]{:S(2)}) collective-permute-start(bf16[256,512]{1,0:T(8,128)(2,1)S(1)} %collective-permute-done.1.refs_2_), channel_id=1, source_target_pairs={{0,16},{4,20},{8,24},{12,28},{16,0},{20,4},{24,8},{28,12},{1,17},{... | collective-permute-start | bytes 786440 | tf_op jit(solution)/shard_map/ppermute | solution.py:342
  16.1 1.2 %collective-permute-done.8.refs_10_ = bf16[256,512]{1,0:T(8,128)(2,1)S(1)} collective-permute-done((bf16[256,512]{1,0:T(8,128)(2,1)}, bf16[256,512]{1,0:T(8,128)(2,1)S(1)}, u32[]{:S(2)}, u32[]{:S(2)}) %collective-permute-start.8) | collective-permute-done | bytes 262176 | tf_op jit(solution)/shard_map/ppermute | solution.py:342
  17.3 0.5 collective-permute-start.2
  17.8 0.1 collective-permute-start.4
  17.9 3.6 %collective-permute-done.12.refs_14_ = bf16[256,512]{1,0:T(8,128)(2,1)S(1)} collective-permute-done((bf16[256,512]{1,0:T(8,128)(2,1)S(1)}, bf16[256,512]{1,0:T(8,128)(2,1)S(1)}, u32[]{:S(2)}, u32[]{:S(2)}) %collective-permute-start.12) | collective-permute-done | bytes 262176 | tf_op jit(solution)/shard_map/ppermute | solution.py:342
  21.4 0.0 collective-permute-start.9
  21.4 0.3 collective-permute-done.5.refs_6_
  21.7 0.2 collective-permute-start.13
  21.9 0.0 collective-permute-done.11.refs_13_
  21.9 0.3 collective-permute-start.6
  22.3 0.7 collective-permute-done.9.refs_11_
  23.0 0.4 collective-permute-done.13.refs_15_
  23.3 0.4 collective-permute-done.6.refs_7_
  23.7 0.7 copy-done.8
  24.4 15.4 %attention.1 = (bf16[256,1024]{1,0:T(8,128)(2,1)}, bf16[384,1024]{1,0:T(8,128)(2,1)S(1)}, bf16[384,1024]{1,0:T(8,128)(2,1)S(1)}, bf16[640,1024]{1,0:T(8,128)(2,1)S(1)}, bf16[640,1024]{1,0:T(8,128)(2,1)S(1)}) custom-call(s32[4,4,16]{2,1,0:T(4,128)S(1)} %copy-done.8, bf16[256,512]{1,0:T(8,128)(2,1)} %refs_0_.1, ...), custom_call_target="tpu_custom_call" | custom-call | flops 2684354560 | bytes 33554432 | tf_op jit(solution)/shard_map/attention/pallas_call | solution.py:193
  39.8 0.2 collective-permute-start.18
  40.0 0.4 collective-permute-start.14
  40.4 3.6 %collective-permute-done.14.refs_1_ = bf16[384,1024]{1,0:T(8,128)(2,1)S(1)} collective-permute-done((bf16[384,1024]{1,0:T(8,128)(2,1)S(1)}, bf16[384,1024]{1,0:T(8,128)(2,1)S(1)}, u32[]{:S(2)}, u32[]{:S(2)}) %collective-permute-start.14) | collective-permute-done | bytes 786464 | tf_op jit(solution)/shard_map/ppermute | solution.py:342
  44.0 0.2 add_convert_fusion.3
  44.2 2.5 %collective-permute-start.15 = (bf16[96,1024]{1,0:T(8,128)(2,1)S(1)}, bf16[96,1024]{1,0:T(8,128)(2,1)S(1)}, u32[]{:S(2)}, u32[]{:S(2)}) collective-permute-start(bf16[96,1024]{1,0:T(8,128)(2,1)S(1)} %get-tuple-element.53), channel_id=1, source_target_pairs={{0,24},{4,28},{8,16},{12,20},{16,8},{20,12},{24,0},{28,4},{1,25},{... | collective-permute-start | bytes 589832 | tf_op jit(solution)/shard_map/ppermute | solution.py:342
  46.7 0.6 collective-permute-start.16
  47.3 0.5 collective-permute-start.17
  47.8 1.2 %add_convert_fusion = (bf16[160,1024]{1,0:T(8,128)(2,1)}, bf16[160,1024]{1,0:T(8,128)(2,1)}, bf16[160,1024]{1,0:T(8,128)(2,1)}) fusion(bf16[640,1024]{1,0:T(8,128)(2,1)S(1)} %collective-permute-done.18.refs_1_, bf16[640,1024]{1,0:T(8,128)(2,1)S(1)} %get-tuple-element.32.refs_0_), kind=kLoop, calls=%fused_computation.8 | loop fusion | flops 1966080 | bytes 2949120 | tf_op jit(solution)/shard_map/convert_element_type | solution.py:365
  49.0 0.2 copy-done.3
  49.2 2.4 %collective-permute-start.19 = (bf16[160,1024]{1,0:T(8,128)(2,1)}, bf16[160,1024]{1,0:T(8,128)(2,1)S(1)}, u32[]{:S(2)}, u32[]{:S(2)}) collective-permute-start(bf16[160,1024]{1,0:T(8,128)(2,1)} %get-tuple-element.50), channel_id=1, source_target_pairs={{0,24},{4,28},{8,16},{12,20},{16,8},{20,12},{24,0},{28,4},{1,25},{... | collective-permute-start | bytes 983048 | tf_op jit(solution)/shard_map/ppermute | solution.py:342
  51.6 0.6 collective-permute-start.20
  52.1 0.9 collective-permute-done.15.refs_2_
  53.0 1.5 %collective-permute-start.21 = (bf16[160,1024]{1,0:T(8,128)(2,1)}, bf16[160,1024]{1,0:T(8,128)(2,1)}, u32[]{:S(2)}, u32[]{:S(2)}) collective-permute-start(bf16[160,1024]{1,0:T(8,128)(2,1)} %get-tuple-element.48), channel_id=1, source_target_pairs={{0,8},{4,12},{8,0},{12,4},{16,24},{20,28},{24,16},{28,20},{1,9},{5... | collective-permute-start | bytes 983048 | tf_op jit(solution)/shard_map/ppermute | solution.py:342
  54.5 3.6 %query_term.1.refs_5_.refs_2_ = bf16[4,256,1152]{2,1,0:T(8,128)(2,1)S(1)} custom-call(bf16[256,1024]{1,0:T(8,128)(2,1)S(1)} %copy-done.5, bf16[4608,1024]{1,0:T(8,128)(2,1)S(1)} %copy-done), custom_call_target="tpu_custom_call" | custom-call | flops 2415919104 | bytes 9437184 | tf_op jit(solution)/shard_map/query_term/pallas_call | solution.py:233
  58.1 5.1 %projection.4 = (bf16[96,512]{1,0:T(8,128)(2,1)S(1)}, bf16[96,512]{1,0:T(8,128)(2,1)S(1)}, bf16[96,1152]{1,0:T(8,128)(2,1)}, bf16[96,1152]{1,0:T(8,128)(2,1)S(1)}) custom-call(bf16[384,1024]{1,0:T(8,128)(2,1)S(1)} %get-tuple-element.27.refs_0_, bf16[384,1024]{1,0:T(8,128)(2,1)S(1)} %collective-permute-done.14.refs_1_, ...), custom_call_target="tpu_custom_call" | custom-call | flops 452984832 | bytes 4718592 | tf_op jit(solution)/shard_map/projection/pallas_call | solution.py:315
  63.2 0.0 copy-start.6
  63.2 0.7 copy-done.6
  63.9 0.3 collective-permute-start.22
  64.3 4.5 %projection.6 = (bf16[96,1152]{1,0:T(8,128)(2,1)S(1)}, bf16[96,1152]{1,0:T(8,128)(2,1)S(1)}) custom-call(bf16[96,512]{1,0:T(8,128)(2,1)S(1)} %get-tuple-element.29.refs_0_, bf16[96,512]{1,0:T(8,128)(2,1)S(1)} %get-tuple-element.35.refs_1_, bf16[4,256,1152]{2,1,0:T(8,128)(2,1)S(1)} %query_term.1.refs_5_.refs_2_, bf16[4608,512]{1,0:T(8,128)(2,1)} %refs_3_.3, ...), custom_call_target="tpu_custom_call" | custom-call | flops 452984832 | bytes 4718592 | tf_op jit(solution)/shard_map/projection/pallas_call | solution.py:315
  68.8 1.8 %collective-permute-start.24 = (bf16[96,1152]{1,0:T(8,128)(2,1)S(1)}, bf16[96,1152]{1,0:T(8,128)(2,1)S(1)}, u32[]{:S(2)}, u32[]{:S(2)}) collective-permute-start(bf16[96,1152]{1,0:T(8,128)(2,1)S(1)} %get-tuple-element.40), channel_id=1, source_target_pairs={{0,1},{2,3},{1,0},{3,2},{4,5},{6,7},{5,4},{7,6},{8,9},{10,11},{9,8... | collective-permute-start | bytes 663560 | tf_op jit(solution)/shard_map/ppermute | solution.py:385
  70.5 0.0 collective-permute-done.19.refs_2_
  70.5 0.7 collective-permute-start.23
  71.2 0.0 collective-permute-done.20.refs_3_
  71.2 5.0 %projection.5 = (bf16[160,512]{1,0:T(8,128)(2,1)S(1)}, bf16[160,512]{1,0:T(8,128)(2,1)S(1)}, bf16[160,1152]{1,0:T(8,128)(2,1)S(1)}, bf16[160,1152]{1,0:T(8,128)(2,1)S(1)}) custom-call(bf16[640,1024]{1,0:T(8,128)(2,1)S(1)} %copy-done.2, bf16[640,1024]{1,0:T(8,128)(2,1)S(1)} %copy-done.4, bf16[160,1024]{1,0:T(8,128)(2,1)S(1)} %collective-permute-done.19.refs_2_, ...), custom_call_target="tpu_custom_call" | custom-call | flops 754974720 | bytes 4718592 | tf_op jit(solution)/shard_map/projection/pallas_call | solution.py:315
  76.2 4.0 %collective-permute-start.26 = (bf16[160,1152]{1,0:T(8,128)(2,1)S(1)}, bf16[160,1152]{1,0:T(8,128)(2,1)S(1)}, u32[]{:S(2)}, u32[]{:S(2)}) collective-permute-start(bf16[160,1152]{1,0:T(8,128)(2,1)S(1)} %get-tuple-element.45), channel_id=1, source_target_pairs={{0,1},{3,2},{1,3},{2,0},{4,5},{7,6},{5,7},{6,4},{8,9},{11,10},{9,1... | collective-permute-start | bytes 1105928 | tf_op jit(solution)/shard_map/ppermute | solution.py:383
  80.2 1.0 fusion.11
  81.2 4.6 %collective-permute-start.25 = (bf16[96,1152]{1,0:T(8,128)(2,1)S(1)}, bf16[96,1152]{1,0:T(8,128)(2,1)S(1)}, u32[]{:S(2)}, u32[]{:S(2)}) collective-permute-start(bf16[96,1152]{1,0:T(8,128)(2,1)S(1)} %fusion.11), channel_id=1, source_target_pairs={{1,2},{2,1},{5,6},{6,5},{9,10},{10,9},{13,14},{14,13},{17,18},{18,... | collective-permute-start | bytes 663560 | tf_op jit(solution)/shard_map/ppermute | solution.py:387
  85.8 4.5 %projection.7 = (bf16[160,1152]{1,0:T(8,128)(2,1)S(1)}, bf16[160,1152]{1,0:T(8,128)(2,1)S(1)}) custom-call(bf16[160,512]{1,0:T(8,128)(2,1)S(1)} %get-tuple-element.34.refs_0_, bf16[160,512]{1,0:T(8,128)(2,1)S(1)} %get-tuple-element.36.refs_1_, bf16[4,256,1152]{2,1,0:T(8,128)(2,1)S(1)} %query_term.1.refs_5_.refs_2_, bf16[4608,512]{1,0:T(8,128)(2,1)} %refs_3_.3, ...), custom_call_target="tpu_custom_call" | custom-call | flops 754974720 | bytes 4718592 | tf_op jit(solution)/shard_map/projection/pallas_call | solution.py:315
  90.3 0.7 collective-permute-start.27
  91.0 0.1 collective-permute-start.28
  91.1 4.5 %collective-permute-done.26 = bf16[160,1152]{1,0:T(8,128)(2,1)S(1)} collective-permute-done((bf16[160,1152]{1,0:T(8,128)(2,1)S(1)}, bf16[160,1152]{1,0:T(8,128)(2,1)S(1)}, u32[]{:S(2)}, u32[]{:S(2)}) %collective-permute-start.26) | collective-permute-done | bytes 368672 | tf_op jit(solution)/shard_map/ppermute | solution.py:383
  95.6 0.1 fusion.5
  95.7 4.6 %collective-permute-start.29 = (bf16[160,1152]{1,0:T(8,128)(2,1)S(1)}, bf16[160,1152]{1,0:T(8,128)(2,1)S(1)}, u32[]{:S(2)}, u32[]{:S(2)}) collective-permute-start(bf16[160,1152]{1,0:T(8,128)(2,1)S(1)} %fusion.5), channel_id=1, source_target_pairs={{1,2},{2,1},{5,6},{6,5},{9,10},{10,9},{13,14},{14,13},{17,18},{18,... | collective-permute-start | bytes 1105928 | tf_op jit(solution)/shard_map/ppermute | solution.py:387
  100.2 4.8 %collective-permute-done.25 = bf16[96,1152]{1,0:T(8,128)(2,1)S(1)} collective-permute-done((bf16[96,1152]{1,0:T(8,128)(2,1)S(1)}, bf16[96,1152]{1,0:T(8,128)(2,1)S(1)}, u32[]{:S(2)}, u32[]{:S(2)}) %collective-permute-start.25) | collective-permute-done | bytes 221216 | tf_op jit(solution)/shard_map/ppermute | solution.py:387
  105.0 1.1 fusion.10
  106.1 0.8 pad_maximum_fusion.1
  106.9 4.3 %collective-permute-done.29 = bf16[160,1152]{1,0:T(8,128)(2,1)S(1)} collective-permute-done((bf16[160,1152]{1,0:T(8,128)(2,1)S(1)}, bf16[160,1152]{1,0:T(8,128)(2,1)S(1)}, u32[]{:S(2)}, u32[]{:S(2)}) %collective-permute-start.29) | collective-permute-done | bytes 368672 | tf_op jit(solution)/shard_map/ppermute | solution.py:387
  111.2 0.3 fusion.4
  111.5 0.9 pad_maximum_fusion
  (28 shorter events, 0.1 us)
Async XLA Ops:
  0.6 9.5 %collective-permute-start.10 = (bf16[256,512]{1,0:T(8,128)(2,1)}, bf16[256,512]{1,0:T(8,128)(2,1)S(1)}, u32[]{:S(2)}, u32[]{:S(2)}) collective-permute-start(bf16[256,512]{1,0:T(8,128)(2,1)} %refs_8_.1), channel_id=1, source_target_pairs={{0,16},{4,20},{8,24},{12,28},{16,0},{20,4},{24,8},{28,12},{1,17},{... | collective-permute-start | bytes 786440 | tf_op jit(solution)/shard_map/ppermute | solution.py:342
  2.2 9.4 %collective-permute-start.1 = (bf16[256,512]{1,0:T(8,128)(2,1)}, bf16[256,512]{1,0:T(8,128)(2,1)S(1)}, u32[]{:S(2)}, u32[]{:S(2)}) collective-permute-start(bf16[256,512]{1,0:T(8,128)(2,1)} %refs_0_.1), channel_id=1, source_target_pairs={{0,8},{4,12},{8,0},{12,4},{16,24},{20,28},{24,16},{28,20},{1,9},{5... | collective-permute-start | bytes 786440 | tf_op jit(solution)/shard_map/ppermute | solution.py:342
  3.7 10.9 %collective-permute-start.3 = (bf16[256,512]{1,0:T(8,128)(2,1)}, bf16[256,512]{1,0:T(8,128)(2,1)S(1)}, u32[]{:S(2)}, u32[]{:S(2)}) collective-permute-start(bf16[256,512]{1,0:T(8,128)(2,1)} %refs_0_.1), channel_id=1, source_target_pairs={{0,16},{4,20},{8,24},{12,28},{16,0},{20,4},{24,8},{28,12},{1,17},{... | collective-permute-start | bytes 786440 | tf_op jit(solution)/shard_map/ppermute | solution.py:342
  4.2 13.1 %collective-permute-start.8 = (bf16[256,512]{1,0:T(8,128)(2,1)}, bf16[256,512]{1,0:T(8,128)(2,1)S(1)}, u32[]{:S(2)}, u32[]{:S(2)}) collective-permute-start(bf16[256,512]{1,0:T(8,128)(2,1)} %refs_8_.1), channel_id=1, source_target_pairs={{0,8},{4,12},{8,0},{12,4},{16,24},{20,28},{24,16},{28,20},{1,9},{5... | collective-permute-start | bytes 786440 | tf_op jit(solution)/shard_map/ppermute | solution.py:342
  4.8 12.5 %collective-permute-start = (bf16[256,512]{1,0:T(8,128)(2,1)}, bf16[256,512]{1,0:T(8,128)(2,1)S(1)}, u32[]{:S(2)}, u32[]{:S(2)}) collective-permute-start(bf16[256,512]{1,0:T(8,128)(2,1)} %refs_0_.1), channel_id=1, source_target_pairs={{0,4},{4,0},{8,12},{12,8},{16,20},{20,16},{24,28},{28,24},{1,5},{5... | collective-permute-start | bytes 786440 | tf_op jit(solution)/shard_map/ppermute | solution.py:342
  10.1 7.7 %collective-permute-start.7 = (bf16[256,512]{1,0:T(8,128)(2,1)}, bf16[256,512]{1,0:T(8,128)(2,1)S(1)}, u32[]{:S(2)}, u32[]{:S(2)}) collective-permute-start(bf16[256,512]{1,0:T(8,128)(2,1)} %refs_8_.1), channel_id=1, source_target_pairs={{0,4},{4,0},{8,12},{12,8},{16,20},{20,16},{24,28},{28,24},{1,5},{5... | collective-permute-start | bytes 786440 | tf_op jit(solution)/shard_map/ppermute | solution.py:342
  11.7 9.8 %collective-permute-start.12 = (bf16[256,512]{1,0:T(8,128)(2,1)S(1)}, bf16[256,512]{1,0:T(8,128)(2,1)S(1)}, u32[]{:S(2)}, u32[]{:S(2)}) collective-permute-start(bf16[256,512]{1,0:T(8,128)(2,1)S(1)} %collective-permute-done.10.refs_12_), channel_id=1, source_target_pairs={{0,8},{4,12},{8,0},{12,4},{16,24},{20,28},{24,16},{28,20},{1,9},{5... | collective-permute-start | bytes 786440 | tf_op jit(solution)/shard_map/ppermute | solution.py:342
  14.6 7.2 %collective-permute-start.5 = (bf16[256,512]{1,0:T(8,128)(2,1)S(1)}, bf16[256,512]{1,0:T(8,128)(2,1)S(1)}, u32[]{:S(2)}, u32[]{:S(2)}) collective-permute-start(bf16[256,512]{1,0:T(8,128)(2,1)S(1)} %collective-permute-done.1.refs_2_), channel_id=1, source_target_pairs={{0,16},{4,20},{8,24},{12,28},{16,0},{20,4},{24,8},{28,12},{1,17},{... | collective-permute-start | bytes 786440 | tf_op jit(solution)/shard_map/ppermute | solution.py:342
  17.3 4.7 %collective-permute-start.11 = (bf16[256,512]{1,0:T(8,128)(2,1)S(1)}, bf16[256,512]{1,0:T(8,128)(2,1)S(1)}, u32[]{:S(2)}, u32[]{:S(2)}) collective-permute-start(bf16[256,512]{1,0:T(8,128)(2,1)S(1)} %collective-permute-done.10.refs_12_), channel_id=1, source_target_pairs={{0,4},{4,0},{8,12},{12,8},{16,20},{20,16},{24,28},{28,24},{1,5},{5... | collective-permute-start | bytes 786440 | tf_op jit(solution)/shard_map/ppermute | solution.py:342
  17.3 5.0 %collective-permute-start.2 = (bf16[256,512]{1,0:T(8,128)(2,1)S(1)}, bf16[256,512]{1,0:T(8,128)(2,1)S(1)}, u32[]{:S(2)}, u32[]{:S(2)}) collective-permute-start(bf16[256,512]{1,0:T(8,128)(2,1)S(1)} %collective-permute-done.1.refs_2_), channel_id=1, source_target_pairs={{0,4},{4,0},{8,12},{12,8},{16,20},{20,16},{24,28},{28,24},{1,5},{5... | collective-permute-start | bytes 786440 | tf_op jit(solution)/shard_map/ppermute | solution.py:342
  17.8 4.5 %collective-permute-start.4 = (bf16[256,512]{1,0:T(8,128)(2,1)S(1)}, bf16[256,512]{1,0:T(8,128)(2,1)S(1)}, u32[]{:S(2)}, u32[]{:S(2)}) collective-permute-start(bf16[256,512]{1,0:T(8,128)(2,1)S(1)} %collective-permute-done.3.refs_4_), channel_id=1, source_target_pairs={{0,4},{4,0},{8,12},{12,8},{16,20},{20,16},{24,28},{28,24},{1,5},{5... | collective-permute-start | bytes 786440 | tf_op jit(solution)/shard_map/ppermute | solution.py:342
  21.4 1.5 %collective-permute-start.9 = (bf16[256,512]{1,0:T(8,128)(2,1)S(1)}, bf16[256,512]{1,0:T(8,128)(2,1)S(1)}, u32[]{:S(2)}, u32[]{:S(2)}) collective-permute-start(bf16[256,512]{1,0:T(8,128)(2,1)S(1)} %collective-permute-done.8.refs_10_), channel_id=1, source_target_pairs={{0,4},{4,0},{8,12},{12,8},{16,20},{20,16},{24,28},{28,24},{1,5},{5... | collective-permute-start | bytes 786440 | tf_op jit(solution)/shard_map/ppermute | solution.py:342
  21.7 1.6 %collective-permute-start.13 = (bf16[256,512]{1,0:T(8,128)(2,1)S(1)}, bf16[256,512]{1,0:T(8,128)(2,1)S(1)}, u32[]{:S(2)}, u32[]{:S(2)}) collective-permute-start(bf16[256,512]{1,0:T(8,128)(2,1)S(1)} %collective-permute-done.12.refs_14_), channel_id=1, source_target_pairs={{0,4},{4,0},{8,12},{12,8},{16,20},{20,16},{24,28},{28,24},{1,5},{5... | collective-permute-start | bytes 786440 | tf_op jit(solution)/shard_map/ppermute | solution.py:342
  21.9 1.8 %collective-permute-start.6 = (bf16[256,512]{1,0:T(8,128)(2,1)S(1)}, bf16[256,512]{1,0:T(8,128)(2,1)S(1)}, u32[]{:S(2)}, u32[]{:S(2)}) collective-permute-start(bf16[256,512]{1,0:T(8,128)(2,1)S(1)} %collective-permute-done.5.refs_6_), channel_id=1, source_target_pairs={{0,4},{4,0},{8,12},{12,8},{16,20},{20,16},{24,28},{28,24},{1,5},{5... | collective-permute-start | bytes 786440 | tf_op jit(solution)/shard_map/ppermute | solution.py:342
  23.7 0.7 copy-start.8
  24.4 30.1 %copy-start = (bf16[4608,1024]{1,0:T(8,128)(2,1)S(1)}, bf16[4608,1024]{1,0:T(8,128)(2,1)}, u32[]{:S(2)}) copy-start(bf16[4608,1024]{1,0:T(8,128)(2,1)} %w_ref.1) | copy-start | bytes 28311556
  39.8 9.2 %copy-start.1 = (bf16[640,1024]{1,0:T(8,128)(2,1)}, bf16[640,1024]{1,0:T(8,128)(2,1)S(1)}, u32[]{:S(2)}) copy-start(bf16[640,1024]{1,0:T(8,128)(2,1)S(1)} %get-tuple-element.32.refs_0_) | copy-start | bytes 3932164
  39.8 8.0 %collective-permute-start.18 = (bf16[640,1024]{1,0:T(8,128)(2,1)S(1)}, bf16[640,1024]{1,0:T(8,128)(2,1)S(1)}, u32[]{:S(2)}, u32[]{:S(2)}) collective-permute-start(bf16[640,1024]{1,0:T(8,128)(2,1)S(1)} %get-tuple-element.31), channel_id=1, source_target_pairs={{0,4},{4,0},{8,12},{12,8},{16,20},{20,16},{24,28},{28,24},{1,5},{5... | collective-permute-start | bytes 3932168 | tf_op jit(solution)/shard_map/ppermute | solution.py:342
  40.0 4.0 %collective-permute-start.14 = (bf16[384,1024]{1,0:T(8,128)(2,1)S(1)}, bf16[384,1024]{1,0:T(8,128)(2,1)S(1)}, u32[]{:S(2)}, u32[]{:S(2)}) collective-permute-start(bf16[384,1024]{1,0:T(8,128)(2,1)S(1)} %get-tuple-element.28), channel_id=1, source_target_pairs={{0,4},{4,0},{8,12},{12,8},{16,20},{20,16},{24,28},{28,24},{1,5},{5... | collective-permute-start | bytes 2359304 | tf_op jit(solution)/shard_map/ppermute | solution.py:342
  44.2 8.8 %collective-permute-start.15 = (bf16[96,1024]{1,0:T(8,128)(2,1)S(1)}, bf16[96,1024]{1,0:T(8,128)(2,1)S(1)}, u32[]{:S(2)}, u32[]{:S(2)}) collective-permute-start(bf16[96,1024]{1,0:T(8,128)(2,1)S(1)} %get-tuple-element.53), channel_id=1, source_target_pairs={{0,24},{4,28},{8,16},{12,20},{16,8},{20,12},{24,0},{28,4},{1,25},{... | collective-permute-start | bytes 589832 | tf_op jit(solution)/shard_map/ppermute | solution.py:342
  46.7 11.4 %collective-permute-start.16 = (bf16[96,1024]{1,0:T(8,128)(2,1)S(1)}, bf16[96,1024]{1,0:T(8,128)(2,1)S(1)}, u32[]{:S(2)}, u32[]{:S(2)}) collective-permute-start(bf16[96,1024]{1,0:T(8,128)(2,1)S(1)} %get-tuple-element.52), channel_id=1, source_target_pairs={{0,16},{4,20},{8,24},{12,28},{16,0},{20,4},{24,8},{28,12},{1,17},{... | collective-permute-start | bytes 589832 | tf_op jit(solution)/shard_map/ppermute | solution.py:342
  47.3 10.8 %collective-permute-start.17 = (bf16[96,1024]{1,0:T(8,128)(2,1)S(1)}, bf16[96,1024]{1,0:T(8,128)(2,1)S(1)}, u32[]{:S(2)}, u32[]{:S(2)}) collective-permute-start(bf16[96,1024]{1,0:T(8,128)(2,1)S(1)} %get-tuple-element.51), channel_id=1, source_target_pairs={{0,8},{4,12},{8,0},{12,4},{16,24},{20,28},{24,16},{28,20},{1,9},{5... | collective-permute-start | bytes 589832 | tf_op jit(solution)/shard_map/ppermute | solution.py:342
  47.8 1.4 %copy-start.3 = (bf16[640,1024]{1,0:T(8,128)(2,1)}, bf16[640,1024]{1,0:T(8,128)(2,1)S(1)}, u32[]{:S(2)}) copy-start(bf16[640,1024]{1,0:T(8,128)(2,1)S(1)} %collective-permute-done.18.refs_1_) | copy-start | bytes 3932164
  47.8 6.7 %copy-start.5 = (bf16[256,1024]{1,0:T(8,128)(2,1)S(1)}, bf16[256,1024]{1,0:T(8,128)(2,1)}, u32[]{:S(2)}) copy-start(bf16[256,1024]{1,0:T(8,128)(2,1)} %get-tuple-element.22.gq_ref) | copy-start | bytes 1572868
  49.2 21.3 %collective-permute-start.19 = (bf16[160,1024]{1,0:T(8,128)(2,1)}, bf16[160,1024]{1,0:T(8,128)(2,1)S(1)}, u32[]{:S(2)}, u32[]{:S(2)}) collective-permute-start(bf16[160,1024]{1,0:T(8,128)(2,1)} %get-tuple-element.50), channel_id=1, source_target_pairs={{0,24},{4,28},{8,16},{12,20},{16,8},{20,12},{24,0},{28,4},{1,25},{... | collective-permute-start | bytes 983048 | tf_op jit(solution)/shard_map/ppermute | solution.py:342
  51.6 19.6 %collective-permute-start.20 = (bf16[160,1024]{1,0:T(8,128)(2,1)}, bf16[160,1024]{1,0:T(8,128)(2,1)S(1)}, u32[]{:S(2)}, u32[]{:S(2)}) collective-permute-start(bf16[160,1024]{1,0:T(8,128)(2,1)} %get-tuple-element.49), channel_id=1, source_target_pairs={{0,16},{4,20},{8,24},{12,28},{16,0},{20,4},{24,8},{28,12},{1,17},{... | collective-permute-start | bytes 983048 | tf_op jit(solution)/shard_map/ppermute | solution.py:342
  53.0 18.2 %collective-permute-start.21 = (bf16[160,1024]{1,0:T(8,128)(2,1)}, bf16[160,1024]{1,0:T(8,128)(2,1)}, u32[]{:S(2)}, u32[]{:S(2)}) collective-permute-start(bf16[160,1024]{1,0:T(8,128)(2,1)} %get-tuple-element.48), channel_id=1, source_target_pairs={{0,8},{4,12},{8,0},{12,4},{16,24},{20,28},{24,16},{28,20},{1,9},{5... | collective-permute-start | bytes 983048 | tf_op jit(solution)/shard_map/ppermute | solution.py:342
  63.2 0.7 copy-start.6
  63.9 16.3 %collective-permute-start.22 = (bf16[96,1152]{1,0:T(8,128)(2,1)}, bf16[96,1152]{1,0:T(8,128)(2,1)}, u32[]{:S(2)}, u32[]{:S(2)}) collective-permute-start(bf16[96,1152]{1,0:T(8,128)(2,1)} %get-tuple-element.38), channel_id=1, source_target_pairs={{0,1},{3,2},{1,3},{2,0},{4,5},{7,6},{5,7},{6,4},{8,9},{11,10},{9,1... | collective-permute-start | bytes 663560 | tf_op jit(solution)/shard_map/ppermute | solution.py:383
  64.3 6.2 %copy-start.7 = (bf16[96,1152]{1,0:T(8,128)(2,1)S(1)}, bf16[96,1152]{1,0:T(8,128)(2,1)}, u32[]{:S(2)}) copy-start(bf16[96,1152]{1,0:T(8,128)(2,1)} %copy-done.6) | copy-start | bytes 663556
  64.3 6.9 %copy-start.2 = (bf16[640,1024]{1,0:T(8,128)(2,1)S(1)}, bf16[640,1024]{1,0:T(8,128)(2,1)}, u32[]{:S(2)}) copy-start(bf16[640,1024]{1,0:T(8,128)(2,1)} %copy-done.1) | copy-start | bytes 3932164
  64.3 6.9 %copy-start.4 = (bf16[640,1024]{1,0:T(8,128)(2,1)S(1)}, bf16[640,1024]{1,0:T(8,128)(2,1)}, u32[]{:S(2)}) copy-start(bf16[640,1024]{1,0:T(8,128)(2,1)} %copy-done.3) | copy-start | bytes 3932164
  68.8 21.5 %collective-permute-start.24 = (bf16[96,1152]{1,0:T(8,128)(2,1)S(1)}, bf16[96,1152]{1,0:T(8,128)(2,1)S(1)}, u32[]{:S(2)}, u32[]{:S(2)}) collective-permute-start(bf16[96,1152]{1,0:T(8,128)(2,1)S(1)} %get-tuple-element.40), channel_id=1, source_target_pairs={{0,1},{2,3},{1,0},{3,2},{4,5},{6,7},{5,4},{7,6},{8,9},{10,11},{9,8... | collective-permute-start | bytes 663560 | tf_op jit(solution)/shard_map/ppermute | solution.py:385
  70.5 19.8 %collective-permute-start.23 = (bf16[96,1152]{1,0:T(8,128)(2,1)S(1)}, bf16[96,1152]{1,0:T(8,128)(2,1)S(1)}, u32[]{:S(2)}, u32[]{:S(2)}) collective-permute-start(bf16[96,1152]{1,0:T(8,128)(2,1)S(1)} %copy-done.7), channel_id=1, source_target_pairs={{0,3},{3,0},{4,7},{7,4},{8,11},{11,8},{12,15},{15,12},{16,19},{19,... | collective-permute-start | bytes 663560 | tf_op jit(solution)/shard_map/ppermute | solution.py:384
  76.2 19.4 %collective-permute-start.26 = (bf16[160,1152]{1,0:T(8,128)(2,1)S(1)}, bf16[160,1152]{1,0:T(8,128)(2,1)S(1)}, u32[]{:S(2)}, u32[]{:S(2)}) collective-permute-start(bf16[160,1152]{1,0:T(8,128)(2,1)S(1)} %get-tuple-element.45), channel_id=1, source_target_pairs={{0,1},{3,2},{1,3},{2,0},{4,5},{7,6},{5,7},{6,4},{8,9},{11,10},{9,1... | collective-permute-start | bytes 1105928 | tf_op jit(solution)/shard_map/ppermute | solution.py:383
  81.2 23.8 %collective-permute-start.25 = (bf16[96,1152]{1,0:T(8,128)(2,1)S(1)}, bf16[96,1152]{1,0:T(8,128)(2,1)S(1)}, u32[]{:S(2)}, u32[]{:S(2)}) collective-permute-start(bf16[96,1152]{1,0:T(8,128)(2,1)S(1)} %fusion.11), channel_id=1, source_target_pairs={{1,2},{2,1},{5,6},{6,5},{9,10},{10,9},{13,14},{14,13},{17,18},{18,... | collective-permute-start | bytes 663560 | tf_op jit(solution)/shard_map/ppermute | solution.py:387
  90.3 16.6 %collective-permute-start.27 = (bf16[160,1152]{1,0:T(8,128)(2,1)S(1)}, bf16[160,1152]{1,0:T(8,128)(2,1)S(1)}, u32[]{:S(2)}, u32[]{:S(2)}) collective-permute-start(bf16[160,1152]{1,0:T(8,128)(2,1)S(1)} %get-tuple-element.46), channel_id=1, source_target_pairs={{0,3},{3,0},{4,7},{7,4},{8,11},{11,8},{12,15},{15,12},{16,19},{19,... | collective-permute-start | bytes 1105928 | tf_op jit(solution)/shard_map/ppermute | solution.py:384
  91.0 16.0 %collective-permute-start.28 = (bf16[160,1152]{1,0:T(8,128)(2,1)S(1)}, bf16[160,1152]{1,0:T(8,128)(2,1)S(1)}, u32[]{:S(2)}, u32[]{:S(2)}) collective-permute-start(bf16[160,1152]{1,0:T(8,128)(2,1)S(1)} %get-tuple-element.47), channel_id=1, source_target_pairs={{0,1},{2,3},{1,0},{3,2},{4,5},{6,7},{5,4},{7,6},{8,9},{10,11},{9,8... | collective-permute-start | bytes 1105928 | tf_op jit(solution)/shard_map/ppermute | solution.py:385
  95.7 15.6 %collective-permute-start.29 = (bf16[160,1152]{1,0:T(8,128)(2,1)S(1)}, bf16[160,1152]{1,0:T(8,128)(2,1)S(1)}, u32[]{:S(2)}, u32[]{:S(2)}) collective-permute-start(bf16[160,1152]{1,0:T(8,128)(2,1)S(1)} %fusion.5), channel_id=1, source_target_pairs={{1,2},{2,1},{5,6},{6,5},{9,10},{10,9},{13,14},{14,13},{17,18},{18,... | collective-permute-start | bytes 1105928 | tf_op jit(solution)/shard_map/ppermute | solution.py:387

commit v3 on v2

--- a/solution.py
+++ b/solution.py
@@ -17,9 +17,9 @@
     return pltpu.with_memory_space_constraint(x, pltpu.HBM)
 
 
-def attention_kernel(axis, n_ctx, topk, cuts, chosen, *refs):
-    pieces, (q_hbm, g_hbm, dq_hbm, *out_hbm), scratch = refs[: 2 * n_ctx], refs[2 * n_ctx : -13], refs[-13:]
-    k_all, v_all, q_all, g_all, acc, near, scores, packed, operand, dq_all, staged, arrived, left = scratch
+def attention_kernel(axis, n_ctx, topk, cuts, chosen_hbm, *refs):
+    pieces, (q_hbm, g_hbm, dq_hbm, *out_hbm), scratch = refs[: 2 * n_ctx], refs[2 * n_ctx : -14], refs[-14:]
+    k_all, v_all, q_all, g_all, acc, near, scores, packed, operand, dq_all, staged, chosen, arrived, left = scratch
     calls = acc.shape[0]
     rows = q_hbm.shape[0]
     wide = 2 * HEAD_DIM
@@ -36,7 +36,7 @@
 
     def arrivals(late):
         at = slice(HEAD_DIM, None) if late else slice(0, HEAD_DIM)
-        copies = [] if late else [(q_hbm, q_all), (g_hbm, g_all)]
+        copies = [] if late else [(chosen_hbm, chosen), (q_hbm, q_all), (g_hbm, g_all)]
         for side, held in ((0, k_all), (1, v_all)):
             for k in range(n_ctx):
                 copies.append((pieces[side * n_ctx + k].at[:, at], held.at[device_rows(k), at]))
@@ -120,12 +120,12 @@
         for i in range(topk):
             acc[j, block_rows(picks[i]), :] += terms[tile(i), :]
         dq = scaling * lax.dot_general(
+            near[b][:, :HEAD_DIM],
             packed[b][:, :lanes],
-            near[b][:, :HEAD_DIM],
             (((0,), (0,)), ((), ())),
             preferred_element_type=jnp.float32,
         )
-        dq = dq.astype(jnp.bfloat16)
+        dq = dq.T.astype(jnp.bfloat16)
         for h in range(heads_per):
             dq_all[tile(b), columns_of(j * heads_per + h)] = dq[tile(h), :]
 
@@ -194,31 +194,28 @@
         functools.partial(attention_kernel, axis, n_ctx, topk, cuts),
         out_shape=[jax.ShapeDtypeStruct(queries.shape, jnp.bfloat16)]
         + [jax.ShapeDtypeStruct((size, groups * wide), jnp.bfloat16) for size in sizes],
-        grid_spec=pltpu.PrefetchScalarGridSpec(
-            num_scalar_prefetch=1,
-            grid=(1,),
-            in_specs=[anywhere] * (2 * n_ctx + 2),
-            out_specs=[anywhere] * (1 + len(sizes)),
-            scratch_shapes=[
-                bf16(n_ctx * rows, groups * HEAD_DIM),
-                bf16(n_ctx * rows, groups * HEAD_DIM),
-                bf16(*queries.shape),
-                bf16(*queries.shape),
-                f32(groups, n_ctx * rows, wide),
-                [bf16(near, wide)] * blocks,
-                [f32(near, 2 * lanes)] * blocks,
-                [bf16(near, 2 * lanes)] * blocks,
-                [bf16(2 * lanes, wide)] * blocks,
-                bf16(*queries.shape),
-                bf16(groups, n_ctx * rows, wide),
-                pltpu.SemaphoreType.DMA((2, 2 * n_ctx + 2)),
-                pltpu.SemaphoreType.DMA((groups, 1 + len(sizes))),
-            ],
-        ),
-        compiler_params=pltpu.CompilerParams(vmem_limit_bytes=36 * 2**20),
+        in_specs=[anywhere] * (2 * n_ctx + 3),
+        out_specs=[anywhere] * (1 + len(sizes)),
+        scratch_shapes=[
+            bf16(n_ctx * rows, groups * HEAD_DIM),
+            bf16(n_ctx * rows, groups * HEAD_DIM),
+            bf16(*queries.shape),
+            bf16(*queries.shape),
+            f32(groups, n_ctx * rows, wide),
+            [bf16(near, wide)] * blocks,
+            [f32(near, 2 * lanes)] * blocks,
+            [bf16(near, 2 * lanes)] * blocks,
+            [bf16(2 * lanes, wide)] * blocks,
+            bf16(*queries.shape),
+            bf16(groups, n_ctx * rows, wide),
+            pltpu.SMEM(chosen.shape, jnp.int32),
+            pltpu.SemaphoreType.DMA((2, 2 * n_ctx + 3)),
+            pltpu.SemaphoreType.DMA((groups, 1 + len(sizes))),
+        ],
+        compiler_params=pltpu.CompilerParams(vmem_limit_bytes=28 * 2**20),
         cost_estimate=pl.CostEstimate(flops=flops, bytes_accessed=16 * n_ctx * rows * wide * groups, transcendentals=0),
         name="attention",
-    )(chosen, *pieces, in_hbm(queries), in_hbm(grad_out))
+    )(in_hbm(chosen), *pieces, in_hbm(queries), in_hbm(grad_out))
 
 
 def query_term_kernel(gq_ref, w_ref, out_ref):
@@ -307,7 +304,7 @@
     rows = cut.stop - cut.start
     columns = weights[0].shape[1]
     width = term.shape[2]
-    out_shape = [jax.ShapeDtypeStruct((rows, width), jnp.bfloat16)] * count
+    out_shape = [pltpu.HBM((rows, width), jnp.bfloat16)] * count
     if summed > 2:
         out_shape = [jax.ShapeDtypeStruct((rows, columns), jnp.bfloat16)] * 2 + out_shape
     bf16 = lambda *shape: pltpu.VMEM(shape, jnp.bfloat16)
@@ -408,13 +405,17 @@
 
 def body(queries, keys, values, grad_out, chosen, w_query, w_key, w_value):
     rows = queries.shape[0]
-    front = rows * 3 // 8 // 16 * 16
+    front = rows * 5 // 16 // 16 * 16
     cuts = [slice(0, front), slice(front, rows)]
     shares = lax.axis_size("head")
     pieces = gather_pieces((keys, values), "ctx")
     pieces[0], pieces[len(pieces) // 2] = in_hbm(keys), in_hbm(values)
     grad_queries, *terms = attention("ctx", pieces, queries, grad_out, chosen, cuts)
-    held = [(keep, exchange(send, "ctx", 1)) for keep, send in zip(terms[::2], terms[1::2])]
+    held = []
+    for keep, send in zip(terms[::2], terms[1::2]):
+        if held:
+            send, _ = lax.optimization_barrier((send, held[-1][1]))
+        held.append((keep, exchange(send, "ctx", 1)))
     term = query_term(shares, grad_queries, w_query)
     weights = (w_key, w_value)
     received = []
@@ -427,11 +428,15 @@
     grads = []
     after = []
     for cut, arrived in zip(cuts, received):
-        grad_k, grad_v, *chunks = projection("head", range(shares // 2), cut, arrived, term, weights)
-        chunks += projection("head", range(shares // 2, shares), cut, [grad_k, grad_v], term, weights)
+        early = shares // 2
+        grad_k, grad_v, *chunks = projection("head", range(early), cut, arrived, term, weights)
+        chunks += projection("head", range(early, shares), cut, [grad_k, grad_v], term, weights)
         total, after = line_sum(chunks, "head", after)
         grads.append((grad_k, grad_v, total))
-    grad_keys, grad_values, grad_input = (jnp.concatenate(halves, axis=0) for halves in zip(*grads))
+    grad_keys, grad_values, grad_input = (
+        lax.dynamic_update_slice(jnp.pad(head, ((0, tail.shape[0]), (0, 0))), tail, (head.shape[0], 0))
+        for head, tail in zip(*grads)
+    )
     return (grad_queries, grad_keys, grad_values, grad_input)
 
 

time: 113 us -> 109 us (0.965)
  other arithmetic: 5.51 us -> 3.7 us
  local copies, waits for them, and re-layouts: 1.61 us -> 0.24 us
    ppermute x2, waiting for transfers between devices: 4.5 us -> 7.41 us  [line_sum(): got_first = lax.ppermute(first, axis, [(0, 1), (3, 2), (1, 3), (2, 0)])]
    ppermute x2, waiting for transfers between devices: 9.07 us -> 6.17 us  [line_sum(): got_passed = lax.ppermute(passed, axis, [(1, 2), (2, 1)])]
    ppermute x22, waiting for transfers between devices: 19.4 us -> 17.5 us  [exchange(): return lax.ppermute(x, axis, [(i, i ^ mask) for i in range(n)])]
    concatenate x2 -> x0, other arithmetic: 1.69 us -> none  [body(): jnp.concatenate(halves, axis=0)]
    dynamic_update_slice x0 -> x2, other arithmetic: none -> 1.69 us  [body(): lax.dynamic_update_slice(jnp.pad(head, ((0, tail.shape[0]), (0, 0))), tai...]
    pallas_call x4, Pallas kernels: 19 us -> 20.5 us  [projection(): pl.pallas_call(functools.partial(projection_kernel, axis, places, cut, su...]
    unnamed x18 -> x20, local copies, waits for them, and re-layouts: 1.61 us -> 0.24 us
  transfers between devices with their start and end apart: 30 -> 30, of which waited for: 14 -> 16; matrix products, arithmetic and copies ran while one was open for 4% -> 2% of each run, Pallas kernels for 20% -> 22%
where the time goes in v3:
time: 109 us
  Pallas kernels  38.6 us (35%)
  starting transfers between devices  33.4 us (31%)
  waiting for transfers between devices  32.1 us (29%)
  other arithmetic  3.7 us (3%)
    pallas_call x4, Pallas kernels, projection(): pl.pallas_call(functools.partial(projection_kernel, axis, places, cut, su...  20.5 us
    ppermute x22, waiting for transfers between devices, exchange(): return lax.ppermute(x, axis, [(i, i ^ mask) for i in range(n)])  17.5 us
    ppermute x22, starting transfers between devices, exchange(): return lax.ppermute(x, axis, [(i, i ^ mask) for i in range(n)])  16.6 us
    pallas_call x1, Pallas kernels, attention(): pl.pallas_call(functools.partial(attention_kernel, axis, n_ctx, topk, cut...  14.6 us
    ppermute x2, starting transfers between devices, line_sum(): got_passed = lax.ppermute(passed, axis, [(1, 2), (2, 1)])  9.55 us
    ppermute x2, waiting for transfers between devices, line_sum(): got_first = lax.ppermute(first, axis, [(0, 1), (3, 2), (1, 3), (2, 0)])  7.41 us
    ppermute x2, waiting for transfers between devices, line_sum(): got_passed = lax.ppermute(passed, axis, [(1, 2), (2, 1)])  6.17 us
    ppermute x2, starting transfers between devices, line_sum(): got_first = lax.ppermute(first, axis, [(0, 1), (3, 2), (1, 3), (2, 0)])  3.98 us
  transfers between devices with their start and end apart: 30, of which 16 were waited for; matrix products, arithmetic and copies ran while one was open for 2% of the time, Pallas kernels for 22%

profile of v3, /device:TPU:16, one launch (start us, length us, event | category | flops | bytes accessed | tf_op | source)
XLA Modules:
  0.0 109.0 jit_solution(1923826835768817388)
XLA Ops:
  0.6 1.6 %collective-permute-start.10 = (bf16[256,512]{1,0:T(8,128)(2,1)}, bf16[256,512]{1,0:T(8,128)(2,1)S(1)}, u32[]{:S(2)}, u32[]{:S(2)}) collective-permute-start(bf16[256,512]{1,0:T(8,128)(2,1)} %refs_8_.1), channel_id=1, source_target_pairs={{0,16},{4,20},{8,24},{12,28},{16,0},{20,4},{24,8},{28,12},{1,17},{... | collective-permute-start | bytes 786440 | tf_op jit(solution)/shard_map/ppermute | solution.py:339
  2.2 1.5 %collective-permute-start.1 = (bf16[256,512]{1,0:T(8,128)(2,1)}, bf16[256,512]{1,0:T(8,128)(2,1)S(1)}, u32[]{:S(2)}, u32[]{:S(2)}) collective-permute-start(bf16[256,512]{1,0:T(8,128)(2,1)} %refs_0_.1), channel_id=1, source_target_pairs={{0,8},{4,12},{8,0},{12,4},{16,24},{20,28},{24,16},{28,20},{1,9},{5... | collective-permute-start | bytes 786440 | tf_op jit(solution)/shard_map/ppermute | solution.py:339
  3.7 0.5 collective-permute-start.3
  4.2 0.5 collective-permute-start.8
  4.8 5.3 %collective-permute-done.10.refs_12_ = bf16[256,512]{1,0:T(8,128)(2,1)S(1)} collective-permute-done((bf16[256,512]{1,0:T(8,128)(2,1)}, bf16[256,512]{1,0:T(8,128)(2,1)S(1)}, u32[]{:S(2)}, u32[]{:S(2)}) %collective-permute-start.10) | collective-permute-done | bytes 262176 | tf_op jit(solution)/shard_map/ppermute | solution.py:339
  10.1 1.6 %collective-permute-done.1.refs_2_ = bf16[256,512]{1,0:T(8,128)(2,1)S(1)} collective-permute-done((bf16[256,512]{1,0:T(8,128)(2,1)}, bf16[256,512]{1,0:T(8,128)(2,1)S(1)}, u32[]{:S(2)}, u32[]{:S(2)}) %collective-permute-start.1) | collective-permute-done | bytes 262176 | tf_op jit(solution)/shard_map/ppermute | solution.py:339
  11.7 1.5 %collective-permute-start.12 = (bf16[256,512]{1,0:T(8,128)(2,1)S(1)}, bf16[256,512]{1,0:T(8,128)(2,1)S(1)}, u32[]{:S(2)}, u32[]{:S(2)}) collective-permute-start(bf16[256,512]{1,0:T(8,128)(2,1)S(1)} %collective-permute-done.10.refs_12_), channel_id=1, source_target_pairs={{0,8},{4,12},{8,0},{12,4},{16,24},{20,28},{24,16},{28,20},{1,9},{5... | collective-permute-start | bytes 786440 | tf_op jit(solution)/shard_map/ppermute | solution.py:339
  13.2 1.4 %collective-permute-done.3.refs_4_ = bf16[256,512]{1,0:T(8,128)(2,1)S(1)} collective-permute-done((bf16[256,512]{1,0:T(8,128)(2,1)}, bf16[256,512]{1,0:T(8,128)(2,1)S(1)}, u32[]{:S(2)}, u32[]{:S(2)}) %collective-permute-start.3) | collective-permute-done | bytes 262176 | tf_op jit(solution)/shard_map/ppermute | solution.py:339
  14.6 1.5 %collective-permute-start.5 = (bf16[256,512]{1,0:T(8,128)(2,1)S(1)}, bf16[256,512]{1,0:T(8,128)(2,1)S(1)}, u32[]{:S(2)}, u32[]{:S(2)}) collective-permute-start(bf16[256,512]{1,0:T(8,128)(2,1)S(1)} %collective-permute-done.1.refs_2_), channel_id=1, source_target_pairs={{0,16},{4,20},{8,24},{12,28},{16,0},{20,4},{24,8},{28,12},{1,17},{... | collective-permute-start | bytes 786440 | tf_op jit(solution)/shard_map/ppermute | solution.py:339
  16.1 1.2 %collective-permute-done.8.refs_10_ = bf16[256,512]{1,0:T(8,128)(2,1)S(1)} collective-permute-done((bf16[256,512]{1,0:T(8,128)(2,1)}, bf16[256,512]{1,0:T(8,128)(2,1)S(1)}, u32[]{:S(2)}, u32[]{:S(2)}) %collective-permute-start.8) | collective-permute-done | bytes 262176 | tf_op jit(solution)/shard_map/ppermute | solution.py:339
  17.3 0.0 collective-permute-start.11
  17.3 0.0 collective-permute-done.refs_1_
  17.3 0.5 collective-permute-start.2
  17.8 0.0 collective-permute-done.7.refs_9_
  17.8 0.1 collective-permute-start.4
  17.9 3.6 %collective-permute-done.12.refs_14_ = bf16[256,512]{1,0:T(8,128)(2,1)S(1)} collective-permute-done((bf16[256,512]{1,0:T(8,128)(2,1)S(1)}, bf16[256,512]{1,0:T(8,128)(2,1)S(1)}, u32[]{:S(2)}, u32[]{:S(2)}) %collective-permute-start.12) | collective-permute-done | bytes 262176 | tf_op jit(solution)/shard_map/ppermute | solution.py:339
  21.4 0.3 collective-permute-done.5.refs_6_
  21.7 0.2 collective-permute-start.13
  21.9 0.3 collective-permute-start.6
  22.3 0.0 collective-permute-done.2.refs_3_
  22.3 0.0 collective-permute-done.4.refs_5_
  22.3 0.7 collective-permute-done.9.refs_11_
  23.0 0.4 collective-permute-done.13.refs_15_
  23.3 0.4 collective-permute-done.6.refs_7_
  23.7 14.6 %attention.1 = (bf16[256,1024]{1,0:T(8,128)(2,1)}, bf16[320,1024]{1,0:T(8,128)(2,1)S(1)}, bf16[320,1024]{1,0:T(8,128)(2,1)S(1)}, bf16[704,1024]{1,0:T(8,128)(2,1)S(1)}, bf16[704,1024]{1,0:T(8,128)(2,1)S(1)}) custom-call(s32[4,4,16]{2,1,0:T(4,128)} %chosen_hbm.1, bf16[256,512]{1,0:T(8,128)(2,1)} %refs_0_.1, ...), custom_call_target="tpu_custom_call" | custom-call | flops 2684354560 | bytes 33554432 | tf_op jit(solution)/shard_map/attention/pallas_call | solution.py:193
  38.3 0.2 collective-permute-start.14
  38.5 2.0 %collective-permute-done.14.refs_1_ = bf16[320,1024]{1,0:T(8,128)(2,1)S(1)} collective-permute-done((bf16[320,1024]{1,0:T(8,128)(2,1)S(1)}, bf16[320,1024]{1,0:T(8,128)(2,1)S(1)}, u32[]{:S(2)}, u32[]{:S(2)}) %collective-permute-start.14) | collective-permute-done | bytes 655392 | tf_op jit(solution)/shard_map/ppermute | solution.py:339
  40.5 0.1 collective-permute-start.18
  40.6 0.2 add_convert_fusion.3
  40.8 2.5 %collective-permute-start.15 = (bf16[80,1024]{1,0:T(8,128)(2,1)S(1)}, bf16[80,1024]{1,0:T(8,128)(2,1)S(1)}, u32[]{:S(2)}, u32[]{:S(2)}) collective-permute-start(bf16[80,1024]{1,0:T(8,128)(2,1)S(1)} %get-tuple-element.55), channel_id=1, source_target_pairs={{0,24},{4,28},{8,16},{12,20},{16,8},{20,12},{24,0},{28,4},{1,25},{... | collective-permute-start | bytes 491528 | tf_op jit(solution)/shard_map/ppermute | solution.py:339
  43.3 0.5 collective-permute-start.16
  43.8 0.5 collective-permute-start.17
  44.4 1.3 %add_convert_fusion = (bf16[176,1024]{1,0:T(8,128)(2,1)}, bf16[176,1024]{1,0:T(8,128)(2,1)}, bf16[176,1024]{1,0:T(8,128)(2,1)}) fusion(bf16[704,1024]{1,0:T(8,128)(2,1)S(1)} %collective-permute-done.18.refs_1_, bf16[704,1024]{1,0:T(8,128)(2,1)S(1)} %get-tuple-element.34.refs_0_), kind=kLoop, calls=%fused_computation.8 | loop fusion | flops 2162688 | bytes 3244032 | tf_op jit(solution)/shard_map/convert_element_type | solution.py:362
  45.6 0.2 copy-done.3
  45.8 2.4 %collective-permute-start.19 = (bf16[176,1024]{1,0:T(8,128)(2,1)}, bf16[176,1024]{1,0:T(8,128)(2,1)S(1)}, u32[]{:S(2)}, u32[]{:S(2)}) collective-permute-start(bf16[176,1024]{1,0:T(8,128)(2,1)} %get-tuple-element.52), channel_id=1, source_target_pairs={{0,24},{4,28},{8,16},{12,20},{16,8},{20,12},{24,0},{28,4},{1,25},{... | collective-permute-start | bytes 1081352 | tf_op jit(solution)/shard_map/ppermute | solution.py:339
  48.2 0.5 collective-permute-start.20
  48.8 0.0 collective-permute-done.15.refs_2_
  48.8 1.5 %collective-permute-start.21 = (bf16[176,1024]{1,0:T(8,128)(2,1)}, bf16[176,1024]{1,0:T(8,128)(2,1)}, u32[]{:S(2)}, u32[]{:S(2)}) collective-permute-start(bf16[176,1024]{1,0:T(8,128)(2,1)} %get-tuple-element.50), channel_id=1, source_target_pairs={{0,8},{4,12},{8,0},{12,4},{16,24},{20,28},{24,16},{28,20},{1,9},{5... | collective-permute-start | bytes 1081352 | tf_op jit(solution)/shard_map/ppermute | solution.py:339
  50.3 3.5 %query_term.1.refs_5_.refs_2_ = bf16[4,256,1152]{2,1,0:T(8,128)(2,1)S(1)} custom-call(bf16[256,1024]{1,0:T(8,128)(2,1)S(1)} %copy-done.5, bf16[4608,1024]{1,0:T(8,128)(2,1)S(1)} %copy-done), custom_call_target="tpu_custom_call" | custom-call | flops 2415919104 | bytes 9437184 | tf_op jit(solution)/shard_map/query_term/pallas_call | solution.py:230
  53.9 5.3 %projection.4 = (bf16[80,512]{1,0:T(8,128)(2,1)S(1)}, bf16[80,512]{1,0:T(8,128)(2,1)S(1)}, bf16[80,1152]{1,0:T(8,128)(2,1)}, bf16[80,1152]{1,0:T(8,128)(2,1)}) custom-call(bf16[320,1024]{1,0:T(8,128)(2,1)S(1)} %get-tuple-element.28.refs_0_, bf16[320,1024]{1,0:T(8,128)(2,1)S(1)} %collective-permute-done.14.refs_1_, ...), custom_call_target="tpu_custom_call" | custom-call | flops 377487360 | bytes 4718592 | tf_op jit(solution)/shard_map/projection/pallas_call | solution.py:312
  59.2 0.6 collective-permute-start.22
  59.8 4.5 %projection.6 = (bf16[80,1152]{1,0:T(8,128)(2,1)}, bf16[80,1152]{1,0:T(8,128)(2,1)}) custom-call(bf16[80,512]{1,0:T(8,128)(2,1)S(1)} %get-tuple-element.30.refs_0_, bf16[80,512]{1,0:T(8,128)(2,1)S(1)} %get-tuple-element.37.refs_1_, bf16[4,256,1152]{2,1,0:T(8,128)(2,1)S(1)} %query_term.1.refs_5_.refs_2_, bf16[4608,512]{1,0:T(8,128)(2,1)} %refs_3_.3, ...), custom_call_target="tpu_custom_call" | custom-call | flops 377487360 | bytes 4718592 | tf_op jit(solution)/shard_map/projection/pallas_call | solution.py:312
  64.3 1.7 %collective-permute-start.24 = (bf16[80,1152]{1,0:T(8,128)(2,1)}, bf16[80,1152]{1,0:T(8,128)(2,1)S(1)}, u32[]{:S(2)}, u32[]{:S(2)}) collective-permute-start(bf16[80,1152]{1,0:T(8,128)(2,1)} %get-tuple-element.42), channel_id=1, source_target_pairs={{0,1},{2,3},{1,0},{3,2},{4,5},{6,7},{5,4},{7,6},{8,9},{10,11},{9,8... | collective-permute-start | bytes 552968 | tf_op jit(solution)/shard_map/ppermute | solution.py:382
  66.1 0.7 collective-permute-start.23
  66.7 0.6 collective-permute-done.20.refs_3_
  67.3 0.1 collective-permute-done.21.refs_4_
  67.4 5.7 %projection.5 = (bf16[176,512]{1,0:T(8,128)(2,1)S(1)}, bf16[176,512]{1,0:T(8,128)(2,1)S(1)}, bf16[176,1152]{1,0:T(8,128)(2,1)}, bf16[176,1152]{1,0:T(8,128)(2,1)}) custom-call(bf16[704,1024]{1,0:T(8,128)(2,1)S(1)} %copy-done.2, bf16[704,1024]{1,0:T(8,128)(2,1)S(1)} %copy-done.4, bf16[176,1024]{1,0:T(8,128)(2,1)S(1)} %collective-permute-done.19.refs_2_, ...), custom_call_target="tpu_custom_call" | custom-call | flops 830472192 | bytes 4718592 | tf_op jit(solution)/shard_map/projection/pallas_call | solution.py:312
  73.0 3.4 %collective-permute-start.26 = (bf16[176,1152]{1,0:T(8,128)(2,1)}, bf16[176,1152]{1,0:T(8,128)(2,1)S(1)}, u32[]{:S(2)}, u32[]{:S(2)}) collective-permute-start(bf16[176,1152]{1,0:T(8,128)(2,1)} %get-tuple-element.47), channel_id=1, source_target_pairs={{0,1},{3,2},{1,3},{2,0},{4,5},{7,6},{5,7},{6,4},{8,9},{11,10},{9,1... | collective-permute-start | bytes 1216520 | tf_op jit(solution)/shard_map/ppermute | solution.py:380
  76.5 4.6 %collective-permute-start.25 = (bf16[80,1152]{1,0:T(8,128)(2,1)S(1)}, bf16[80,1152]{1,0:T(8,128)(2,1)S(1)}, u32[]{:S(2)}, u32[]{:S(2)}) collective-permute-start(bf16[80,1152]{1,0:T(8,128)(2,1)S(1)} %fusion.11), channel_id=1, source_target_pairs={{1,2},{2,1},{5,6},{6,5},{9,10},{10,9},{13,14},{14,13},{17,18},{18,... | collective-permute-start | bytes 552968 | tf_op jit(solution)/shard_map/ppermute | solution.py:384
  81.1 5.0 %projection.7 = (bf16[176,1152]{1,0:T(8,128)(2,1)}, bf16[176,1152]{1,0:T(8,128)(2,1)}) custom-call(bf16[176,512]{1,0:T(8,128)(2,1)S(1)} %get-tuple-element.36.refs_0_, bf16[176,512]{1,0:T(8,128)(2,1)S(1)} %get-tuple-element.38.refs_1_, bf16[4,256,1152]{2,1,0:T(8,128)(2,1)S(1)} %query_term.1.refs_5_.refs_2_, bf16[4608,512]{1,0:T(8,128)(2,1)} %refs_3_.3, ...), custom_call_target="tpu_custom_call" | custom-call | flops 830472192 | bytes 4718592 | tf_op jit(solution)/shard_map/projection/pallas_call | solution.py:312
  86.2 0.0 collective-permute-done.24
  86.2 0.8 collective-permute-start.27
  87.0 0.1 collective-permute-start.28
  87.1 7.4 %collective-permute-done.26 = bf16[176,1152]{1,0:T(8,128)(2,1)S(1)} collective-permute-done((bf16[176,1152]{1,0:T(8,128)(2,1)}, bf16[176,1152]{1,0:T(8,128)(2,1)S(1)}, u32[]{:S(2)}, u32[]{:S(2)}) %collective-permute-start.26) | collective-permute-done | bytes 405536 | tf_op jit(solution)/shard_map/ppermute | solution.py:380
  94.5 0.1 fusion.5
  94.6 5.0 %collective-permute-start.29 = (bf16[176,1152]{1,0:T(8,128)(2,1)S(1)}, bf16[176,1152]{1,0:T(8,128)(2,1)S(1)}, u32[]{:S(2)}, u32[]{:S(2)}) collective-permute-start(bf16[176,1152]{1,0:T(8,128)(2,1)S(1)} %fusion.5), channel_id=1, source_target_pairs={{1,2},{2,1},{5,6},{6,5},{9,10},{10,9},{13,14},{14,13},{17,18},{18,... | collective-permute-start | bytes 1216520 | tf_op jit(solution)/shard_map/ppermute | solution.py:384
  99.6 2.7 %collective-permute-done.25 = bf16[80,1152]{1,0:T(8,128)(2,1)S(1)} collective-permute-done((bf16[80,1152]{1,0:T(8,128)(2,1)S(1)}, bf16[80,1152]{1,0:T(8,128)(2,1)S(1)}, u32[]{:S(2)}, u32[]{:S(2)}) %collective-permute-start.25) | collective-permute-done | bytes 184352 | tf_op jit(solution)/shard_map/ppermute | solution.py:384
  102.3 0.1 fusion.10
  102.4 0.8 pad_maximum_fusion.1
  103.2 0.0 collective-permute-done.27
  103.2 1.1 collective-permute-done.28
  104.3 3.5 %collective-permute-done.29 = bf16[176,1152]{1,0:T(8,128)(2,1)S(1)} collective-permute-done((bf16[176,1152]{1,0:T(8,128)(2,1)S(1)}, bf16[176,1152]{1,0:T(8,128)(2,1)S(1)}, u32[]{:S(2)}, u32[]{:S(2)}) %collective-permute-start.29) | collective-permute-done | bytes 405536 | tf_op jit(solution)/shard_map/ppermute | solution.py:384
  107.8 0.3 fusion.4
  108.1 0.9 pad_maximum_fusion
  (30 shorter events, 0.1 us)
Async XLA Ops:
  0.6 9.5 %collective-permute-start.10 = (bf16[256,512]{1,0:T(8,128)(2,1)}, bf16[256,512]{1,0:T(8,128)(2,1)S(1)}, u32[]{:S(2)}, u32[]{:S(2)}) collective-permute-start(bf16[256,512]{1,0:T(8,128)(2,1)} %refs_8_.1), channel_id=1, source_target_pairs={{0,16},{4,20},{8,24},{12,28},{16,0},{20,4},{24,8},{28,12},{1,17},{... | collective-permute-start | bytes 786440 | tf_op jit(solution)/shard_map/ppermute | solution.py:339
  2.2 9.4 %collective-permute-start.1 = (bf16[256,512]{1,0:T(8,128)(2,1)}, bf16[256,512]{1,0:T(8,128)(2,1)S(1)}, u32[]{:S(2)}, u32[]{:S(2)}) collective-permute-start(bf16[256,512]{1,0:T(8,128)(2,1)} %refs_0_.1), channel_id=1, source_target_pairs={{0,8},{4,12},{8,0},{12,4},{16,24},{20,28},{24,16},{28,20},{1,9},{5... | collective-permute-start | bytes 786440 | tf_op jit(solution)/shard_map/ppermute | solution.py:339
  3.7 10.9 %collective-permute-start.3 = (bf16[256,512]{1,0:T(8,128)(2,1)}, bf16[256,512]{1,0:T(8,128)(2,1)S(1)}, u32[]{:S(2)}, u32[]{:S(2)}) collective-permute-start(bf16[256,512]{1,0:T(8,128)(2,1)} %refs_0_.1), channel_id=1, source_target_pairs={{0,16},{4,20},{8,24},{12,28},{16,0},{20,4},{24,8},{28,12},{1,17},{... | collective-permute-start | bytes 786440 | tf_op jit(solution)/shard_map/ppermute | solution.py:339
  4.2 13.1 %collective-permute-start.8 = (bf16[256,512]{1,0:T(8,128)(2,1)}, bf16[256,512]{1,0:T(8,128)(2,1)S(1)}, u32[]{:S(2)}, u32[]{:S(2)}) collective-permute-start(bf16[256,512]{1,0:T(8,128)(2,1)} %refs_8_.1), channel_id=1, source_target_pairs={{0,8},{4,12},{8,0},{12,4},{16,24},{20,28},{24,16},{28,20},{1,9},{5... | collective-permute-start | bytes 786440 | tf_op jit(solution)/shard_map/ppermute | solution.py:339
  4.8 12.5 %collective-permute-start = (bf16[256,512]{1,0:T(8,128)(2,1)}, bf16[256,512]{1,0:T(8,128)(2,1)S(1)}, u32[]{:S(2)}, u32[]{:S(2)}) collective-permute-start(bf16[256,512]{1,0:T(8,128)(2,1)} %refs_0_.1), channel_id=1, source_target_pairs={{0,4},{4,0},{8,12},{12,8},{16,20},{20,16},{24,28},{28,24},{1,5},{5... | collective-permute-start | bytes 786440 | tf_op jit(solution)/shard_map/ppermute | solution.py:339
  10.1 7.7 %collective-permute-start.7 = (bf16[256,512]{1,0:T(8,128)(2,1)}, bf16[256,512]{1,0:T(8,128)(2,1)S(1)}, u32[]{:S(2)}, u32[]{:S(2)}) collective-permute-start(bf16[256,512]{1,0:T(8,128)(2,1)} %refs_8_.1), channel_id=1, source_target_pairs={{0,4},{4,0},{8,12},{12,8},{16,20},{20,16},{24,28},{28,24},{1,5},{5... | collective-permute-start | bytes 786440 | tf_op jit(solution)/shard_map/ppermute | solution.py:339
  11.7 9.8 %collective-permute-start.12 = (bf16[256,512]{1,0:T(8,128)(2,1)S(1)}, bf16[256,512]{1,0:T(8,128)(2,1)S(1)}, u32[]{:S(2)}, u32[]{:S(2)}) collective-permute-start(bf16[256,512]{1,0:T(8,128)(2,1)S(1)} %collective-permute-done.10.refs_12_), channel_id=1, source_target_pairs={{0,8},{4,12},{8,0},{12,4},{16,24},{20,28},{24,16},{28,20},{1,9},{5... | collective-permute-start | bytes 786440 | tf_op jit(solution)/shard_map/ppermute | solution.py:339
  14.6 7.2 %collective-permute-start.5 = (bf16[256,512]{1,0:T(8,128)(2,1)S(1)}, bf16[256,512]{1,0:T(8,128)(2,1)S(1)}, u32[]{:S(2)}, u32[]{:S(2)}) collective-permute-start(bf16[256,512]{1,0:T(8,128)(2,1)S(1)} %collective-permute-done.1.refs_2_), channel_id=1, source_target_pairs={{0,16},{4,20},{8,24},{12,28},{16,0},{20,4},{24,8},{28,12},{1,17},{... | collective-permute-start | bytes 786440 | tf_op jit(solution)/shard_map/ppermute | solution.py:339
  17.3 4.7 %collective-permute-start.11 = (bf16[256,512]{1,0:T(8,128)(2,1)S(1)}, bf16[256,512]{1,0:T(8,128)(2,1)S(1)}, u32[]{:S(2)}, u32[]{:S(2)}) collective-permute-start(bf16[256,512]{1,0:T(8,128)(2,1)S(1)} %collective-permute-done.10.refs_12_), channel_id=1, source_target_pairs={{0,4},{4,0},{8,12},{12,8},{16,20},{20,16},{24,28},{28,24},{1,5},{5... | collective-permute-start | bytes 786440 | tf_op jit(solution)/shard_map/ppermute | solution.py:339
  17.3 5.0 %collective-permute-start.2 = (bf16[256,512]{1,0:T(8,128)(2,1)S(1)}, bf16[256,512]{1,0:T(8,128)(2,1)S(1)}, u32[]{:S(2)}, u32[]{:S(2)}) collective-permute-start(bf16[256,512]{1,0:T(8,128)(2,1)S(1)} %collective-permute-done.1.refs_2_), channel_id=1, source_target_pairs={{0,4},{4,0},{8,12},{12,8},{16,20},{20,16},{24,28},{28,24},{1,5},{5... | collective-permute-start | bytes 786440 | tf_op jit(solution)/shard_map/ppermute | solution.py:339
  17.8 4.5 %collective-permute-start.4 = (bf16[256,512]{1,0:T(8,128)(2,1)S(1)}, bf16[256,512]{1,0:T(8,128)(2,1)S(1)}, u32[]{:S(2)}, u32[]{:S(2)}) collective-permute-start(bf16[256,512]{1,0:T(8,128)(2,1)S(1)} %collective-permute-done.3.refs_4_), channel_id=1, source_target_pairs={{0,4},{4,0},{8,12},{12,8},{16,20},{20,16},{24,28},{28,24},{1,5},{5... | collective-permute-start | bytes 786440 | tf_op jit(solution)/shard_map/ppermute | solution.py:339
  21.4 1.5 %collective-permute-start.9 = (bf16[256,512]{1,0:T(8,128)(2,1)S(1)}, bf16[256,512]{1,0:T(8,128)(2,1)S(1)}, u32[]{:S(2)}, u32[]{:S(2)}) collective-permute-start(bf16[256,512]{1,0:T(8,128)(2,1)S(1)} %collective-permute-done.8.refs_10_), channel_id=1, source_target_pairs={{0,4},{4,0},{8,12},{12,8},{16,20},{20,16},{24,28},{28,24},{1,5},{5... | collective-permute-start | bytes 786440 | tf_op jit(solution)/shard_map/ppermute | solution.py:339
  21.7 1.6 %collective-permute-start.13 = (bf16[256,512]{1,0:T(8,128)(2,1)S(1)}, bf16[256,512]{1,0:T(8,128)(2,1)S(1)}, u32[]{:S(2)}, u32[]{:S(2)}) collective-permute-start(bf16[256,512]{1,0:T(8,128)(2,1)S(1)} %collective-permute-done.12.refs_14_), channel_id=1, source_target_pairs={{0,4},{4,0},{8,12},{12,8},{16,20},{20,16},{24,28},{28,24},{1,5},{5... | collective-permute-start | bytes 786440 | tf_op jit(solution)/shard_map/ppermute | solution.py:339
  21.9 1.8 %collective-permute-start.6 = (bf16[256,512]{1,0:T(8,128)(2,1)S(1)}, bf16[256,512]{1,0:T(8,128)(2,1)S(1)}, u32[]{:S(2)}, u32[]{:S(2)}) collective-permute-start(bf16[256,512]{1,0:T(8,128)(2,1)S(1)} %collective-permute-done.5.refs_6_), channel_id=1, source_target_pairs={{0,4},{4,0},{8,12},{12,8},{16,20},{20,16},{24,28},{28,24},{1,5},{5... | collective-permute-start | bytes 786440 | tf_op jit(solution)/shard_map/ppermute | solution.py:339
  23.7 26.6 %copy-start = (bf16[4608,1024]{1,0:T(8,128)(2,1)S(1)}, bf16[4608,1024]{1,0:T(8,128)(2,1)}, u32[]{:S(2)}) copy-start(bf16[4608,1024]{1,0:T(8,128)(2,1)} %w_ref.1) | copy-start | bytes 28311556
  38.3 7.3 %copy-start.1 = (bf16[704,1024]{1,0:T(8,128)(2,1)}, bf16[704,1024]{1,0:T(8,128)(2,1)S(1)}, u32[]{:S(2)}) copy-start(bf16[704,1024]{1,0:T(8,128)(2,1)S(1)} %get-tuple-element.34.refs_0_) | copy-start | bytes 4325380
  38.3 2.2 %collective-permute-start.14 = (bf16[320,1024]{1,0:T(8,128)(2,1)S(1)}, bf16[320,1024]{1,0:T(8,128)(2,1)S(1)}, u32[]{:S(2)}, u32[]{:S(2)}) collective-permute-start(bf16[320,1024]{1,0:T(8,128)(2,1)S(1)} %get-tuple-element.29), channel_id=1, source_target_pairs={{0,4},{4,0},{8,12},{12,8},{16,20},{20,16},{24,28},{28,24},{1,5},{5... | collective-permute-start | bytes 1966088 | tf_op jit(solution)/shard_map/ppermute | solution.py:339
  40.5 3.9 %collective-permute-start.18 = (bf16[704,1024]{1,0:T(8,128)(2,1)S(1)}, bf16[704,1024]{1,0:T(8,128)(2,1)S(1)}, u32[]{:S(2)}, u32[]{:S(2)}) collective-permute-start(bf16[704,1024]{1,0:T(8,128)(2,1)S(1)} %get-tuple-element.33), channel_id=1, source_target_pairs={{0,4},{4,0},{8,12},{12,8},{16,20},{20,16},{24,28},{28,24},{1,5},{5... | collective-permute-start | bytes 4325384 | tf_op jit(solution)/shard_map/ppermute | solution.py:339
  40.8 8.0 %collective-permute-start.15 = (bf16[80,1024]{1,0:T(8,128)(2,1)S(1)}, bf16[80,1024]{1,0:T(8,128)(2,1)S(1)}, u32[]{:S(2)}, u32[]{:S(2)}) collective-permute-start(bf16[80,1024]{1,0:T(8,128)(2,1)S(1)} %get-tuple-element.55), channel_id=1, source_target_pairs={{0,24},{4,28},{8,16},{12,20},{16,8},{20,12},{24,0},{28,4},{1,25},{... | collective-permute-start | bytes 491528 | tf_op jit(solution)/shard_map/ppermute | solution.py:339
  43.3 10.6 %collective-permute-start.16 = (bf16[80,1024]{1,0:T(8,128)(2,1)S(1)}, bf16[80,1024]{1,0:T(8,128)(2,1)S(1)}, u32[]{:S(2)}, u32[]{:S(2)}) collective-permute-start(bf16[80,1024]{1,0:T(8,128)(2,1)S(1)} %get-tuple-element.54), channel_id=1, source_target_pairs={{0,16},{4,20},{8,24},{12,28},{16,0},{20,4},{24,8},{28,12},{1,17},{... | collective-permute-start | bytes 491528 | tf_op jit(solution)/shard_map/ppermute | solution.py:339
  43.8 10.1 %collective-permute-start.17 = (bf16[80,1024]{1,0:T(8,128)(2,1)S(1)}, bf16[80,1024]{1,0:T(8,128)(2,1)S(1)}, u32[]{:S(2)}, u32[]{:S(2)}) collective-permute-start(bf16[80,1024]{1,0:T(8,128)(2,1)S(1)} %get-tuple-element.53), channel_id=1, source_target_pairs={{0,8},{4,12},{8,0},{12,4},{16,24},{20,28},{24,16},{28,20},{1,9},{5... | collective-permute-start | bytes 491528 | tf_op jit(solution)/shard_map/ppermute | solution.py:339
  44.4 1.5 %copy-start.3 = (bf16[704,1024]{1,0:T(8,128)(2,1)}, bf16[704,1024]{1,0:T(8,128)(2,1)S(1)}, u32[]{:S(2)}) copy-start(bf16[704,1024]{1,0:T(8,128)(2,1)S(1)} %collective-permute-done.18.refs_1_) | copy-start | bytes 4325380
  44.4 6.0 %copy-start.5 = (bf16[256,1024]{1,0:T(8,128)(2,1)S(1)}, bf16[256,1024]{1,0:T(8,128)(2,1)}, u32[]{:S(2)}) copy-start(bf16[256,1024]{1,0:T(8,128)(2,1)} %get-tuple-element.23.gq_ref) | copy-start | bytes 1572868
  45.8 20.2 %collective-permute-start.19 = (bf16[176,1024]{1,0:T(8,128)(2,1)}, bf16[176,1024]{1,0:T(8,128)(2,1)S(1)}, u32[]{:S(2)}, u32[]{:S(2)}) collective-permute-start(bf16[176,1024]{1,0:T(8,128)(2,1)} %get-tuple-element.52), channel_id=1, source_target_pairs={{0,24},{4,28},{8,16},{12,20},{16,8},{20,12},{24,0},{28,4},{1,25},{... | collective-permute-start | bytes 1081352 | tf_op jit(solution)/shard_map/ppermute | solution.py:339
  48.2 19.1 %collective-permute-start.20 = (bf16[176,1024]{1,0:T(8,128)(2,1)}, bf16[176,1024]{1,0:T(8,128)(2,1)}, u32[]{:S(2)}, u32[]{:S(2)}) collective-permute-start(bf16[176,1024]{1,0:T(8,128)(2,1)} %get-tuple-element.51), channel_id=1, source_target_pairs={{0,16},{4,20},{8,24},{12,28},{16,0},{20,4},{24,8},{28,12},{1,17},{... | collective-permute-start | bytes 1081352 | tf_op jit(solution)/shard_map/ppermute | solution.py:339
  48.8 18.6 %collective-permute-start.21 = (bf16[176,1024]{1,0:T(8,128)(2,1)}, bf16[176,1024]{1,0:T(8,128)(2,1)}, u32[]{:S(2)}, u32[]{:S(2)}) collective-permute-start(bf16[176,1024]{1,0:T(8,128)(2,1)} %get-tuple-element.50), channel_id=1, source_target_pairs={{0,8},{4,12},{8,0},{12,4},{16,24},{20,28},{24,16},{28,20},{1,9},{5... | collective-permute-start | bytes 1081352 | tf_op jit(solution)/shard_map/ppermute | solution.py:339
  59.2 17.3 %collective-permute-start.22 = (bf16[80,1152]{1,0:T(8,128)(2,1)}, bf16[80,1152]{1,0:T(8,128)(2,1)S(1)}, u32[]{:S(2)}, u32[]{:S(2)}) collective-permute-start(bf16[80,1152]{1,0:T(8,128)(2,1)} %get-tuple-element.40), channel_id=1, source_target_pairs={{0,1},{3,2},{1,3},{2,0},{4,5},{7,6},{5,7},{6,4},{8,9},{11,10},{9,1... | collective-permute-start | bytes 552968 | tf_op jit(solution)/shard_map/ppermute | solution.py:380
  59.8 6.3 %copy-start.9 = (bf16[80,1152]{1,0:T(8,128)(2,1)S(1)}, bf16[80,1152]{1,0:T(8,128)(2,1)}, u32[]{:S(2)}) copy-start(bf16[80,1152]{1,0:T(8,128)(2,1)} %get-tuple-element.41) | copy-start | bytes 552964
  59.8 7.6 %copy-start.2 = (bf16[704,1024]{1,0:T(8,128)(2,1)S(1)}, bf16[704,1024]{1,0:T(8,128)(2,1)}, u32[]{:S(2)}) copy-start(bf16[704,1024]{1,0:T(8,128)(2,1)} %copy-done.1) | copy-start | bytes 4325380
  59.8 7.6 %copy-start.4 = (bf16[704,1024]{1,0:T(8,128)(2,1)S(1)}, bf16[704,1024]{1,0:T(8,128)(2,1)}, u32[]{:S(2)}) copy-start(bf16[704,1024]{1,0:T(8,128)(2,1)} %copy-done.3) | copy-start | bytes 4325380
  64.3 21.9 %collective-permute-start.24 = (bf16[80,1152]{1,0:T(8,128)(2,1)}, bf16[80,1152]{1,0:T(8,128)(2,1)S(1)}, u32[]{:S(2)}, u32[]{:S(2)}) collective-permute-start(bf16[80,1152]{1,0:T(8,128)(2,1)} %get-tuple-element.42), channel_id=1, source_target_pairs={{0,1},{2,3},{1,0},{3,2},{4,5},{6,7},{5,4},{7,6},{8,9},{10,11},{9,8... | collective-permute-start | bytes 552968 | tf_op jit(solution)/shard_map/ppermute | solution.py:382
  66.1 20.1 %collective-permute-start.23 = (bf16[80,1152]{1,0:T(8,128)(2,1)S(1)}, bf16[80,1152]{1,0:T(8,128)(2,1)S(1)}, u32[]{:S(2)}, u32[]{:S(2)}) collective-permute-start(bf16[80,1152]{1,0:T(8,128)(2,1)S(1)} %copy-done.9), channel_id=1, source_target_pairs={{0,3},{3,0},{4,7},{7,4},{8,11},{11,8},{12,15},{15,12},{16,19},{19,... | collective-permute-start | bytes 552968 | tf_op jit(solution)/shard_map/ppermute | solution.py:381
  73.0 21.5 %collective-permute-start.26 = (bf16[176,1152]{1,0:T(8,128)(2,1)}, bf16[176,1152]{1,0:T(8,128)(2,1)S(1)}, u32[]{:S(2)}, u32[]{:S(2)}) collective-permute-start(bf16[176,1152]{1,0:T(8,128)(2,1)} %get-tuple-element.47), channel_id=1, source_target_pairs={{0,1},{3,2},{1,3},{2,0},{4,5},{7,6},{5,7},{6,4},{8,9},{11,10},{9,1... | collective-permute-start | bytes 1216520 | tf_op jit(solution)/shard_map/ppermute | solution.py:380
  76.5 25.8 %collective-permute-start.25 = (bf16[80,1152]{1,0:T(8,128)(2,1)S(1)}, bf16[80,1152]{1,0:T(8,128)(2,1)S(1)}, u32[]{:S(2)}, u32[]{:S(2)}) collective-permute-start(bf16[80,1152]{1,0:T(8,128)(2,1)S(1)} %fusion.11), channel_id=1, source_target_pairs={{1,2},{2,1},{5,6},{6,5},{9,10},{10,9},{13,14},{14,13},{17,18},{18,... | collective-permute-start | bytes 552968 | tf_op jit(solution)/shard_map/ppermute | solution.py:384
  81.1 5.1 %copy-start.6 = (bf16[176,1152]{1,0:T(8,128)(2,1)S(1)}, bf16[176,1152]{1,0:T(8,128)(2,1)}, u32[]{:S(2)}) copy-start(bf16[176,1152]{1,0:T(8,128)(2,1)} %get-tuple-element.48) | copy-start | bytes 1216516
  81.1 21.2 %copy-start.8 = (bf16[80,1152]{1,0:T(8,128)(2,1)S(1)}, bf16[80,1152]{1,0:T(8,128)(2,1)}, u32[]{:S(2)}) copy-start(bf16[80,1152]{1,0:T(8,128)(2,1)} %get-tuple-element.39) | copy-start | bytes 552964
  86.2 21.6 %copy-start.7 = (bf16[176,1152]{1,0:T(8,128)(2,1)S(1)}, bf16[176,1152]{1,0:T(8,128)(2,1)}, u32[]{:S(2)}) copy-start(bf16[176,1152]{1,0:T(8,128)(2,1)} %get-tuple-element.46) | copy-start | bytes 1216516
  86.2 17.0 %collective-permute-start.27 = (bf16[176,1152]{1,0:T(8,128)(2,1)S(1)}, bf16[176,1152]{1,0:T(8,128)(2,1)S(1)}, u32[]{:S(2)}, u32[]{:S(2)}) collective-permute-start(bf16[176,1152]{1,0:T(8,128)(2,1)S(1)} %copy-done.6), channel_id=1, source_target_pairs={{0,3},{3,0},{4,7},{7,4},{8,11},{11,8},{12,15},{15,12},{16,19},{19,... | collective-permute-start | bytes 1216520 | tf_op jit(solution)/shard_map/ppermute | solution.py:381
  87.0 17.3 %collective-permute-start.28 = (bf16[176,1152]{1,0:T(8,128)(2,1)}, bf16[176,1152]{1,0:T(8,128)(2,1)S(1)}, u32[]{:S(2)}, u32[]{:S(2)}) collective-permute-start(bf16[176,1152]{1,0:T(8,128)(2,1)} %get-tuple-element.49), channel_id=1, source_target_pairs={{0,1},{2,3},{1,0},{3,2},{4,5},{6,7},{5,4},{7,6},{8,9},{10,11},{9,8... | collective-permute-start | bytes 1216520 | tf_op jit(solution)/shard_map/ppermute | solution.py:382
  94.6 13.2 %collective-permute-start.29 = (bf16[176,1152]{1,0:T(8,128)(2,1)S(1)}, bf16[176,1152]{1,0:T(8,128)(2,1)S(1)}, u32[]{:S(2)}, u32[]{:S(2)}) collective-permute-start(bf16[176,1152]{1,0:T(8,128)(2,1)S(1)} %fusion.5), channel_id=1, source_target_pairs={{1,2},{2,1},{5,6},{6,5},{9,10},{10,9},{13,14},{14,13},{17,18},{18,... | collective-permute-start | bytes 1216520 | tf_op jit(solution)/shard_map/ppermute | solution.py:384

commit v4 on v3

--- a/solution.py
+++ b/solution.py
@@ -428,7 +428,7 @@
     grads = []
     after = []
     for cut, arrived in zip(cuts, received):
-        early = shares // 2
+        early = shares // 2 if after else shares - 1
         grad_k, grad_v, *chunks = projection("head", range(early), cut, arrived, term, weights)
         chunks += projection("head", range(early, shares), cut, [grad_k, grad_v], term, weights)
         total, after = line_sum(chunks, "head", after)

time: 109 us -> 108 us (level)
    ppermute x2, starting transfers between devices: 1.81 us -> 7.28 us  [line_sum(): got_third = lax.ppermute(third, axis, [(0, 1), (2, 3), (1, 0), (3, 2)])]
    ppermute x2, starting transfers between devices: 9.55 us -> 5.79 us  [line_sum(): got_passed = lax.ppermute(passed, axis, [(1, 2), (2, 1)])]
    ppermute x2, waiting for transfers between devices: 7.41 us -> 4.34 us  [line_sum(): got_first = lax.ppermute(first, axis, [(0, 1), (3, 2), (1, 3), (2, 0)])]
    ppermute x2, starting transfers between devices: 3.98 us -> 1.49 us  [line_sum(): got_first = lax.ppermute(first, axis, [(0, 1), (3, 2), (1, 3), (2, 0)])]
    ppermute x2, waiting for transfers between devices: 6.17 us -> 8.44 us  [line_sum(): got_passed = lax.ppermute(passed, axis, [(1, 2), (2, 1)])]
    ppermute x2, waiting for transfers between devices: 1.07 us -> 2.28 us  [line_sum(): got_third = lax.ppermute(third, axis, [(0, 1), (2, 3), (1, 0), (3, 2)])]
  transfers between devices with their start and end apart: 30 -> 30, of which waited for: 16 -> 14; matrix products, arithmetic and copies ran while one was open for 2% -> 2% of each run, Pallas kernels for 22% -> 22%
where the time goes in v4:
time: 108 us
  Pallas kernels  38.5 us (36%)
  starting transfers between devices  32.8 us (30%)
  waiting for transfers between devices  31.9 us (30%)
  other arithmetic  3.7 us (3%)
    pallas_call x4, Pallas kernels, projection(): pl.pallas_call(functools.partial(projection_kernel, axis, places, cut, su...  20.4 us
    ppermute x22, waiting for transfers between devices, exchange(): return lax.ppermute(x, axis, [(i, i ^ mask) for i in range(n)])  16.8 us
    ppermute x22, starting transfers between devices, exchange(): return lax.ppermute(x, axis, [(i, i ^ mask) for i in range(n)])  16.6 us
    pallas_call x1, Pallas kernels, attention(): pl.pallas_call(functools.partial(attention_kernel, axis, n_ctx, topk, cut...  14.6 us
    ppermute x2, waiting for transfers between devices, line_sum(): got_passed = lax.ppermute(passed, axis, [(1, 2), (2, 1)])  8.44 us
    ppermute x2, starting transfers between devices, line_sum(): got_third = lax.ppermute(third, axis, [(0, 1), (2, 3), (1, 0), (3, 2)])  7.28 us
    ppermute x2, starting transfers between devices, line_sum(): got_passed = lax.ppermute(passed, axis, [(1, 2), (2, 1)])  5.79 us
    ppermute x2, waiting for transfers between devices, line_sum(): got_first = lax.ppermute(first, axis, [(0, 1), (3, 2), (1, 3), (2, 0)])  4.34 us
  transfers between devices with their start and end apart: 30, of which 14 were waited for; matrix products, arithmetic and copies ran while one was open for 2% of the time, Pallas kernels for 22%

profile of v4, /device:TPU:16, one launch (start us, length us, event | category | flops | bytes accessed | tf_op | source)
XLA Modules:
  0.0 108.1 jit_solution(10820520476917368402)
XLA Ops:
  0.6 1.6 %collective-permute-start.10 = (bf16[256,512]{1,0:T(8,128)(2,1)}, bf16[256,512]{1,0:T(8,128)(2,1)S(1)}, u32[]{:S(2)}, u32[]{:S(2)}) collective-permute-start(bf16[256,512]{1,0:T(8,128)(2,1)} %refs_8_.1), channel_id=1, source_target_pairs={{0,16},{4,20},{8,24},{12,28},{16,0},{20,4},{24,8},{28,12},{1,17},{... | collective-permute-start | bytes 786440 | tf_op jit(solution)/shard_map/ppermute | solution.py:339
  2.2 1.5 %collective-permute-start.1 = (bf16[256,512]{1,0:T(8,128)(2,1)}, bf16[256,512]{1,0:T(8,128)(2,1)S(1)}, u32[]{:S(2)}, u32[]{:S(2)}) collective-permute-start(bf16[256,512]{1,0:T(8,128)(2,1)} %refs_0_.1), channel_id=1, source_target_pairs={{0,8},{4,12},{8,0},{12,4},{16,24},{20,28},{24,16},{28,20},{1,9},{5... | collective-permute-start | bytes 786440 | tf_op jit(solution)/shard_map/ppermute | solution.py:339
  3.7 0.5 collective-permute-start.3
  4.2 0.5 collective-permute-start.8
  4.8 0.0 collective-permute-start
  4.8 5.3 %collective-permute-done.10.refs_12_ = bf16[256,512]{1,0:T(8,128)(2,1)S(1)} collective-permute-done((bf16[256,512]{1,0:T(8,128)(2,1)}, bf16[256,512]{1,0:T(8,128)(2,1)S(1)}, u32[]{:S(2)}, u32[]{:S(2)}) %collective-permute-start.10) | collective-permute-done | bytes 262176 | tf_op jit(solution)/shard_map/ppermute | solution.py:339
  10.1 0.0 collective-permute-start.7
  10.1 1.6 %collective-permute-done.1.refs_2_ = bf16[256,512]{1,0:T(8,128)(2,1)S(1)} collective-permute-done((bf16[256,512]{1,0:T(8,128)(2,1)}, bf16[256,512]{1,0:T(8,128)(2,1)S(1)}, u32[]{:S(2)}, u32[]{:S(2)}) %collective-permute-start.1) | collective-permute-done | bytes 262176 | tf_op jit(solution)/shard_map/ppermute | solution.py:339
  11.7 1.5 %collective-permute-start.12 = (bf16[256,512]{1,0:T(8,128)(2,1)S(1)}, bf16[256,512]{1,0:T(8,128)(2,1)S(1)}, u32[]{:S(2)}, u32[]{:S(2)}) collective-permute-start(bf16[256,512]{1,0:T(8,128)(2,1)S(1)} %collective-permute-done.10.refs_12_), channel_id=1, source_target_pairs={{0,8},{4,12},{8,0},{12,4},{16,24},{20,28},{24,16},{28,20},{1,9},{5... | collective-permute-start | bytes 786440 | tf_op jit(solution)/shard_map/ppermute | solution.py:339
  13.2 1.4 %collective-permute-done.3.refs_4_ = bf16[256,512]{1,0:T(8,128)(2,1)S(1)} collective-permute-done((bf16[256,512]{1,0:T(8,128)(2,1)}, bf16[256,512]{1,0:T(8,128)(2,1)S(1)}, u32[]{:S(2)}, u32[]{:S(2)}) %collective-permute-start.3) | collective-permute-done | bytes 262176 | tf_op jit(solution)/shard_map/ppermute | solution.py:339
  14.6 1.5 %collective-permute-start.5 = (bf16[256,512]{1,0:T(8,128)(2,1)S(1)}, bf16[256,512]{1,0:T(8,128)(2,1)S(1)}, u32[]{:S(2)}, u32[]{:S(2)}) collective-permute-start(bf16[256,512]{1,0:T(8,128)(2,1)S(1)} %collective-permute-done.1.refs_2_), channel_id=1, source_target_pairs={{0,16},{4,20},{8,24},{12,28},{16,0},{20,4},{24,8},{28,12},{1,17},{... | collective-permute-start | bytes 786440 | tf_op jit(solution)/shard_map/ppermute | solution.py:339
  16.1 1.2 %collective-permute-done.8.refs_10_ = bf16[256,512]{1,0:T(8,128)(2,1)S(1)} collective-permute-done((bf16[256,512]{1,0:T(8,128)(2,1)}, bf16[256,512]{1,0:T(8,128)(2,1)S(1)}, u32[]{:S(2)}, u32[]{:S(2)}) %collective-permute-start.8) | collective-permute-done | bytes 262176 | tf_op jit(solution)/shard_map/ppermute | solution.py:339
  17.3 0.5 collective-permute-start.2
  17.8 0.1 collective-permute-start.4
  17.9 3.6 %collective-permute-done.12.refs_14_ = bf16[256,512]{1,0:T(8,128)(2,1)S(1)} collective-permute-done((bf16[256,512]{1,0:T(8,128)(2,1)S(1)}, bf16[256,512]{1,0:T(8,128)(2,1)S(1)}, u32[]{:S(2)}, u32[]{:S(2)}) %collective-permute-start.12) | collective-permute-done | bytes 262176 | tf_op jit(solution)/shard_map/ppermute | solution.py:339
  21.4 0.0 collective-permute-start.9
  21.4 0.3 collective-permute-done.5.refs_6_
  21.7 0.2 collective-permute-start.13
  21.9 0.0 collective-permute-done.11.refs_13_
  21.9 0.3 collective-permute-start.6
  22.3 0.7 collective-permute-done.9.refs_11_
  23.0 0.4 collective-permute-done.13.refs_15_
  23.3 0.4 collective-permute-done.6.refs_7_
  23.7 14.6 %attention.1 = (bf16[256,1024]{1,0:T(8,128)(2,1)}, bf16[320,1024]{1,0:T(8,128)(2,1)S(1)}, bf16[320,1024]{1,0:T(8,128)(2,1)S(1)}, bf16[704,1024]{1,0:T(8,128)(2,1)S(1)}, bf16[704,1024]{1,0:T(8,128)(2,1)S(1)}) custom-call(s32[4,4,16]{2,1,0:T(4,128)} %chosen_hbm.1, bf16[256,512]{1,0:T(8,128)(2,1)} %refs_0_.1, ...), custom_call_target="tpu_custom_call" | custom-call | flops 2684354560 | bytes 33554432 | tf_op jit(solution)/shard_map/attention/pallas_call | solution.py:193
  38.3 0.2 collective-permute-start.14
  38.5 2.0 %collective-permute-done.14.refs_1_ = bf16[320,1024]{1,0:T(8,128)(2,1)S(1)} collective-permute-done((bf16[320,1024]{1,0:T(8,128)(2,1)S(1)}, bf16[320,1024]{1,0:T(8,128)(2,1)S(1)}, u32[]{:S(2)}, u32[]{:S(2)}) %collective-permute-start.14) | collective-permute-done | bytes 655392 | tf_op jit(solution)/shard_map/ppermute | solution.py:339
  40.5 0.1 collective-permute-start.18
  40.6 0.2 add_convert_fusion.3
  40.8 2.5 %collective-permute-start.15 = (bf16[80,1024]{1,0:T(8,128)(2,1)S(1)}, bf16[80,1024]{1,0:T(8,128)(2,1)S(1)}, u32[]{:S(2)}, u32[]{:S(2)}) collective-permute-start(bf16[80,1024]{1,0:T(8,128)(2,1)S(1)} %get-tuple-element.53), channel_id=1, source_target_pairs={{0,24},{4,28},{8,16},{12,20},{16,8},{20,12},{24,0},{28,4},{1,25},{... | collective-permute-start | bytes 491528 | tf_op jit(solution)/shard_map/ppermute | solution.py:339
  43.3 0.5 collective-permute-start.16
  43.8 0.5 collective-permute-start.17
  44.4 0.0 collective-permute-done.18.refs_1_
  44.4 1.3 %add_convert_fusion = (bf16[176,1024]{1,0:T(8,128)(2,1)}, bf16[176,1024]{1,0:T(8,128)(2,1)}, bf16[176,1024]{1,0:T(8,128)(2,1)}) fusion(bf16[704,1024]{1,0:T(8,128)(2,1)S(1)} %collective-permute-done.18.refs_1_, bf16[704,1024]{1,0:T(8,128)(2,1)S(1)} %get-tuple-element.33.refs_0_), kind=kLoop, calls=%fused_computation.8 | loop fusion | flops 2162688 | bytes 3244032 | tf_op jit(solution)/shard_map/convert_element_type | solution.py:362
  45.6 0.2 copy-done.3
  45.8 2.4 %collective-permute-start.19 = (bf16[176,1024]{1,0:T(8,128)(2,1)}, bf16[176,1024]{1,0:T(8,128)(2,1)S(1)}, u32[]{:S(2)}, u32[]{:S(2)}) collective-permute-start(bf16[176,1024]{1,0:T(8,128)(2,1)} %get-tuple-element.50), channel_id=1, source_target_pairs={{0,24},{4,28},{8,16},{12,20},{16,8},{20,12},{24,0},{28,4},{1,25},{... | collective-permute-start | bytes 1081352 | tf_op jit(solution)/shard_map/ppermute | solution.py:339
  48.2 0.5 collective-permute-start.20
  48.8 0.0 collective-permute-done.15.refs_2_
  48.8 1.5 %collective-permute-start.21 = (bf16[176,1024]{1,0:T(8,128)(2,1)}, bf16[176,1024]{1,0:T(8,128)(2,1)}, u32[]{:S(2)}, u32[]{:S(2)}) collective-permute-start(bf16[176,1024]{1,0:T(8,128)(2,1)} %get-tuple-element.48), channel_id=1, source_target_pairs={{0,8},{4,12},{8,0},{12,4},{16,24},{20,28},{24,16},{28,20},{1,9},{5... | collective-permute-start | bytes 1081352 | tf_op jit(solution)/shard_map/ppermute | solution.py:339
  50.3 3.5 %query_term.1.refs_5_.refs_2_ = bf16[4,256,1152]{2,1,0:T(8,128)(2,1)S(1)} custom-call(bf16[256,1024]{1,0:T(8,128)(2,1)S(1)} %copy-done.5, bf16[4608,1024]{1,0:T(8,128)(2,1)S(1)} %copy-done), custom_call_target="tpu_custom_call" | custom-call | flops 2415919104 | bytes 9437184 | tf_op jit(solution)/shard_map/query_term/pallas_call | solution.py:230
  53.9 0.0 collective-permute-done.16.refs_3_
  53.9 0.0 collective-permute-done.17.refs_4_
  53.9 6.2 %projection.4 = (bf16[80,512]{1,0:T(8,128)(2,1)S(1)}, bf16[80,512]{1,0:T(8,128)(2,1)S(1)}, bf16[80,1152]{1,0:T(8,128)(2,1)}, bf16[80,1152]{1,0:T(8,128)(2,1)}, bf16[80,1152]{1,0:T(8,128)(2,1)}) custom-call(bf16[320,1024]{1,0:T(8,128)(2,1)S(1)} %get-tuple-element.27.refs_0_, bf16[320,1024]{1,0:T(8,128)(2,1)S(1)} %collective-permute-done.14.refs_1_, ...), custom_call_target="tpu_custom_call" | custom-call | flops 566231040 | bytes 7077888 | tf_op jit(solution)/shard_map/projection/pallas_call | solution.py:312
  60.1 0.4 collective-permute-start.22
  60.5 0.8 collective-permute-start.23
  61.3 3.5 %projection.6 = bf16[80,1152]{1,0:T(8,128)(2,1)} custom-call(bf16[80,512]{1,0:T(8,128)(2,1)S(1)} %get-tuple-element.29.refs_0_, bf16[80,512]{1,0:T(8,128)(2,1)S(1)} %get-tuple-element.36.refs_1_, bf16[4,256,1152]{2,1,0:T(8,128)(2,1)S(1)} %query_term.1.refs_5_.refs_2_, bf16[4608,512]{1,0:T(8,128)(2,1)} %refs_3_.3, bf16[4608,512]{1,0:T(8,128)(2,1)} %refs_4_.3), custom_call_target="tpu_custom_call" | custom-call | flops 188743680 | bytes 2359296 | tf_op jit(solution)/shard_map/projection/pallas_call | solution.py:312
  64.9 0.0 collective-permute-done.19.refs_2_
  64.9 0.0 copy-start.9
  64.9 4.3 %collective-permute-start.24 = (bf16[80,1152]{1,0:T(8,128)(2,1)S(1)}, bf16[80,1152]{1,0:T(8,128)(2,1)S(1)}, u32[]{:S(2)}, u32[]{:S(2)}) collective-permute-start(bf16[80,1152]{1,0:T(8,128)(2,1)S(1)} %copy-done.10), channel_id=1, source_target_pairs={{0,1},{2,3},{1,0},{3,2},{4,5},{6,7},{5,4},{7,6},{8,9},{10,11},{9,8... | collective-permute-start | bytes 552968 | tf_op jit(solution)/shard_map/ppermute | solution.py:382
  69.3 5.7 %projection.5 = (bf16[176,512]{1,0:T(8,128)(2,1)S(1)}, bf16[176,512]{1,0:T(8,128)(2,1)S(1)}, bf16[176,1152]{1,0:T(8,128)(2,1)}, bf16[176,1152]{1,0:T(8,128)(2,1)}) custom-call(bf16[704,1024]{1,0:T(8,128)(2,1)S(1)} %copy-done.2, bf16[704,1024]{1,0:T(8,128)(2,1)S(1)} %copy-done.4, bf16[176,1024]{1,0:T(8,128)(2,1)S(1)} %collective-permute-done.19.refs_2_, ...), custom_call_target="tpu_custom_call" | custom-call | flops 830472192 | bytes 4718592 | tf_op jit(solution)/shard_map/projection/pallas_call | solution.py:312
  75.0 1.1 %collective-permute-start.26 = (bf16[176,1152]{1,0:T(8,128)(2,1)}, bf16[176,1152]{1,0:T(8,128)(2,1)S(1)}, u32[]{:S(2)}, u32[]{:S(2)}) collective-permute-start(bf16[176,1152]{1,0:T(8,128)(2,1)} %get-tuple-element.45), channel_id=1, source_target_pairs={{0,1},{3,2},{1,3},{2,0},{4,5},{7,6},{5,7},{6,4},{8,9},{11,10},{9,1... | collective-permute-start | bytes 1216520 | tf_op jit(solution)/shard_map/ppermute | solution.py:380
  76.1 2.5 %collective-permute-start.25 = (bf16[80,1152]{1,0:T(8,128)(2,1)S(1)}, bf16[80,1152]{1,0:T(8,128)(2,1)S(1)}, u32[]{:S(2)}, u32[]{:S(2)}) collective-permute-start(bf16[80,1152]{1,0:T(8,128)(2,1)S(1)} %fusion.11), channel_id=1, source_target_pairs={{1,2},{2,1},{5,6},{6,5},{9,10},{10,9},{13,14},{14,13},{17,18},{18,... | collective-permute-start | bytes 552968 | tf_op jit(solution)/shard_map/ppermute | solution.py:384
  78.6 5.0 %projection.7 = (bf16[176,1152]{1,0:T(8,128)(2,1)}, bf16[176,1152]{1,0:T(8,128)(2,1)}) custom-call(bf16[176,512]{1,0:T(8,128)(2,1)S(1)} %get-tuple-element.35.refs_0_, bf16[176,512]{1,0:T(8,128)(2,1)S(1)} %get-tuple-element.37.refs_1_, bf16[4,256,1152]{2,1,0:T(8,128)(2,1)S(1)} %query_term.1.refs_5_.refs_2_, bf16[4608,512]{1,0:T(8,128)(2,1)} %refs_3_.3, ...), custom_call_target="tpu_custom_call" | custom-call | flops 830472192 | bytes 4718592 | tf_op jit(solution)/shard_map/projection/pallas_call | solution.py:312
  83.7 0.8 collective-permute-start.27
  84.5 2.9 %collective-permute-start.28 = (bf16[176,1152]{1,0:T(8,128)(2,1)}, bf16[176,1152]{1,0:T(8,128)(2,1)S(1)}, u32[]{:S(2)}, u32[]{:S(2)}) collective-permute-start(bf16[176,1152]{1,0:T(8,128)(2,1)} %get-tuple-element.47), channel_id=1, source_target_pairs={{0,1},{2,3},{1,0},{3,2},{4,5},{6,7},{5,4},{7,6},{8,9},{10,11},{9,8... | collective-permute-start | bytes 1216520 | tf_op jit(solution)/shard_map/ppermute | solution.py:382
  87.5 4.3 %collective-permute-done.26 = bf16[176,1152]{1,0:T(8,128)(2,1)S(1)} collective-permute-done((bf16[176,1152]{1,0:T(8,128)(2,1)}, bf16[176,1152]{1,0:T(8,128)(2,1)S(1)}, u32[]{:S(2)}, u32[]{:S(2)}) %collective-permute-start.26) | collective-permute-done | bytes 405536 | tf_op jit(solution)/shard_map/ppermute | solution.py:380
  91.8 0.1 fusion.5
  91.9 3.3 %collective-permute-start.29 = (bf16[176,1152]{1,0:T(8,128)(2,1)S(1)}, bf16[176,1152]{1,0:T(8,128)(2,1)S(1)}, u32[]{:S(2)}, u32[]{:S(2)}) collective-permute-start(bf16[176,1152]{1,0:T(8,128)(2,1)S(1)} %fusion.5), channel_id=1, source_target_pairs={{1,2},{2,1},{5,6},{6,5},{9,10},{10,9},{13,14},{14,13},{17,18},{18,... | collective-permute-start | bytes 1216520 | tf_op jit(solution)/shard_map/ppermute | solution.py:384
  95.2 4.5 %collective-permute-done.25 = bf16[80,1152]{1,0:T(8,128)(2,1)S(1)} collective-permute-done((bf16[80,1152]{1,0:T(8,128)(2,1)S(1)}, bf16[80,1152]{1,0:T(8,128)(2,1)S(1)}, u32[]{:S(2)}, u32[]{:S(2)}) %collective-permute-start.25) | collective-permute-done | bytes 184352 | tf_op jit(solution)/shard_map/ppermute | solution.py:384
  99.8 0.1 fusion.10
  99.9 0.8 pad_maximum_fusion.1
  100.7 2.3 %collective-permute-done.28 = bf16[176,1152]{1,0:T(8,128)(2,1)S(1)} collective-permute-done((bf16[176,1152]{1,0:T(8,128)(2,1)}, bf16[176,1152]{1,0:T(8,128)(2,1)S(1)}, u32[]{:S(2)}, u32[]{:S(2)}) %collective-permute-start.28) | collective-permute-done | bytes 405536 | tf_op jit(solution)/shard_map/ppermute | solution.py:382
  103.0 3.9 %collective-permute-done.29 = bf16[176,1152]{1,0:T(8,128)(2,1)S(1)} collective-permute-done((bf16[176,1152]{1,0:T(8,128)(2,1)S(1)}, bf16[176,1152]{1,0:T(8,128)(2,1)S(1)}, u32[]{:S(2)}, u32[]{:S(2)}) %collective-permute-start.29) | collective-permute-done | bytes 405536 | tf_op jit(solution)/shard_map/ppermute | solution.py:384
  106.9 0.3 fusion.4
  107.2 0.9 pad_maximum_fusion
  (32 shorter events, 0.1 us)
Async XLA Ops:
  0.6 9.5 %collective-permute-start.10 = (bf16[256,512]{1,0:T(8,128)(2,1)}, bf16[256,512]{1,0:T(8,128)(2,1)S(1)}, u32[]{:S(2)}, u32[]{:S(2)}) collective-permute-start(bf16[256,512]{1,0:T(8,128)(2,1)} %refs_8_.1), channel_id=1, source_target_pairs={{0,16},{4,20},{8,24},{12,28},{16,0},{20,4},{24,8},{28,12},{1,17},{... | collective-permute-start | bytes 786440 | tf_op jit(solution)/shard_map/ppermute | solution.py:339
  2.2 9.4 %collective-permute-start.1 = (bf16[256,512]{1,0:T(8,128)(2,1)}, bf16[256,512]{1,0:T(8,128)(2,1)S(1)}, u32[]{:S(2)}, u32[]{:S(2)}) collective-permute-start(bf16[256,512]{1,0:T(8,128)(2,1)} %refs_0_.1), channel_id=1, source_target_pairs={{0,8},{4,12},{8,0},{12,4},{16,24},{20,28},{24,16},{28,20},{1,9},{5... | collective-permute-start | bytes 786440 | tf_op jit(solution)/shard_map/ppermute | solution.py:339
  3.7 10.9 %collective-permute-start.3 = (bf16[256,512]{1,0:T(8,128)(2,1)}, bf16[256,512]{1,0:T(8,128)(2,1)S(1)}, u32[]{:S(2)}, u32[]{:S(2)}) collective-permute-start(bf16[256,512]{1,0:T(8,128)(2,1)} %refs_0_.1), channel_id=1, source_target_pairs={{0,16},{4,20},{8,24},{12,28},{16,0},{20,4},{24,8},{28,12},{1,17},{... | collective-permute-start | bytes 786440 | tf_op jit(solution)/shard_map/ppermute | solution.py:339
  4.2 13.1 %collective-permute-start.8 = (bf16[256,512]{1,0:T(8,128)(2,1)}, bf16[256,512]{1,0:T(8,128)(2,1)S(1)}, u32[]{:S(2)}, u32[]{:S(2)}) collective-permute-start(bf16[256,512]{1,0:T(8,128)(2,1)} %refs_8_.1), channel_id=1, source_target_pairs={{0,8},{4,12},{8,0},{12,4},{16,24},{20,28},{24,16},{28,20},{1,9},{5... | collective-permute-start | bytes 786440 | tf_op jit(solution)/shard_map/ppermute | solution.py:339
  4.8 12.5 %collective-permute-start = (bf16[256,512]{1,0:T(8,128)(2,1)}, bf16[256,512]{1,0:T(8,128)(2,1)S(1)}, u32[]{:S(2)}, u32[]{:S(2)}) collective-permute-start(bf16[256,512]{1,0:T(8,128)(2,1)} %refs_0_.1), channel_id=1, source_target_pairs={{0,4},{4,0},{8,12},{12,8},{16,20},{20,16},{24,28},{28,24},{1,5},{5... | collective-permute-start | bytes 786440 | tf_op jit(solution)/shard_map/ppermute | solution.py:339
  10.1 7.7 %collective-permute-start.7 = (bf16[256,512]{1,0:T(8,128)(2,1)}, bf16[256,512]{1,0:T(8,128)(2,1)S(1)}, u32[]{:S(2)}, u32[]{:S(2)}) collective-permute-start(bf16[256,512]{1,0:T(8,128)(2,1)} %refs_8_.1), channel_id=1, source_target_pairs={{0,4},{4,0},{8,12},{12,8},{16,20},{20,16},{24,28},{28,24},{1,5},{5... | collective-permute-start | bytes 786440 | tf_op jit(solution)/shard_map/ppermute | solution.py:339
  11.7 9.8 %collective-permute-start.12 = (bf16[256,512]{1,0:T(8,128)(2,1)S(1)}, bf16[256,512]{1,0:T(8,128)(2,1)S(1)}, u32[]{:S(2)}, u32[]{:S(2)}) collective-permute-start(bf16[256,512]{1,0:T(8,128)(2,1)S(1)} %collective-permute-done.10.refs_12_), channel_id=1, source_target_pairs={{0,8},{4,12},{8,0},{12,4},{16,24},{20,28},{24,16},{28,20},{1,9},{5... | collective-permute-start | bytes 786440 | tf_op jit(solution)/shard_map/ppermute | solution.py:339
  14.6 7.2 %collective-permute-start.5 = (bf16[256,512]{1,0:T(8,128)(2,1)S(1)}, bf16[256,512]{1,0:T(8,128)(2,1)S(1)}, u32[]{:S(2)}, u32[]{:S(2)}) collective-permute-start(bf16[256,512]{1,0:T(8,128)(2,1)S(1)} %collective-permute-done.1.refs_2_), channel_id=1, source_target_pairs={{0,16},{4,20},{8,24},{12,28},{16,0},{20,4},{24,8},{28,12},{1,17},{... | collective-permute-start | bytes 786440 | tf_op jit(solution)/shard_map/ppermute | solution.py:339
  17.3 4.7 %collective-permute-start.11 = (bf16[256,512]{1,0:T(8,128)(2,1)S(1)}, bf16[256,512]{1,0:T(8,128)(2,1)S(1)}, u32[]{:S(2)}, u32[]{:S(2)}) collective-permute-start(bf16[256,512]{1,0:T(8,128)(2,1)S(1)} %collective-permute-done.10.refs_12_), channel_id=1, source_target_pairs={{0,4},{4,0},{8,12},{12,8},{16,20},{20,16},{24,28},{28,24},{1,5},{5... | collective-permute-start | bytes 786440 | tf_op jit(solution)/shard_map/ppermute | solution.py:339
  17.3 5.0 %collective-permute-start.2 = (bf16[256,512]{1,0:T(8,128)(2,1)S(1)}, bf16[256,512]{1,0:T(8,128)(2,1)S(1)}, u32[]{:S(2)}, u32[]{:S(2)}) collective-permute-start(bf16[256,512]{1,0:T(8,128)(2,1)S(1)} %collective-permute-done.1.refs_2_), channel_id=1, source_target_pairs={{0,4},{4,0},{8,12},{12,8},{16,20},{20,16},{24,28},{28,24},{1,5},{5... | collective-permute-start | bytes 786440 | tf_op jit(solution)/shard_map/ppermute | solution.py:339
  17.8 4.5 %collective-permute-start.4 = (bf16[256,512]{1,0:T(8,128)(2,1)S(1)}, bf16[256,512]{1,0:T(8,128)(2,1)S(1)}, u32[]{:S(2)}, u32[]{:S(2)}) collective-permute-start(bf16[256,512]{1,0:T(8,128)(2,1)S(1)} %collective-permute-done.3.refs_4_), channel_id=1, source_target_pairs={{0,4},{4,0},{8,12},{12,8},{16,20},{20,16},{24,28},{28,24},{1,5},{5... | collective-permute-start | bytes 786440 | tf_op jit(solution)/shard_map/ppermute | solution.py:339
  21.4 1.5 %collective-permute-start.9 = (bf16[256,512]{1,0:T(8,128)(2,1)S(1)}, bf16[256,512]{1,0:T(8,128)(2,1)S(1)}, u32[]{:S(2)}, u32[]{:S(2)}) collective-permute-start(bf16[256,512]{1,0:T(8,128)(2,1)S(1)} %collective-permute-done.8.refs_10_), channel_id=1, source_target_pairs={{0,4},{4,0},{8,12},{12,8},{16,20},{20,16},{24,28},{28,24},{1,5},{5... | collective-permute-start | bytes 786440 | tf_op jit(solution)/shard_map/ppermute | solution.py:339
  21.7 1.6 %collective-permute-start.13 = (bf16[256,512]{1,0:T(8,128)(2,1)S(1)}, bf16[256,512]{1,0:T(8,128)(2,1)S(1)}, u32[]{:S(2)}, u32[]{:S(2)}) collective-permute-start(bf16[256,512]{1,0:T(8,128)(2,1)S(1)} %collective-permute-done.12.refs_14_), channel_id=1, source_target_pairs={{0,4},{4,0},{8,12},{12,8},{16,20},{20,16},{24,28},{28,24},{1,5},{5... | collective-permute-start | bytes 786440 | tf_op jit(solution)/shard_map/ppermute | solution.py:339
  21.9 1.8 %collective-permute-start.6 = (bf16[256,512]{1,0:T(8,128)(2,1)S(1)}, bf16[256,512]{1,0:T(8,128)(2,1)S(1)}, u32[]{:S(2)}, u32[]{:S(2)}) collective-permute-start(bf16[256,512]{1,0:T(8,128)(2,1)S(1)} %collective-permute-done.5.refs_6_), channel_id=1, source_target_pairs={{0,4},{4,0},{8,12},{12,8},{16,20},{20,16},{24,28},{28,24},{1,5},{5... | collective-permute-start | bytes 786440 | tf_op jit(solution)/shard_map/ppermute | solution.py:339
  23.7 26.6 %copy-start = (bf16[4608,1024]{1,0:T(8,128)(2,1)S(1)}, bf16[4608,1024]{1,0:T(8,128)(2,1)}, u32[]{:S(2)}) copy-start(bf16[4608,1024]{1,0:T(8,128)(2,1)} %w_ref.1) | copy-start | bytes 28311556
  38.3 7.3 %copy-start.1 = (bf16[704,1024]{1,0:T(8,128)(2,1)}, bf16[704,1024]{1,0:T(8,128)(2,1)S(1)}, u32[]{:S(2)}) copy-start(bf16[704,1024]{1,0:T(8,128)(2,1)S(1)} %get-tuple-element.33.refs_0_) | copy-start | bytes 4325380
  38.3 2.2 %collective-permute-start.14 = (bf16[320,1024]{1,0:T(8,128)(2,1)S(1)}, bf16[320,1024]{1,0:T(8,128)(2,1)S(1)}, u32[]{:S(2)}, u32[]{:S(2)}) collective-permute-start(bf16[320,1024]{1,0:T(8,128)(2,1)S(1)} %get-tuple-element.28), channel_id=1, source_target_pairs={{0,4},{4,0},{8,12},{12,8},{16,20},{20,16},{24,28},{28,24},{1,5},{5... | collective-permute-start | bytes 1966088 | tf_op jit(solution)/shard_map/ppermute | solution.py:339
  40.5 3.9 %collective-permute-start.18 = (bf16[704,1024]{1,0:T(8,128)(2,1)S(1)}, bf16[704,1024]{1,0:T(8,128)(2,1)S(1)}, u32[]{:S(2)}, u32[]{:S(2)}) collective-permute-start(bf16[704,1024]{1,0:T(8,128)(2,1)S(1)} %get-tuple-element.32), channel_id=1, source_target_pairs={{0,4},{4,0},{8,12},{12,8},{16,20},{20,16},{24,28},{28,24},{1,5},{5... | collective-permute-start | bytes 4325384 | tf_op jit(solution)/shard_map/ppermute | solution.py:339
  40.8 8.0 %collective-permute-start.15 = (bf16[80,1024]{1,0:T(8,128)(2,1)S(1)}, bf16[80,1024]{1,0:T(8,128)(2,1)S(1)}, u32[]{:S(2)}, u32[]{:S(2)}) collective-permute-start(bf16[80,1024]{1,0:T(8,128)(2,1)S(1)} %get-tuple-element.53), channel_id=1, source_target_pairs={{0,24},{4,28},{8,16},{12,20},{16,8},{20,12},{24,0},{28,4},{1,25},{... | collective-permute-start | bytes 491528 | tf_op jit(solution)/shard_map/ppermute | solution.py:339
  43.3 10.6 %collective-permute-start.16 = (bf16[80,1024]{1,0:T(8,128)(2,1)S(1)}, bf16[80,1024]{1,0:T(8,128)(2,1)S(1)}, u32[]{:S(2)}, u32[]{:S(2)}) collective-permute-start(bf16[80,1024]{1,0:T(8,128)(2,1)S(1)} %get-tuple-element.52), channel_id=1, source_target_pairs={{0,16},{4,20},{8,24},{12,28},{16,0},{20,4},{24,8},{28,12},{1,17},{... | collective-permute-start | bytes 491528 | tf_op jit(solution)/shard_map/ppermute | solution.py:339
  43.8 10.1 %collective-permute-start.17 = (bf16[80,1024]{1,0:T(8,128)(2,1)S(1)}, bf16[80,1024]{1,0:T(8,128)(2,1)S(1)}, u32[]{:S(2)}, u32[]{:S(2)}) collective-permute-start(bf16[80,1024]{1,0:T(8,128)(2,1)S(1)} %get-tuple-element.51), channel_id=1, source_target_pairs={{0,8},{4,12},{8,0},{12,4},{16,24},{20,28},{24,16},{28,20},{1,9},{5... | collective-permute-start | bytes 491528 | tf_op jit(solution)/shard_map/ppermute | solution.py:339
  44.4 1.5 %copy-start.3 = (bf16[704,1024]{1,0:T(8,128)(2,1)}, bf16[704,1024]{1,0:T(8,128)(2,1)S(1)}, u32[]{:S(2)}) copy-start(bf16[704,1024]{1,0:T(8,128)(2,1)S(1)} %collective-permute-done.18.refs_1_) | copy-start | bytes 4325380
  44.4 6.0 %copy-start.5 = (bf16[256,1024]{1,0:T(8,128)(2,1)S(1)}, bf16[256,1024]{1,0:T(8,128)(2,1)}, u32[]{:S(2)}) copy-start(bf16[256,1024]{1,0:T(8,128)(2,1)} %get-tuple-element.22.gq_ref) | copy-start | bytes 1572868
  45.8 19.1 %collective-permute-start.19 = (bf16[176,1024]{1,0:T(8,128)(2,1)}, bf16[176,1024]{1,0:T(8,128)(2,1)S(1)}, u32[]{:S(2)}, u32[]{:S(2)}) collective-permute-start(bf16[176,1024]{1,0:T(8,128)(2,1)} %get-tuple-element.50), channel_id=1, source_target_pairs={{0,24},{4,28},{8,16},{12,20},{16,8},{20,12},{24,0},{28,4},{1,25},{... | collective-permute-start | bytes 1081352 | tf_op jit(solution)/shard_map/ppermute | solution.py:339
  48.2 21.0 %collective-permute-start.20 = (bf16[176,1024]{1,0:T(8,128)(2,1)}, bf16[176,1024]{1,0:T(8,128)(2,1)}, u32[]{:S(2)}, u32[]{:S(2)}) collective-permute-start(bf16[176,1024]{1,0:T(8,128)(2,1)} %get-tuple-element.49), channel_id=1, source_target_pairs={{0,16},{4,20},{8,24},{12,28},{16,0},{20,4},{24,8},{28,12},{1,17},{... | collective-permute-start | bytes 1081352 | tf_op jit(solution)/shard_map/ppermute | solution.py:339
  48.8 20.5 %collective-permute-start.21 = (bf16[176,1024]{1,0:T(8,128)(2,1)}, bf16[176,1024]{1,0:T(8,128)(2,1)}, u32[]{:S(2)}, u32[]{:S(2)}) collective-permute-start(bf16[176,1024]{1,0:T(8,128)(2,1)} %get-tuple-element.48), channel_id=1, source_target_pairs={{0,8},{4,12},{8,0},{12,4},{16,24},{20,28},{24,16},{28,20},{1,9},{5... | collective-permute-start | bytes 1081352 | tf_op jit(solution)/shard_map/ppermute | solution.py:339
  60.1 16.0 %collective-permute-start.22 = (bf16[80,1152]{1,0:T(8,128)(2,1)}, bf16[80,1152]{1,0:T(8,128)(2,1)S(1)}, u32[]{:S(2)}, u32[]{:S(2)}) collective-permute-start(bf16[80,1152]{1,0:T(8,128)(2,1)} %get-tuple-element.38), channel_id=1, source_target_pairs={{0,1},{3,2},{1,3},{2,0},{4,5},{7,6},{5,7},{6,4},{8,9},{11,10},{9,1... | collective-permute-start | bytes 552968 | tf_op jit(solution)/shard_map/ppermute | solution.py:380
  60.5 23.2 %collective-permute-start.23 = (bf16[80,1152]{1,0:T(8,128)(2,1)}, bf16[80,1152]{1,0:T(8,128)(2,1)S(1)}, u32[]{:S(2)}, u32[]{:S(2)}) collective-permute-start(bf16[80,1152]{1,0:T(8,128)(2,1)} %get-tuple-element.39), channel_id=1, source_target_pairs={{0,3},{3,0},{4,7},{7,4},{8,11},{11,8},{12,15},{15,12},{16,19},{19,... | collective-permute-start | bytes 552968 | tf_op jit(solution)/shard_map/ppermute | solution.py:381
  61.3 3.6 %copy-start.10 = (bf16[80,1152]{1,0:T(8,128)(2,1)S(1)}, bf16[80,1152]{1,0:T(8,128)(2,1)}, u32[]{:S(2)}) copy-start(bf16[80,1152]{1,0:T(8,128)(2,1)} %get-tuple-element.40) | copy-start | bytes 552964
  61.3 8.0 %copy-start.2 = (bf16[704,1024]{1,0:T(8,128)(2,1)S(1)}, bf16[704,1024]{1,0:T(8,128)(2,1)}, u32[]{:S(2)}) copy-start(bf16[704,1024]{1,0:T(8,128)(2,1)} %copy-done.1) | copy-start | bytes 4325380
  61.3 8.0 %copy-start.4 = (bf16[704,1024]{1,0:T(8,128)(2,1)S(1)}, bf16[704,1024]{1,0:T(8,128)(2,1)}, u32[]{:S(2)}) copy-start(bf16[704,1024]{1,0:T(8,128)(2,1)} %copy-done.3) | copy-start | bytes 4325380
  64.9 11.1 %copy-start.9 = (bf16[80,1152]{1,0:T(8,128)(2,1)S(1)}, bf16[80,1152]{1,0:T(8,128)(2,1)}, u32[]{:S(2)}) copy-start(bf16[80,1152]{1,0:T(8,128)(2,1)} %get-tuple-element.39) | copy-start | bytes 552964
  64.9 18.8 %collective-permute-start.24 = (bf16[80,1152]{1,0:T(8,128)(2,1)S(1)}, bf16[80,1152]{1,0:T(8,128)(2,1)S(1)}, u32[]{:S(2)}, u32[]{:S(2)}) collective-permute-start(bf16[80,1152]{1,0:T(8,128)(2,1)S(1)} %copy-done.10), channel_id=1, source_target_pairs={{0,1},{2,3},{1,0},{3,2},{4,5},{6,7},{5,4},{7,6},{8,9},{10,11},{9,8... | collective-permute-start | bytes 552968 | tf_op jit(solution)/shard_map/ppermute | solution.py:382
  75.0 16.8 %collective-permute-start.26 = (bf16[176,1152]{1,0:T(8,128)(2,1)}, bf16[176,1152]{1,0:T(8,128)(2,1)S(1)}, u32[]{:S(2)}, u32[]{:S(2)}) collective-permute-start(bf16[176,1152]{1,0:T(8,128)(2,1)} %get-tuple-element.45), channel_id=1, source_target_pairs={{0,1},{3,2},{1,3},{2,0},{4,5},{7,6},{5,7},{6,4},{8,9},{11,10},{9,1... | collective-permute-start | bytes 1216520 | tf_op jit(solution)/shard_map/ppermute | solution.py:380
  76.1 23.7 %collective-permute-start.25 = (bf16[80,1152]{1,0:T(8,128)(2,1)S(1)}, bf16[80,1152]{1,0:T(8,128)(2,1)S(1)}, u32[]{:S(2)}, u32[]{:S(2)}) collective-permute-start(bf16[80,1152]{1,0:T(8,128)(2,1)S(1)} %fusion.11), channel_id=1, source_target_pairs={{1,2},{2,1},{5,6},{6,5},{9,10},{10,9},{13,14},{14,13},{17,18},{18,... | collective-permute-start | bytes 552968 | tf_op jit(solution)/shard_map/ppermute | solution.py:384
  78.6 5.1 %copy-start.7 = (bf16[176,1152]{1,0:T(8,128)(2,1)S(1)}, bf16[176,1152]{1,0:T(8,128)(2,1)}, u32[]{:S(2)}) copy-start(bf16[176,1152]{1,0:T(8,128)(2,1)} %get-tuple-element.46) | copy-start | bytes 1216516
  78.6 21.2 %copy-start.6 = (bf16[80,1152]{1,0:T(8,128)(2,1)S(1)}, bf16[80,1152]{1,0:T(8,128)(2,1)}, u32[]{:S(2)}) copy-start(bf16[80,1152]{1,0:T(8,128)(2,1)} %projection.6) | copy-start | bytes 552964
  83.7 23.2 %copy-start.8 = (bf16[176,1152]{1,0:T(8,128)(2,1)S(1)}, bf16[176,1152]{1,0:T(8,128)(2,1)}, u32[]{:S(2)}) copy-start(bf16[176,1152]{1,0:T(8,128)(2,1)} %get-tuple-element.44) | copy-start | bytes 1216516
  83.7 17.0 %collective-permute-start.27 = (bf16[176,1152]{1,0:T(8,128)(2,1)S(1)}, bf16[176,1152]{1,0:T(8,128)(2,1)S(1)}, u32[]{:S(2)}, u32[]{:S(2)}) collective-permute-start(bf16[176,1152]{1,0:T(8,128)(2,1)S(1)} %copy-done.7), channel_id=1, source_target_pairs={{0,3},{3,0},{4,7},{7,4},{8,11},{11,8},{12,15},{15,12},{16,19},{19,... | collective-permute-start | bytes 1216520 | tf_op jit(solution)/shard_map/ppermute | solution.py:381
  84.5 18.5 %collective-permute-start.28 = (bf16[176,1152]{1,0:T(8,128)(2,1)}, bf16[176,1152]{1,0:T(8,128)(2,1)S(1)}, u32[]{:S(2)}, u32[]{:S(2)}) collective-permute-start(bf16[176,1152]{1,0:T(8,128)(2,1)} %get-tuple-element.47), channel_id=1, source_target_pairs={{0,1},{2,3},{1,0},{3,2},{4,5},{6,7},{5,4},{7,6},{8,9},{10,11},{9,8... | collective-permute-start | bytes 1216520 | tf_op jit(solution)/shard_map/ppermute | solution.py:382
  91.9 15.0 %collective-permute-start.29 = (bf16[176,1152]{1,0:T(8,128)(2,1)S(1)}, bf16[176,1152]{1,0:T(8,128)(2,1)S(1)}, u32[]{:S(2)}, u32[]{:S(2)}) collective-permute-start(bf16[176,1152]{1,0:T(8,128)(2,1)S(1)} %fusion.5), channel_id=1, source_target_pairs={{1,2},{2,1},{5,6},{6,5},{9,10},{10,9},{13,14},{14,13},{17,18},{18,... | collective-permute-start | bytes 1216520 | tf_op jit(solution)/shard_map/ppermute | solution.py:384
